TPU v7x, 256 devices: a whole 4x4x8 slice. The times are simulated.
256 devices in a mesh: tm: 32 (over z, y_lo, core), space: 8 (over x, y_hi).
Axes of the slice: x: 4, y: 4 (y_hi: 2, y_lo: 2; y = y_hi * 2 + y_lo), z: 8, core: 2. Of those that a mesh axis runs over, the one named last changes fastest.
Arguments:
- flux_solution_stack: float32 [128, 1024, 1024], P('tm', 'space'), may hold values from -6 to 6
- source: float32 [128, 1024, 1024], P('tm', 'space'), may hold values from -6 to 6
- notch_offsets: int32 [128], P('tm'), may hold values from 0 to 127
- region_ids: int32 [1024, 1024], P('space'), may hold values from 0 to 7
- nu_table: float32 [8], replicated, may hold values from 0.1 to 10
- sigma_table: float32 [8], replicated, may hold values from 0.05 to 1
Outputs:
- updated: float32 [128, 1024, 1024], P('tm', 'space')
- correction: float32 [1024, 1024], P('space')
All inputs are finite; a program needn't handle non-finite values.
Results may differ from a plain program's by a relative error of at most 0.0003.
Values sent between devices are 32-bit elements; how exact they have to be, the bound alone decides.
No kernel may reach another device: no remote copies, remote signals or barrier semaphores. Data moves between devices by JAX's collectives and lax.ppermute only.
A program may use at most 64 MiB of HBM per device.

v0:
```python
import jax
import jax.numpy as jnp
from jax import lax
from jax.sharding import PartitionSpec as P

SLOT_W = 8
REGIONS = 8
SWEEPS = 4


minimum_floor = 0.2
upper_limit = 2.0


def shifted(block, axis, distance):
    devices = range(lax.axis_size(axis))
    route = [((i - distance) % len(devices), i) for i in devices]
    return lax.ppermute(block, axis, route)


def padded(value, sides, width):
    for axis, dim in sides:
        count, length = (lax.axis_size(axis), value.shape[dim])
        up = [(i, (i + 1) % count) for i in range(count - 1)]
        down = [(j, i) for i, j in up]
        last = lax.slice_in_dim(value, length - width, length, axis=dim)
        first = lax.slice_in_dim(value, 0, width, axis=dim)
        before = lax.ppermute(last, axis, up)
        after = lax.ppermute(first, axis, down)
        value = jnp.concatenate([before, value, after], axis=dim)
    return value


def lookup(region_map, table):
    result = jnp.zeros(region_map.shape, jnp.float32)
    for region in range(REGIONS):
        result = result + jnp.where(region_map == region, table[region], jnp.float32(0.0))
    return result


def harmonic(left, right):
    return 2.0 * left * right / (left + right)


def material_kinds(ids_pad, shift, rotor, nu_table, sigma_table):
    moved = jnp.where(rotor, jnp.roll(ids_pad, shift * SLOT_W, axis=1), ids_pad)
    nu_pad = lookup(moved, nu_table)
    sigma_cells = lookup(moved[1:-1], sigma_table)
    facet_lines = harmonic(nu_pad[:-1], nu_pad[1:])
    core = nu_pad[1:-1]
    wrapped = jnp.concatenate([core[:, -1:], core, core[:, :1]], axis=1)
    face_cols = harmonic(wrapped[:, :-1], wrapped[:, 1:])
    return (facet_lines, face_cols, sigma_cells)


def wrap_cols(field):
    return jnp.concatenate([field[:, -1:], field, field[:, :1]], axis=1)


def operate(field, row_pad, col_pad, facet_lines, face_cols, sigma_cells):
    result = sigma_cells * field
    result = (
        result + facet_lines[:-1] * (field - row_pad[:-2]) + facet_lines[1:] * (field - row_pad[2:])
    )
    result = (
        result
        + face_cols[:, :-1] * (field - col_pad[:, :-2])
        + face_cols[:, 1:] * (field - col_pad[:, 2:])
    )
    return result


def diagonal_of(facet_lines, face_cols, sigma_cells):
    return sigma_cells + facet_lines[:-1] + facet_lines[1:] + face_cols[:, :-1] + face_cols[:, 1:]


def chebyshev(desired_result, apply_op, diagonal):
    center = (upper_limit + minimum_floor) / 2.0
    half_span_width = (upper_limit - minimum_floor) / 2.0
    ratio = center / half_span_width
    coef_old = 1.0 / ratio
    resid = desired_result
    step_field = resid / diagonal / center
    corr = step_field
    for sweep in range(SWEEPS - 1):
        resid = resid - apply_op(step_field)
        coef_new = 1.0 / (2.0 * ratio - coef_old)
        step_field = coef_new * coef_old * step_field + 2.0 * coef_new / half_span_width * (
            resid / diagonal
        )
        corr = corr + step_field
        coef_old = coef_new
    return corr


def per_device(flux_solution_stack, source, notch_offsets, region_ids, nu_table, sigma_table):
    sample_moments = flux_solution_stack.shape[0]
    rows = flux_solution_stack.shape[1]
    mesh_cell_tally = lax.axis_size("tm")
    overall_summation = sample_moments * mesh_cell_tally
    opposite_moment_potential = shifted(flux_solution_stack, "tm", mesh_cell_tally // 2)
    ids_pad = padded(region_ids, (("space", 0),), 1)
    global_rows = lax.axis_index("space") * rows + jnp.arange(-1, rows + 1, dtype=jnp.int32)
    rotor = (global_rows < rows * lax.axis_size("space") // 2)[:, None]
    field_pad = padded(flux_solution_stack, (("space", 1),), 1)
    integer_sequence = lax.axis_index("tm") * sample_moments + jnp.arange(
        sample_moments, dtype=jnp.int32
    )
    polarity_factors = jnp.where(integer_sequence < overall_summation // 2, 1.0, -1.0).astype(
        jnp.float32
    )
    combined_accumulation = jnp.zeros(flux_solution_stack.shape[1:], jnp.float32)
    for sample_moment in range(sample_moments):
        facet_lines, face_cols, sigma_cells = material_kinds(
            ids_pad, notch_offsets[sample_moment], rotor, nu_table, sigma_table
        )
        field = flux_solution_stack[sample_moment]
        image = operate(
            field, field_pad[sample_moment], wrap_cols(field), facet_lines, face_cols, sigma_cells
        )
        combined_accumulation = combined_accumulation + polarity_factors[sample_moment] * (
            source[sample_moment] - image
        )
    target_part = combined_accumulation / overall_summation
    facet_lines, face_cols, sigma_cells = material_kinds(
        ids_pad, jnp.int32(0), rotor, nu_table, sigma_table
    )
    desired_result = lax.psum(target_part, "tm")
    diagonal = diagonal_of(facet_lines, face_cols, sigma_cells)

    def apply_entire_operator(field):
        row_pad = padded(field, (("space", 0),), 1)
        return operate(field, row_pad, wrap_cols(field), facet_lines, face_cols, sigma_cells)

    corr = chebyshev(desired_result, apply_entire_operator, diagonal)
    image = apply_entire_operator(corr)
    upper, lower = lax.psum((jnp.sum(desired_result * corr), jnp.sum(corr * image)), "space")
    omega = upper / lower
    correction = omega * corr
    updated = (
        flux_solution_stack
        - 0.5 * (flux_solution_stack + opposite_moment_potential)
        + polarity_factors[:, None, None] * correction[None]
    )
    return (updated, correction)


def solution(mesh):
    placed = (P("tm", "space", None), P("tm", "space", None), P("tm"), P("space", None), P(), P())
    return jax.shard_map(
        per_device,
        mesh=mesh,
        in_specs=placed,
        out_specs=(P("tm", "space", None), P("space", None)),
        check_vma=False,
    )
```

profile of v0, /device:TPU:2, one launch (start us, length us, event | category | flops | bytes accessed | tf_op | source)
XLA Modules:
  0.0 428.5 jit_solution(2437052993636955578)
XLA Ops:
  8.0 5.1 %collective-permute-start.1 = (s32[1,1024]{1,0:T(1,128)S(1)}, s32[1,1024]{1,0:T(1,128)S(1)}, u32[]{:S(2)}, u32[]{:S(2)}) collective-permute-start(s32[1,1024]{1,0:T(1,128)S(1)} %get-tuple-element.66), channel_id=1, source_target_pairs={{0,1},{1,2},{2,3},{3,4},{4,5},{5,6},{6,7},{8,9},{9,10},{10,11},{11... | collective-permute-start | bytes 12296 | tf_op jit(solution)/shard_map/ppermute | solution.py:28
  13.1 3.1 collective-permute-start.2
  16.2 7.3 %collective-permute-start = (f32[4,128,1024]{2,1,0:T(8,128)}, f32[4,128,1024]{2,1,0:T(8,128)}, u32[]{:S(2)}, u32[]{:S(2)}) collective-permute-start(f32[4,128,1024]{2,1,0:T(8,128)} %param.10), channel_id=1, source_target_pairs={{128,0},{136,8},{144,16},{152,24},{160,32},{168,40},{176,48},{184,... | collective-permute-start | bytes 6291464 | tf_op jit(solution)/shard_map/ppermute | solution.py:18
  23.5 1.6 fusion.121
  25.1 4.2 collective-permute-start.4
  29.3 3.2 collective-permute-start.3
  32.5 2.9 slice_bitcast_fusion.7
  40.6 1.6 fusion.137
  44.9 7.1 %select_add_fusion.4 = (f32[130,1024]{1,0:T(8,128)S(1)}, s32[130,1024]{1,0:T(8,128)}, f32[130,1024]{1,0:T(8,128)S(1)}, s32[130,1024]{1,0:T(8,128)}) fusion(f32[]{:T(128)} %bitcast.19, f32[]{:T(128)} %bitcast.18, f32[]{:T(128)} %bitcast.17, f32[]{:T(128)} %bitcast.16, f32[]{:T(128)} %bitcast.15, f32[]{:T(128)} %bitcast.14, f32[]{:T(128)} %bitcast.13, ...), kind=kLoop, calls=%fused_computation.31 | loop fusion | flops 6656000 | bytes 3727530 | tf_op jit(solution)/shard_map/add | solution.py:37
  52.3 7.1 %select_add_fusion.2 = (f32[130,1024]{1,0:T(8,128)S(1)}, s32[130,1024]{1,0:T(8,128)}, f32[130,1024]{1,0:T(8,128)S(1)}, s32[130,1024]{1,0:T(8,128)}) fusion(f32[]{:T(128)} %bitcast.19, f32[]{:T(128)} %bitcast.18, f32[]{:T(128)} %bitcast.17, f32[]{:T(128)} %bitcast.16, f32[]{:T(128)} %bitcast.15, f32[]{:T(128)} %bitcast.14, f32[]{:T(128)} %bitcast.13, ...), kind=kLoop, calls=%fused_computation.27 | loop fusion | flops 6656000 | bytes 3727530 | tf_op jit(solution)/shard_map/add | solution.py:37
  66.4 5.6 %select_add_fusion = f32[130,1024]{1,0:T(8,128)S(1)} fusion(f32[]{:T(128)} %bitcast.19, f32[]{:T(128)} %bitcast.18, f32[]{:T(128)} %bitcast.17, f32[]{:T(128)} %bitcast.16, f32[]{:T(128)} %bitcast.15, f32[]{:T(128)} %bitcast.14, f32[]{:T(128)} %bitcast.13, f32[]{:T(128)} %bitcast.12, s32[1,1024]{1,0:T(1,128)S(1)} %collective-permute-done.2, ...), kind=kLoop, calls=%fused_computation.23 | loop fusion | flops 3328000 | bytes 1064992 | tf_op jit(solution)/shard_map/add | solution.py:37
  72.0 1.6 dynamic-update-slice.1
  73.6 18.3 %fusion.63 = f32[128,1024]{1,0:T(8,128)} fusion(f32[128,1024]{1,0:T(8,128)} %get-tuple-element.24, f32[128,1]{1,0:T(8,128)} %get-tuple-element.94, f32[128,1025]{1,0:T(8,128)} %add_divide_fusion.1, f32[128,1]{1,0:T(8,128)} %get-tuple-element.95, f32[4,129,1024]{2,1,0:T(8,128)} %dynamic-update-slice.1, f32[129,1024]{1,0:T(8,128)} %get-tuple-element.96, ...), kind=kLoop, calls=%fused_computation.112 | loop fusion | flops 22020096 | bytes 19419184 | tf_op jit(solution)/shard_map/div | solution.py:124
  92.5 225.7 %all-reduce.3.cloned.1.call-done = f32[128,1024]{1,0:T(8,128)} async-done(((f32[128,1024]{1,0:T(8,128)}), f32[128,1024]{1,0:T(8,128)}) %all-reduce.3.cloned.1.call-update) | async-done | bytes 524304 | tf_op jit(solution)/shard_map/psum | solution.py:128
  318.2 6.4 %divide_multiply_fusion = (f32[128,1024]{1,0:T(8,128)S(1)}, f32[128,1024]{1,0:T(8,128)S(1)}) fusion(f32[128,1024]{1,0:T(8,128)} %all-reduce.3.cloned.1.call-done, f32[128,1025]{1,0:T(8,128)S(1)} %add_divide_fusion, f32[129,1024]{1,0:T(8,128)S(1)} %add_divide_fusion.5, f32[]{:T(128)} %bitcast.10, s32[128,1024]{1,0:T(8,128)S(1)} %copy-done, f32[]{:T(128)} %bitcast.9, ...), kind=kLoop, calls=%fused_computation.191 | loop fusion | flops 3801088 | bytes 4194336 | tf_op jit(solution)/shard_map/div | solution.py:83
  324.5 4.6 %collective-permute-start.5 = (f32[1,1024]{1,0:T(1,128)S(1)}, f32[1,1024]{1,0:T(1,128)S(1)}, u32[]{:S(2)}, u32[]{:S(2)}) collective-permute-start(f32[1,1024]{1,0:T(1,128)S(1)} %get-tuple-element.54), channel_id=1, source_target_pairs={{0,1},{1,2},{2,3},{3,4},{4,5},{5,6},{6,7},{8,9},{9,10},{10,11},{11... | collective-permute-start | bytes 12296 | tf_op jit(solution)/shard_map/ppermute | solution.py:28
  329.2 3.6 collective-permute-start.6
  332.9 3.3 collective-permute-done.6
  336.2 5.6 %multiply_add_fusion.2 = (f32[128,1024]{1,0:T(8,128)S(1)}, f32[128,1024]{1,0:T(8,128)S(1)}) fusion(f32[128,1024]{1,0:T(8,128)S(1)} %get-tuple-element.13, f32[128,1024]{1,0:T(8,128)S(1)} %copy-done.2, f32[128,1024]{1,0:T(8,128)S(1)} %get-tuple-element.12, f32[128,1]{1,0:T(8,128)S(1)} %get-tuple-element.57, f32[128,1025]{1,0:T(8,128)S(1)} %add_divide_fusion, ...), kind=kLoop, calls=%fused_computation.184 | loop fusion | flops 6029312 | bytes 5252128 | tf_op jit(solution)/shard_map/add | solution.py:88
  341.8 4.5 %collective-permute-start.7 = (f32[1,1024]{1,0:T(1,128)S(1)}, f32[1,1024]{1,0:T(1,128)S(1)}, u32[]{:S(2)}, u32[]{:S(2)}) collective-permute-start(f32[1,1024]{1,0:T(1,128)S(1)} %get-tuple-element.50), channel_id=1, source_target_pairs={{0,1},{1,2},{2,3},{3,4},{4,5},{5,6},{6,7},{8,9},{9,10},{10,11},{11... | collective-permute-start | bytes 12296 | tf_op jit(solution)/shard_map/ppermute | solution.py:28
  346.4 3.9 collective-permute-start.8
  350.4 3.0 collective-permute-done.8
  353.4 5.7 %multiply_add_fusion.1 = (f32[128,1024]{1,0:T(8,128)S(1)}, f32[128,1024]{1,0:T(8,128)S(1)}) fusion(f32[128,1024]{1,0:T(8,128)S(1)} %get-tuple-element.13, f32[128,1024]{1,0:T(8,128)S(1)} %get-tuple-element.11, f32[128,1024]{1,0:T(8,128)S(1)} %copy-done.2, f32[128,1024]{1,0:T(8,128)S(1)} %get-tuple-element.10, f32[128,1]{1,0:T(8,128)S(1)} %get-tuple-element.53, ...), kind=kLoop, calls=%fused_computation.183 | loop fusion | flops 6553600 | bytes 5776416 | tf_op jit(solution)/shard_map/add | solution.py:88
  359.0 4.6 %collective-permute-start.10 = (f32[1,1024]{1,0:T(1,128)S(1)}, f32[1,1024]{1,0:T(1,128)S(1)}, u32[]{:S(2)}, u32[]{:S(2)}) collective-permute-start(f32[1,1024]{1,0:T(1,128)S(1)} %get-tuple-element.47), channel_id=1, source_target_pairs={{1,0},{2,1},{3,2},{4,3},{5,4},{6,5},{7,6},{9,8},{10,9},{11,10},{12... | collective-permute-start | bytes 12296 | tf_op jit(solution)/shard_map/ppermute | solution.py:29
  363.7 2.7 collective-permute-start.9
  366.5 5.1 %collective-permute-done.9 = f32[1,1024]{1,0:T(1,128)S(1)} collective-permute-done((f32[1,1024]{1,0:T(1,128)S(1)}, f32[1,1024]{1,0:T(1,128)S(1)}, u32[]{:S(2)}, u32[]{:S(2)}) %collective-permute-start.9) | collective-permute-done | bytes 4128 | tf_op jit(solution)/shard_map/ppermute | solution.py:28
  371.6 6.4 %multiply_reduce_fusion = (f32[]{:T(128)}, f32[128,1024]{1,0:T(8,128)S(1)}) fusion(f32[128,1024]{1,0:T(8,128)S(1)} %copy-done.2, f32[128,1024]{1,0:T(8,128)S(1)} %get-tuple-element.13, f32[128,1024]{1,0:T(8,128)S(1)} %get-tuple-element.9, f32[128,1024]{1,0:T(8,128)S(1)} %get-tuple-element.8, f32[128,1]{1,0:T(8,128)S(1)} %get-tuple-element.49, ...), kind=kLoop, calls=%fused_computation.182 | loop fusion | flops 7340031 | bytes 5776420 | tf_op jit(solution)/shard_map/reduce_sum | solution.py:137
  377.9 1.9 collective-permute-start.11
  379.8 6.3 %collective-permute-start.12 = (f32[1,1024]{1,0:T(1,128)S(1)}, f32[1,1024]{1,0:T(1,128)S(1)}, u32[]{:S(2)}, u32[]{:S(2)}) collective-permute-start(f32[1,1024]{1,0:T(1,128)S(1)} %get-tuple-element.43), channel_id=1, source_target_pairs={{1,0},{2,1},{3,2},{4,3},{5,4},{6,5},{7,6},{9,8},{10,9},{11,10},{12... | collective-permute-start | bytes 12296 | tf_op jit(solution)/shard_map/ppermute | solution.py:29
  387.8 6.1 %fusion.4 = f32[]{:T(128)} fusion(f32[128,1024]{1,0:T(8,128)S(1)} %get-tuple-element.7, f32[128,1]{1,0:T(8,128)S(1)} %get-tuple-element.45, f32[128,1]{1,0:T(8,128)S(1)} %get-tuple-element.44, f32[1,1024]{1,0:T(1,128)S(1)} %collective-permute-done.12, f32[1,1024]{1,0:T(1,128)S(1)} %collective-permute-done.11, f32[128,1025]{1,0:T(8,128)S(1)} %add_divide_fusion, ...), kind=kLoop, calls=%fused_computation.37 | loop fusion | flops 5505023 | bytes 3154980 | tf_op jit(solution)/shard_map/reduce_sum | solution.py:137
  393.9 21.9 %all-reduce = (f32[]{:T(128)}, f32[]{:T(128)}) all-reduce(f32[]{:T(128)} %get-tuple-element.6, f32[]{:T(128)} %fusion.4), channel_id=1, replica_groups=mesh['tm'=32,'space'=8] {'space'}, use_global_device_ids=true, to_apply=%region_2.5 | all-reduce | flops 2 | bytes 16 | tf_op jit(solution)/shard_map/psum | solution.py:137
  417.2 4.5 %multiply_add_fusion = f32[4,128,1024]{2,1,0:T(8,128)} fusion(f32[4,128,1024]{2,1,0:T(8,128)} %param.10, f32[4,128,1024]{2,1,0:T(8,128)} %collective-permute-done, f32[128,1024]{1,0:T(8,128)S(1)} %broadcast_multiply_fusion, f32[4]{0:T(128)S(1)} %compare_select_fusion), kind=kLoop, calls=%fused_computation | loop fusion | flops 2621440 | bytes 6815760 | tf_op jit(solution)/shard_map/add | solution.py:141
  (63 shorter events, 15.7 us)
Async XLA Ops:
  7.2 311.0 %all-reduce.3.cloned.1.call-start = ((), (), s32[]{:S(2)}) async-start(), calls=%async_computation | async-start | bytes 1048576 | tf_op jit(solution)/shard_map/psum | solution.py:128
  8.0 36.8 %collective-permute-start.1 = (s32[1,1024]{1,0:T(1,128)S(1)}, s32[1,1024]{1,0:T(1,128)S(1)}, u32[]{:S(2)}, u32[]{:S(2)}) collective-permute-start(s32[1,1024]{1,0:T(1,128)S(1)} %get-tuple-element.66), channel_id=1, source_target_pairs={{0,1},{1,2},{2,3},{3,4},{4,5},{5,6},{6,7},{8,9},{9,10},{10,11},{11... | collective-permute-start | bytes 12296 | tf_op jit(solution)/shard_map/ppermute | solution.py:28
  13.1 31.7 %collective-permute-start.2 = (s32[1,1024]{1,0:T(1,128)S(1)}, s32[1,1024]{1,0:T(1,128)S(1)}, u32[]{:S(2)}, u32[]{:S(2)}) collective-permute-start(s32[1,1024]{1,0:T(1,128)S(1)} %get-tuple-element.67), channel_id=1, source_target_pairs={{1,0},{2,1},{3,2},{4,3},{5,4},{6,5},{7,6},{9,8},{10,9},{11,10},{12... | collective-permute-start | bytes 12296 | tf_op jit(solution)/shard_map/ppermute | solution.py:29
  16.2 400.9 %collective-permute-start = (f32[4,128,1024]{2,1,0:T(8,128)}, f32[4,128,1024]{2,1,0:T(8,128)}, u32[]{:S(2)}, u32[]{:S(2)}) collective-permute-start(f32[4,128,1024]{2,1,0:T(8,128)} %param.10), channel_id=1, source_target_pairs={{128,0},{136,8},{144,16},{152,24},{160,32},{168,40},{176,48},{184,... | collective-permute-start | bytes 6291464 | tf_op jit(solution)/shard_map/ppermute | solution.py:18
  25.1 46.9 %collective-permute-start.4 = (f32[4,1,1024]{2,1,0:T(1,128)}, f32[4,1,1024]{2,1,0:T(1,128)}, u32[]{:S(2)}, u32[]{:S(2)}) collective-permute-start(f32[4,1,1024]{2,1,0:T(1,128)} %get-tuple-element.27), channel_id=1, source_target_pairs={{1,0},{2,1},{3,2},{4,3},{5,4},{6,5},{7,6},{9,8},{10,9},{11,10},{12... | collective-permute-start | bytes 49160 | tf_op jit(solution)/shard_map/ppermute | solution.py:29
  29.3 44.3 %collective-permute-start.3 = (f32[4,1,1024]{2,1,0:T(1,128)S(1)}, f32[4,1,1024]{2,1,0:T(1,128)S(1)}, u32[]{:S(2)}, u32[]{:S(2)}) collective-permute-start(f32[4,1,1024]{2,1,0:T(1,128)S(1)} %get-tuple-element.26), channel_id=1, source_target_pairs={{0,1},{1,2},{2,3},{3,4},{4,5},{5,6},{6,7},{8,9},{9,10},{10,11},{11... | collective-permute-start | bytes 49160 | tf_op jit(solution)/shard_map/ppermute | solution.py:28
  32.5 2.9 copy-start.1
  35.4 4.2 copy-start.3
  35.4 1.6 copy-start.7
  35.4 2.3 copy-start.5
  35.4 2.9 copy-start.6
  35.4 9.4 %copy-start = (s32[128,1024]{1,0:T(8,128)S(1)}, s32[128,1024]{1,0:T(8,128)}, u32[]{:S(2)}) copy-start(s32[128,1024]{1,0:T(8,128)} %param.13) | copy-start | bytes 1572868
  318.2 18.0 %copy-start.2 = (f32[128,1024]{1,0:T(8,128)S(1)}, f32[128,1024]{1,0:T(8,128)}, u32[]{:S(2)}) copy-start(f32[128,1024]{1,0:T(8,128)} %all-reduce.3.cloned.1.call-done) | copy-start | bytes 1572868
  324.5 8.3 %collective-permute-start.5 = (f32[1,1024]{1,0:T(1,128)S(1)}, f32[1,1024]{1,0:T(1,128)S(1)}, u32[]{:S(2)}, u32[]{:S(2)}) collective-permute-start(f32[1,1024]{1,0:T(1,128)S(1)} %get-tuple-element.54), channel_id=1, source_target_pairs={{0,1},{1,2},{2,3},{3,4},{4,5},{5,6},{6,7},{8,9},{9,10},{10,11},{11... | collective-permute-start | bytes 12296 | tf_op jit(solution)/shard_map/ppermute | solution.py:28
  329.2 7.0 %collective-permute-start.6 = (f32[1,1024]{1,0:T(1,128)S(1)}, f32[1,1024]{1,0:T(1,128)S(1)}, u32[]{:S(2)}, u32[]{:S(2)}) collective-permute-start(f32[1,1024]{1,0:T(1,128)S(1)} %get-tuple-element.55), channel_id=1, source_target_pairs={{1,0},{2,1},{3,2},{4,3},{5,4},{6,5},{7,6},{9,8},{10,9},{11,10},{12... | collective-permute-start | bytes 12296 | tf_op jit(solution)/shard_map/ppermute | solution.py:29
  341.8 8.5 %collective-permute-start.7 = (f32[1,1024]{1,0:T(1,128)S(1)}, f32[1,1024]{1,0:T(1,128)S(1)}, u32[]{:S(2)}, u32[]{:S(2)}) collective-permute-start(f32[1,1024]{1,0:T(1,128)S(1)} %get-tuple-element.50), channel_id=1, source_target_pairs={{0,1},{1,2},{2,3},{3,4},{4,5},{5,6},{6,7},{8,9},{9,10},{10,11},{11... | collective-permute-start | bytes 12296 | tf_op jit(solution)/shard_map/ppermute | solution.py:28
  346.4 7.0 %collective-permute-start.8 = (f32[1,1024]{1,0:T(1,128)S(1)}, f32[1,1024]{1,0:T(1,128)S(1)}, u32[]{:S(2)}, u32[]{:S(2)}) collective-permute-start(f32[1,1024]{1,0:T(1,128)S(1)} %get-tuple-element.51), channel_id=1, source_target_pairs={{1,0},{2,1},{3,2},{4,3},{5,4},{6,5},{7,6},{9,8},{10,9},{11,10},{12... | collective-permute-start | bytes 12296 | tf_op jit(solution)/shard_map/ppermute | solution.py:29
  359.0 7.4 %collective-permute-start.10 = (f32[1,1024]{1,0:T(1,128)S(1)}, f32[1,1024]{1,0:T(1,128)S(1)}, u32[]{:S(2)}, u32[]{:S(2)}) collective-permute-start(f32[1,1024]{1,0:T(1,128)S(1)} %get-tuple-element.47), channel_id=1, source_target_pairs={{1,0},{2,1},{3,2},{4,3},{5,4},{6,5},{7,6},{9,8},{10,9},{11,10},{12... | collective-permute-start | bytes 12296 | tf_op jit(solution)/shard_map/ppermute | solution.py:29
  363.7 7.9 %collective-permute-start.9 = (f32[1,1024]{1,0:T(1,128)S(1)}, f32[1,1024]{1,0:T(1,128)S(1)}, u32[]{:S(2)}, u32[]{:S(2)}) collective-permute-start(f32[1,1024]{1,0:T(1,128)S(1)} %get-tuple-element.46), channel_id=1, source_target_pairs={{0,1},{1,2},{2,3},{3,4},{4,5},{5,6},{6,7},{8,9},{9,10},{10,11},{11... | collective-permute-start | bytes 12296 | tf_op jit(solution)/shard_map/ppermute | solution.py:28
  377.9 8.3 %collective-permute-start.11 = (f32[1,1024]{1,0:T(1,128)S(1)}, f32[1,1024]{1,0:T(1,128)S(1)}, u32[]{:S(2)}, u32[]{:S(2)}) collective-permute-start(f32[1,1024]{1,0:T(1,128)S(1)} %get-tuple-element.42), channel_id=1, source_target_pairs={{0,1},{1,2},{2,3},{3,4},{4,5},{5,6},{6,7},{8,9},{9,10},{10,11},{11... | collective-permute-start | bytes 12296 | tf_op jit(solution)/shard_map/ppermute | solution.py:28
  379.8 7.9 %collective-permute-start.12 = (f32[1,1024]{1,0:T(1,128)S(1)}, f32[1,1024]{1,0:T(1,128)S(1)}, u32[]{:S(2)}, u32[]{:S(2)}) collective-permute-start(f32[1,1024]{1,0:T(1,128)S(1)} %get-tuple-element.43), channel_id=1, source_target_pairs={{1,0},{2,1},{3,2},{4,3},{5,4},{6,5},{7,6},{9,8},{10,9},{11,10},{12... | collective-permute-start | bytes 12296 | tf_op jit(solution)/shard_map/ppermute | solution.py:29
  417.2 4.5 %copy-start.4 = (f32[128,1024]{1,0:T(8,128)}, f32[128,1024]{1,0:T(8,128)S(1)}, u32[]{:S(2)}) copy-start(f32[128,1024]{1,0:T(8,128)S(1)} %broadcast_multiply_fusion) | copy-start | bytes 1572868
Sparse Core Ops, SparseCore 0:
  92.1 226.0 all-reduce.2
where the time goes:
time: 430 us; the launch traced here: 429 us
  waiting for transfers between devices  239 us (56%)
  other arithmetic  80.1 us (19%)
  starting transfers between devices  55.1 us (13%)
  blocking collectives  21.9 us (5%)
  between operations  18.3 us (4%)
  local copies, waits for them, and re-layouts  14.6 us (3%)
    psum x1, waiting for transfers between devices, per_device(): desired_result = lax.psum(target_part, 'tm')  226 us
    ppermute x6, starting transfers between devices, padded(): after = lax.ppermute(first, axis, down)  25.8 us
    ppermute x6, starting transfers between devices, padded(): before = lax.ppermute(last, axis, up)  22 us
    psum x1, blocking collectives, per_device(): lax.psum((jnp.sum(desired_result * corr), jnp.sum(corr * image)), 'space')  21.9 us
    add x3, other arithmetic, lookup(): result + jnp.where(region_map == region, table[region], jnp.float32(0.0))  19.8 us
    div x1, other arithmetic, per_device(): target_part = combined_accumulation / overall_summation  18.3 us
    add x2, other arithmetic, chebyshev(): coef_new * coef_old * step_field  11.3 us
  transfers between devices with their start and end apart: 14, of which 5 were waited for; matrix products, arithmetic and copies ran while one was open for 21% of the time, Pallas kernels for 0%

commit v1 on v0

v1 whole, which is shorter than its diff:
```python
import functools

import jax
import jax.numpy as jnp
from jax import lax
from jax.experimental import pallas as pl
from jax.experimental.pallas import tpu as pltpu
from jax.sharding import PartitionSpec as P

SLOT_W = 8
REGIONS = 8
SWEEPS = 4
MINIMUM = 0.2
MAXIMUM = 2.0
ROWS = 128
COLS = 1024
STEPS = 4
PADDED = ROWS + 32
FIRST = 16
EARLY = 48
TILE = 16

ANY = pl.BlockSpec(memory_space=pl.ANY)
VMEM = pl.BlockSpec(memory_space=pltpu.VMEM)
SMEM = pl.BlockSpec(memory_space=pltpu.SMEM)
LIMIT = pltpu.CompilerParams(vmem_limit_bytes=16 * 1024 * 1024)


def struct(*shape):
    return jax.ShapeDtypeStruct(shape, jnp.float32)


def block(i):
    return pl.ds(pl.multiple_of(i * 8, 8), 8)


def harmonic(left, right):
    return 2.0 * left * right / (left + right)


def above(cur, prev, first):
    return jnp.where(first, pltpu.roll(prev, 1, 0), pltpu.roll(cur, 1, 0))


def below(cur, after, last):
    return jnp.where(last, pltpu.roll(after, 7, 0), pltpu.roll(cur, 7, 0))


def row_masks():
    rows = lax.broadcasted_iota(jnp.int32, (8, COLS), 0)
    return rows == 0, rows == 7


def edges_kernel(first_p, last_p, first_ids, last_ids, down_ref, up_ref):
    for out, p, ids, row in ((down_ref, first_p, first_ids, 0), (up_ref, last_p, last_ids, 7)):
        for k in range(STEPS):
            out[k : k + 1, :] = p[k, row : row + 1, :]
            out[STEPS + k : STEPS + k + 1, :] = p[k, row : row + 1, :]
        out[8:16, :] = ids[...].astype(jnp.float32)


def edges(p, ids):
    tail = ROWS // 8 - 1
    return pl.pallas_call(
        edges_kernel,
        grid=(1,),
        in_specs=[
            pl.BlockSpec((STEPS, 8, COLS), lambda i: (0, 0, 0)),
            pl.BlockSpec((STEPS, 8, COLS), lambda i: (0, tail, 0)),
            pl.BlockSpec((8, COLS), lambda i: (0, 0)),
            pl.BlockSpec((8, COLS), lambda i: (tail, 0)),
        ],
        out_specs=[pl.BlockSpec((16, COLS), lambda i: (0, 0))] * 2,
        out_shape=[struct(16, COLS)] * 2,
    )(p, p, ids, ids)


def residual_kernel(
    offs, nu_t, sg_t, p, src, ids, top, bot, mine, send, sg, fr, fc, nu, v, fr_k
):
    first, last = row_masks()
    strip, tm = lax.axis_index("space"), lax.axis_index("tm")
    half_strips = lax.axis_size("space") // 2

    def materials(where, region):
        n = jnp.full((8, COLS), nu_t[0], jnp.float32)
        s = jnp.full((8, COLS), sg_t[0], jnp.float32)
        for r in range(1, REGIONS):
            hit = region == r
            n = jnp.where(hit, nu_t[r], n)
            s = jnp.where(hit, sg_t[r], s)
        nu[where, :] = n
        sg[where, :] = s

    materials(pl.ds(8, 8), top[8:16, :].astype(jnp.int32))
    materials(pl.ds(FIRST + ROWS, 8), bot[8:16, :].astype(jnp.int32))

    @pl.loop(0, ROWS // 8)
    def _(b):
        materials(block(b + 2), ids[block(b), :])

    zeros = jnp.zeros((8, COLS), jnp.float32)
    for ref in (sg, fr, fc):
        ref[0:8, :] = zeros
        ref[PADDED - 8 : PADDED, :] = zeros
    nu[0:8, :] = nu[8:16, :]
    nu[PADDED - 8 : PADDED, :] = nu[PADDED - 16 : PADDED - 8, :]

    @pl.loop(1, PADDED // 8 - 1)
    def _(b):
        cur = nu[block(b), :]
        face = harmonic(cur, below(cur, nu[block(b + 1), :], last))
        fr[block(b), :] = face
        fr_k[block(b), :] = face
        fc[block(b), :] = harmonic(cur, pltpu.roll(cur, COLS - 1, 1))

    sign = jnp.where(tm < lax.axis_size("tm") // 2, 1.0, -1.0).astype(jnp.float32)
    scale = sign / (STEPS * lax.axis_size("tm"))
    core, y = tm & 1, (tm >> 1) & 1
    flip = core * 8 + y * 4

    for k in range(STEPS):
        turn = offs[k] * SLOT_W
        own = jnp.where(strip < half_strips, turn, 0)
        for halo, at, kind, face_row in (
            (top, slice(15, 16), strip - 1, FIRST - 1),
            (bot, slice(FIRST + ROWS, FIRST + ROWS + 1), strip + 1, FIRST + ROWS - 1),
        ):
            other = jnp.where(kind < half_strips, turn, 0)
            beside = jnp.broadcast_to(nu[at, :], (8, COLS))
            beside = pltpu.roll(beside, (other - own) & (COLS - 1), 1)
            edge = FIRST if halo is top else FIRST + ROWS - 1
            face = harmonic(beside, jnp.broadcast_to(nu[edge : edge + 1, :], (8, COLS)))
            fr_k[face_row : face_row + 1, :] = face[0:1, :]
            row = jnp.broadcast_to(halo[k : k + 1, :], (8, COLS))
            row = pltpu.roll(row, (-own) & (COLS - 1), 1)
            if halo is top:
                v[8:16, :] = row
            else:
                v[FIRST + ROWS : FIRST + ROWS + 8, :] = row

        @pl.loop(0, ROWS // 8, unroll=2)
        def _(b):
            v[block(b + 2), :] = pltpu.roll(p[k, block(b), :], (-own) & (COLS - 1), 1)

        for out, shift in ((mine, 0), (send, 8)):

            @pl.loop(0, ROWS // 16, unroll=2)
            def _(i):
                b = (i + shift) ^ flip
                e = b + 2
                cur = v[block(e), :]
                down_face = fr_k[block(e), :]
                up_face = above(down_face, fr_k[block(e - 1), :], first)
                image = sg[block(e), :] * cur
                image += up_face * (cur - above(cur, v[block(e - 1), :], first))
                image += down_face * (cur - below(cur, v[block(e + 1), :], last))
                flow = fc[block(e), :] * (cur - pltpu.roll(cur, COLS - 1, 1))
                image += flow - pltpu.roll(flow, 1, 1)
                part = scale * (src[k, block(b), :] - pltpu.roll(image, own, 1))
                out[block(i), :] = part if k == 0 else out[block(i), :] + part


def residual(offs, nu_t, sg_t, p, src, ids, top, bot):
    return pl.pallas_call(
        residual_kernel,
        in_specs=[SMEM] * 3 + [VMEM] * 5,
        out_specs=[VMEM] * 5,
        out_shape=[struct(ROWS // 2, COLS)] * 2 + [struct(PADDED, COLS)] * 3,
        scratch_shapes=[pltpu.VMEM((PADDED, COLS), jnp.float32)] * 3,
        compiler_params=LIMIT,
        cost_estimate=pl.CostEstimate(flops=20_000_000, bytes_accessed=8_000_000, transcendentals=0),
    )(offs, nu_t, sg_t, p, src, ids, top, bot)


def swap(x, bit):
    return lax.ppermute(x, "tm", [(i, i ^ bit) for i in range(lax.axis_size("tm"))])


def add_kernel(a, b, mine, send):
    n = mine.shape[0]
    mine[...] = a[:n, :] + b[:n, :]
    send[...] = a[n:, :] + b[n:, :]


def halves(a, b):
    n = a.shape[0] // 2
    return pl.pallas_call(
        add_kernel,
        in_specs=[VMEM] * 2,
        out_specs=[VMEM] * 2,
        out_shape=[struct(n, COLS)] * 2,
    )(a, b)


def merge_kernel(a, b, _, out):
    for z in range(out.shape[0]):
        piece = slice(z * 128, z * 128 + 128)
        out[z] = a[:, piece] + b[:, piece]


def merge(a, b, after, count):
    return pl.pallas_call(
        merge_kernel,
        in_specs=[VMEM, VMEM, ANY],
        out_specs=VMEM,
        out_shape=struct(count, a.shape[0], COLS // count),
    )(a, b, after)


def total_kernel(parts, out):
    total = parts[0]
    for i in range(1, parts.shape[0]):
        total = total + parts[i]
    for i in range(parts.shape[0]):
        out[i] = total


def total_for_all(parts):
    return pl.pallas_call(
        total_kernel,
        in_specs=[VMEM],
        out_specs=VMEM,
        out_shape=struct(*parts.shape),
    )(parts)


def among_z(blocks):
    groups = [[z * 4 + q for z in range(blocks.shape[0])] for q in range(4)]
    return lax.all_to_all(blocks, "tm", 0, 0, axis_index_groups=groups)


def gate_kernel(value, _, out):
    pass


def gate(value, after):
    return pl.pallas_call(
        gate_kernel,
        in_specs=[ANY, ANY],
        out_specs=ANY,
        out_shape=struct(*value.shape),
        input_output_aliases={0: 0},
    )(value, after)


def assemble_kernel(x, other, core_part, target, top, bot):
    tm = lax.axis_index("tm")
    flip = (tm & 1) * 8 + ((tm >> 1) & 1) * 4
    count = x.shape[0]
    for ref, lead, start in ((x, 0, 0), (other, 0, 4), (core_part, 0, 8), (core_part, count, 12)):
        for i in range(4):
            for z in range(count):
                piece = slice(z * 128, z * 128 + 128)
                target[block((start + i) ^ flip), piece] = ref[lead + z, 8 * i : 8 * i + 8, :]
    top[...] = target[0:8, :]
    bot[...] = target[ROWS - 8 : ROWS, :]


def assemble(x, other, core_part):
    return pl.pallas_call(
        assemble_kernel,
        in_specs=[VMEM] * 3,
        out_specs=[VMEM] * 3,
        out_shape=[struct(ROWS, COLS), struct(8, COLS), struct(8, COLS)],
    )(x, other, core_part)


def chebyshev_kernel(target, top, bot, sg, fr, fc, c_out, sums, dinv, res, s0, s1, c):
    first, last = row_masks()
    strip = lax.axis_index("space")
    blocks = PADDED // 8
    zeros = jnp.zeros((8, COLS), jnp.float32)
    for ref in (s0, s1, c, dinv):
        ref[0:8, :] = zeros
        ref[PADDED - 8 : PADDED, :] = zeros
    res[8:16, :] = top[...]
    res[FIRST + ROWS : FIRST + ROWS + 8, :] = bot[...]
    res[FIRST : FIRST + ROWS, :] = target[...]

    center = (MAXIMUM + MINIMUM) / 2.0
    half_span = (MAXIMUM - MINIMUM) / 2.0
    ratio = center / half_span

    @pl.loop(1, blocks - 1)
    def _(e):
        down_face, cell = fr[block(e), :], fc[block(e), :]
        diagonal = (
            sg[block(e), :]
            + above(down_face, fr[block(e - 1), :], first)
            + down_face
            + pltpu.roll(cell, 1, 1)
            + cell
        )
        outside = ((strip == 0) & (e == 1)) | (
            (strip == lax.axis_size("space") - 1) & (e == blocks - 2)
        )
        inverse = jnp.where(outside, 0.0, 1.0 / diagonal)
        dinv[block(e), :] = inverse
        step = res[block(e), :] * inverse / center
        s0[block(e), :] = step
        c[block(e), :] = step

    def operate(ref, e):
        cur = ref[block(e), :]
        down_face = fr[block(e), :]
        up_face = above(down_face, fr[block(e - 1), :], first)
        image = sg[block(e), :] * cur
        image += up_face * (cur - above(cur, ref[block(e - 1), :], first))
        image += down_face * (cur - below(cur, ref[block(e + 1), :], last))
        flow = fc[block(e), :] * (cur - pltpu.roll(cur, COLS - 1, 1))
        return cur, image + (flow - pltpu.roll(flow, 1, 1))

    old = 1.0 / ratio
    now, then = s0, s1
    for _sweep in range(SWEEPS - 1):
        new = 1.0 / (2.0 * ratio - old)

        @pl.loop(1, blocks - 1)
        def _(e):
            cur, image = operate(now, e)
            left = res[block(e), :] - image
            res[block(e), :] = left
            step = new * old * cur + (2.0 * new / half_span) * (left * dinv[block(e), :])
            then[block(e), :] = step
            c[block(e), :] += step

        now, then = then, now
        old = new

    def body(i, carry):
        tc, ca = carry
        cur, image = operate(c, i + 2)
        c_out[block(i), :] = cur
        return tc + target[block(i), :] * cur, ca + cur * image

    tc, ca = lax.fori_loop(0, ROWS // 8, body, (zeros, zeros))
    sums[...] = jnp.zeros_like(sums)
    sums[0:1, :] = jnp.full((1, 128), jnp.sum(tc), jnp.float32)
    sums[1:2, :] = jnp.full((1, 128), jnp.sum(ca), jnp.float32)


def chebyshev(target, top, bot, sg, fr, fc):
    return pl.pallas_call(
        chebyshev_kernel,
        in_specs=[VMEM] * 6,
        out_specs=[VMEM] * 2,
        out_shape=[struct(ROWS, COLS), struct(8, 128)],
        scratch_shapes=[pltpu.VMEM((PADDED, COLS), jnp.float32)] * 5,
        compiler_params=LIMIT,
        cost_estimate=pl.CostEstimate(flops=20_000_000, bytes_accessed=4_000_000, transcendentals=0),
    )(target, top, bot, sg, fr, fc)


def step_length(sums):
    return jnp.sum(sums[0:1, 0:1]) / jnp.sum(sums[1:2, 0:1])


def signed():
    tm = lax.axis_index("tm")
    return jnp.where(tm < lax.axis_size("tm") // 2, 1.0, -1.0).astype(jnp.float32)


def correct_kernel(sums, c, out):
    out[...] = step_length(sums) * c[...]


def correct(sums, c):
    return pl.pallas_call(
        correct_kernel,
        in_specs=[VMEM] * 2,
        out_specs=VMEM,
        out_shape=struct(ROWS, COLS),
    )(sums, c)


def first_kernel(p, opposite, correction, out):
    out[...] = p[...] - 0.5 * (p[...] + opposite[...]) + signed() * correction[...][None]


def next_kernel(_, p, opposite, correction, out):
    first_kernel(p, opposite, correction, out)


def update(done, p, opposite, correction, start):
    tile = (STEPS, TILE, COLS)
    at = start // TILE
    specs = [
        pl.BlockSpec(tile, lambda i: (0, at + i, 0)),
        pl.BlockSpec(tile, lambda i: (0, i, 0)),
        pl.BlockSpec((TILE, COLS), lambda i: (at + i, 0)),
    ]
    operands = (p, opposite, correction)
    return pl.pallas_call(
        first_kernel if done is None else next_kernel,
        grid=(opposite.shape[1] // TILE,),
        in_specs=specs if done is None else [ANY] + specs,
        out_specs=pl.BlockSpec(tile, lambda i: (0, at + i, 0)),
        out_shape=struct(STEPS, ROWS, COLS),
        input_output_aliases={} if done is None else {0: 0},
        compiler_params=LIMIT,
    )(*(operands if done is None else (done,) + operands))


def per_device(p, source, offsets, ids, nu_t, sg_t):
    moments = lax.axis_size("tm")
    strips = lax.axis_size("space")
    across = [(i, (i + moments // 2) % moments) for i in range(moments)]
    to_next = [(i, i + 1) for i in range(strips - 1)]
    to_prev = [(j, i) for i, j in to_next]

    early = lax.ppermute(p[:, :EARLY], "tm", across)
    down, up = edges(p, ids)
    top = lax.ppermute(up, "space", to_next)
    bot = lax.ppermute(down, "space", to_prev)
    mine, send, sg, fr, fc = residual(offsets, nu_t, sg_t, p, source, ids, top, bot)

    mine, send = halves(mine, swap(send, 1))
    blocks = merge(mine, swap(send, 2), early, moments // 4)
    x = among_z(total_for_all(among_z(blocks)))
    late = lax.ppermute(gate(p[:, EARLY:], x), "tm", across)
    other = swap(x, 2)
    core_part = swap(jnp.concatenate([x, other]), 1)
    target, first_rows, last_rows = assemble(x, other, core_part)
    t_top = lax.ppermute(last_rows, "space", to_next)
    t_bot = lax.ppermute(first_rows, "space", to_prev)

    c, sums = chebyshev(target, t_top, t_bot, sg, fr, fc)
    every = jnp.broadcast_to(sums[None], (strips,) + sums.shape)
    sums = lax.all_to_all(every, "space", 0, 0).sum(0)
    correction = correct(sums, c)
    updated = update(None, p, early, correction, 0)
    return update(updated, p, late, correction, EARLY), correction


def solution(mesh):
    placed = (P("tm", "space", None), P("tm", "space", None), P("tm"), P("space", None), P(), P())
    return jax.shard_map(
        per_device,
        mesh=mesh,
        in_specs=placed,
        out_specs=(P("tm", "space", None), P("space", None)),
        check_vma=False,
    )
```

time: 430 us -> 149 us (0.35)
  waiting for transfers between devices: 239 us -> 31.9 us
  other arithmetic: 80.1 us -> 1.52 us
  Pallas kernels: 0 us -> 42.6 us
  starting transfers between devices: 55.1 us -> 29.1 us
  between operations: 18.3 us -> 0.79 us
    psum x1 -> x0, waiting for transfers between devices: 226 us -> none  [per_device(): desired_result = lax.psum(target_part, 'tm')]
    pallas_call x0 -> x11, Pallas kernels: none -> 42.6 us  [the longest x1 13.7 us: residual(): pl.pallas_call(residual_kernel, in_specs=[SMEM] * 3 + [VMEM] * 5, out_spe...]
    add x6 -> x0, other arithmetic: 35.6 us -> none  [the longest x3 19.8 us: lookup(): result + jnp.where(region_map == region, table[region], jnp.float32(0.0))]
    div x10 -> x0, other arithmetic: 31.8 us -> none  [the longest x1 18.3 us: per_device(): target_part = combined_accumulation / overall_summation]
    ppermute x13 -> x10, starting transfers between devices: 55.1 us -> 25.8 us  [the longest x1 7.28 us: per_device(): early = lax.ppermute(p[:, :EARLY], 'tm', across)]
    all_to_all x0 -> x2, blocking collectives: none -> 25.8 us  [the longest x1 13.1 us: among_z(): return lax.all_to_all(blocks, 'tm', 0, 0, axis_index_groups=groups)]
    psum x1 -> x0, blocking collectives: 21.9 us -> none  [per_device(): lax.psum((jnp.sum(desired_result * corr), jnp.sum(corr * image)), 'space')]
    reduce_sum x2 -> x1, other arithmetic: 12.5 us -> 0.6 us  [per_device(): sums = lax.all_to_all(every, 'space', 0, 0).sum(0)]
  transfers between devices with their start and end apart: 14 -> 11, of which waited for: 5 -> 10; matrix products, arithmetic and copies ran while one was open for 21% -> 2% of each run, Pallas kernels for 0% -> 24%
where the time goes in v1:
time: 149 us; the launch traced here: 148 us
  Pallas kernels  42.6 us (29%)
  waiting for transfers between devices  31.9 us (21%)
  starting transfers between devices  29.1 us (20%)
  blocking collectives  25.8 us (17%)
  local copies, waits for them, and re-layouts  16.1 us (11%)
  other arithmetic  1.52 us (1%)
    pallas_call x1, Pallas kernels, residual(): pl.pallas_call(residual_kernel, in_specs=[SMEM] * 3 + [VMEM] * 5, out_spe...  13.7 us
    all_to_all x1, blocking collectives, among_z(): return lax.all_to_all(blocks, 'tm', 0, 0, axis_index_groups=groups)  13.1 us
    unnamed x44, local copies, waits for them, and re-layouts  12.8 us
    ppermute x4, waiting for transfers between devices, swap(): lax.ppermute(x, 'tm', [(i, i ^ bit) for i in range(lax.axis_size('tm'))])  12.8 us
    pallas_call x1, Pallas kernels, chebyshev(): pl.pallas_call(chebyshev_kernel, in_specs=[VMEM] * 6, out_specs=[VMEM] *...  12.8 us
    all_to_all x1, blocking collectives, per_device(): sums = lax.all_to_all(every, 'space', 0, 0).sum(0)  12.7 us
    all_to_all x1, waiting for transfers between devices, among_z(): return lax.all_to_all(blocks, 'tm', 0, 0, axis_index_groups=groups)  7.76 us
    ppermute x1, starting transfers between devices, per_device(): early = lax.ppermute(p[:, :EARLY], 'tm', across)  7.28 us
  transfers between devices with their start and end apart: 11, of which 10 were waited for; matrix products, arithmetic and copies ran while one was open for 2% of the time, Pallas kernels for 24%

profile of v1, /device:TPU:2, one launch (start us, length us, event | category | flops | bytes accessed | tf_op | source)
XLA Modules:
  0.0 147.7 jit_solution(7227059774866752931)
XLA Ops:
  0.6 2.1 %slice.6 = f32[4,48,1024]{2,1,0:T(8,128)} slice(f32[4,128,1024]{2,1,0:T(8,128)} %p.5), slice={[0:4], [0:48], [0:1024]} | slice | bytes 1572864 | tf_op jit(solution)/shard_map/slice | solution.py:412
  2.7 7.3 %collective-permute-start = (f32[4,48,1024]{2,1,0:T(8,128)}, f32[4,48,1024]{2,1,0:T(8,128)S(1)}, u32[]{:S(2)}, u32[]{:S(2)}) collective-permute-start(f32[4,48,1024]{2,1,0:T(8,128)} %slice.6), channel_id=1, source_target_pairs={{0,128},{8,136},{16,144},{24,152},{32,160},{40,168},{48,176},{56,1... | collective-permute-start | bytes 2359304 | tf_op jit(solution)/shard_map/ppermute | solution.py:412
  10.0 1.6 %shard_map.77 = (f32[16,1024]{1,0:T(8,128)}, f32[16,1024]{1,0:T(8,128)}) custom-call(f32[4,128,1024]{2,1,0:T(8,128)} %p.5, f32[4,128,1024]{2,1,0:T(8,128)} %p.5, s32[128,1024]{1,0:T(8,128)} %ids.1, s32[128,1024]{1,0:T(8,128)} %ids.1), custom_call_target="tpu_custom_call" | custom-call | tf_op jit(solution)/shard_map/pallas_call | solution.py:64
  11.7 5.1 %collective-permute-start.1 = (f32[16,1024]{1,0:T(8,128)}, f32[16,1024]{1,0:T(8,128)S(1)}, u32[]{:S(2)}, u32[]{:S(2)}) collective-permute-start(f32[16,1024]{1,0:T(8,128)} %get-tuple-element.16), channel_id=1, source_target_pairs={{0,1},{1,2},{2,3},{3,4},{4,5},{5,6},{6,7},{8,9},{9,10},{10,11},{11... | collective-permute-start | bytes 196616 | tf_op jit(solution)/shard_map/ppermute | solution.py:414
  16.8 3.1 %collective-permute-start.2 = (f32[16,1024]{1,0:T(8,128)}, f32[16,1024]{1,0:T(8,128)S(1)}, u32[]{:S(2)}, u32[]{:S(2)}) collective-permute-start(f32[16,1024]{1,0:T(8,128)} %get-tuple-element.17), channel_id=1, source_target_pairs={{1,0},{2,1},{3,2},{4,3},{5,4},{6,5},{7,6},{9,8},{10,9},{11,10},{12... | collective-permute-start | bytes 196616 | tf_op jit(solution)/shard_map/ppermute | solution.py:415
  20.4 4.2 %collective-permute-done.2.bot = f32[16,1024]{1,0:T(8,128)S(1)} collective-permute-done((f32[16,1024]{1,0:T(8,128)}, f32[16,1024]{1,0:T(8,128)S(1)}, u32[]{:S(2)}, u32[]{:S(2)}) %collective-permute-start.2) | collective-permute-done | bytes 65568 | tf_op jit(solution)/shard_map/ppermute | solution.py:415
  24.7 1.6 %copy-done.5 = f32[4,128,1024]{2,1,0:T(8,128)S(1)} copy-done((f32[4,128,1024]{2,1,0:T(8,128)S(1)}, f32[4,128,1024]{2,1,0:T(8,128)}, u32[]{:S(2)}) %copy-start.5) | copy-done | bytes 2097176
  26.3 13.7 %shard_map.78 = (f32[64,1024]{1,0:T(8,128)S(1)}, f32[64,1024]{1,0:T(8,128)S(1)}, f32[160,1024]{1,0:T(8,128)S(1)}, f32[160,1024]{1,0:T(8,128)S(1)}, f32[160,1024]{1,0:T(8,128)S(1)}) custom-call(s32[4]{0:T(128)S(1)} %copy-done.15, f32[8]{0:T(128)S(1)} %copy-done.16, f32[8]{0:T(128)S(1)} %copy-done.17, f32[4,128,1024]{2,1,0:T(8,128)S(1)} %copy-done, ...), custom_call_target="tpu_custom_call" | custom-call | flops 20000000 | bytes 8000000 | tf_op jit(solution)/shard_map/pallas_call | solution.py:165
  43.2 1.5 %collective-permute-done.3.b = f32[64,1024]{1,0:T(8,128)S(1)} collective-permute-done((f32[64,1024]{1,0:T(8,128)S(1)}, f32[64,1024]{1,0:T(8,128)S(1)}, u32[]{:S(2)}, u32[]{:S(2)}) %collective-permute-start.3) | collective-permute-done | bytes 262176 | tf_op jit(solution)/shard_map/ppermute | solution.py:177
  45.5 1.7 %shard_map.79 = (f32[32,1024]{1,0:T(8,128)}, f32[32,1024]{1,0:T(8,128)}) custom-call(f32[64,1024]{1,0:T(8,128)} %copy-done.14, f32[64,1024]{1,0:T(8,128)} %copy-done.20), custom_call_target="tpu_custom_call" | custom-call | tf_op jit(solution)/shard_map/pallas_call | solution.py:188
  47.9 5.1 %collective-permute-done.4.b = f32[32,1024]{1,0:T(8,128)S(1)} collective-permute-done((f32[32,1024]{1,0:T(8,128)}, f32[32,1024]{1,0:T(8,128)S(1)}, u32[]{:S(2)}, u32[]{:S(2)}) %collective-permute-start.4) | collective-permute-done | bytes 131104 | tf_op jit(solution)/shard_map/ppermute | solution.py:177
  53.9 1.6 %shard_map.80 = f32[8,32,128]{2,1,0:T(8,128)} custom-call(f32[32,1024]{1,0:T(8,128)} %get-tuple-element.20.a, f32[32,1024]{1,0:T(8,128)} %copy-done.21, f32[4,48,1024]{2,1,0:T(8,128)} %copy-done.3), custom_call_target="tpu_custom_call" | custom-call | tf_op jit(solution)/shard_map/pallas_call | solution.py:203
  55.5 13.1 %all_to_all.15.parts = f32[8,32,128]{2,1,0:T(8,128)} all-to-all(f32[8,32,128]{2,1,0:T(8,128)} %shard_map.80), channel_id=1, replica_groups={{0,32,64,96,128,160,192,224},{8,40,72,104,136,168,200,232},{16,48,80,11..., dimensions={0} | all-to-all | bytes 262144 | tf_op jit(solution)/shard_map/all_to_all | solution.py:230
  68.6 1.6 %shard_map.81 = f32[8,32,128]{2,1,0:T(8,128)} custom-call(f32[8,32,128]{2,1,0:T(8,128)} %all_to_all.15.parts), custom_call_target="tpu_custom_call" | custom-call | tf_op jit(solution)/shard_map/pallas_call | solution.py:220
  70.1 3.4 %all-to-all-start.1 = ((f32[8,32,128]{2,1,0:T(8,128)}), f32[8,32,128]{2,1,0:T(8,128)S(1)}, u32[]{:S(2)}, u32[]{:S(2)}) async-start(f32[8,32,128]{2,1,0:T(8,128)} %shard_map.81), calls=%async_computation.1 | async-start | bytes 262144 | tf_op jit(solution)/shard_map/all_to_all | solution.py:230
  73.5 1.2 slice.7.value
  74.7 7.8 %all-to-all-done.1.x._ = f32[8,32,128]{2,1,0:T(8,128)S(1)} async-done(((f32[8,32,128]{2,1,0:T(8,128)}), f32[8,32,128]{2,1,0:T(8,128)S(1)}, u32[]{:S(2)}, u32[]{:S(2)}) %all-to-all-start.1) | async-done | bytes 131104 | tf_op jit(solution)/shard_map/all_to_all | solution.py:230
  84.4 4.5 %collective-permute-done.5.other = f32[8,32,128]{2,1,0:T(8,128)S(1)} collective-permute-done((f32[8,32,128]{2,1,0:T(8,128)}, f32[8,32,128]{2,1,0:T(8,128)S(1)}, u32[]{:S(2)}, u32[]{:S(2)}) %collective-permute-start.5) | collective-permute-done | bytes 131104 | tf_op jit(solution)/shard_map/ppermute | solution.py:177
  90.6 1.7 %collective-permute-done.6.core_part = f32[16,32,128]{2,1,0:T(8,128)} collective-permute-done((f32[16,32,128]{2,1,0:T(8,128)S(1)}, f32[16,32,128]{2,1,0:T(8,128)}, u32[]{:S(2)}, u32[]{:S(2)}) %collective-permute-start.6) | collective-permute-done | bytes 262176 | tf_op jit(solution)/shard_map/ppermute | solution.py:177
  92.2 1.9 %shard_map.82 = (f32[128,1024]{1,0:T(8,128)}, f32[8,1024]{1,0:T(8,128)}, f32[8,1024]{1,0:T(8,128)}) custom-call(f32[8,32,128]{2,1,0:T(8,128)} %copy-done.18, f32[8,32,128]{2,1,0:T(8,128)} %copy-done.19, f32[16,32,128]{2,1,0:T(8,128)} %collective-permute-done.6.core_part), custom_call_target="tpu_custom_call" | custom-call | tf_op jit(solution)/shard_map/pallas_call | solution.py:261
  94.2 4.6 %collective-permute-start.7 = (f32[8,1024]{1,0:T(8,128)}, f32[8,1024]{1,0:T(8,128)S(1)}, u32[]{:S(2)}, u32[]{:S(2)}) collective-permute-start(f32[8,1024]{1,0:T(8,128)} %get-tuple-element.23), channel_id=1, source_target_pairs={{0,1},{1,2},{2,3},{3,4},{4,5},{5,6},{6,7},{8,9},{9,10},{10,11},{11... | collective-permute-start | bytes 98312 | tf_op jit(solution)/shard_map/ppermute | solution.py:425
  98.7 3.7 %collective-permute-start.8 = (f32[8,1024]{1,0:T(8,128)}, f32[8,1024]{1,0:T(8,128)S(1)}, u32[]{:S(2)}, u32[]{:S(2)}) collective-permute-start(f32[8,1024]{1,0:T(8,128)} %get-tuple-element.24), channel_id=1, source_target_pairs={{1,0},{2,1},{3,2},{4,3},{5,4},{6,5},{7,6},{9,8},{10,9},{11,10},{12... | collective-permute-start | bytes 98312 | tf_op jit(solution)/shard_map/ppermute | solution.py:426
  102.6 3.7 %collective-permute-done.8.bot = f32[8,1024]{1,0:T(8,128)S(1)} collective-permute-done((f32[8,1024]{1,0:T(8,128)}, f32[8,1024]{1,0:T(8,128)S(1)}, u32[]{:S(2)}, u32[]{:S(2)}) %collective-permute-start.8) | collective-permute-done | bytes 32800 | tf_op jit(solution)/shard_map/ppermute | solution.py:426
  106.3 1.1 copy-done.9
  107.3 1.1 copy-done.11
  109.5 12.8 %shard_map.83 = (f32[128,1024]{1,0:T(8,128)S(1)}, f32[8,128]{1,0:T(8,128)S(1)}) custom-call(f32[128,1024]{1,0:T(8,128)S(1)} %copy-done.12, f32[8,1024]{1,0:T(8,128)S(1)} %collective-permute-done.7.top, f32[8,1024]{1,0:T(8,128)S(1)} %collective-permute-done.8.bot, f32[160,1024]{1,0:T(8,128)S(1)} %copy-done.7, f32[160,1024]{1,0:T(8,128)S(1)} %copy-done.9, ...), custom_call_target="tpu_custom_call" | custom-call | flops 20000000 | bytes 4000000 | tf_op jit(solution)/shard_map/pallas_call | solution.py:344
  123.0 12.7 %all_to_all.16 = f32[8,8,128]{2,1,0:T(8,128)S(1)} all-to-all(f32[8,8,128]{2,1,0:T(8,128)S(1)} %broadcast_in_dim.2), channel_id=1, replica_groups=mesh['tm'=32,'space'=8] {'space'}, dimensions={0} | all-to-all | bytes 65536 | tf_op jit(solution)/shard_map/all_to_all | solution.py:430
  136.3 1.9 %shard_map.84.correction = f32[128,1024]{1,0:T(8,128)} custom-call(f32[8,128]{1,0:T(8,128)} %reduce_sum.9.sums, f32[128,1024]{1,0:T(8,128)} %copy-done.13), custom_call_target="tpu_custom_call" | custom-call | tf_op jit(solution)/shard_map/pallas_call | solution.py:369
  138.3 1.0 copy-done.2
  139.3 1.6 %shard_map.85._ = f32[4,128,1024]{2,1,0:T(8,128)} custom-call(f32[4,128,1024]{2,1,0:T(8,128)S(1)} %copy-done, f32[4,48,1024]{2,1,0:T(8,128)S(1)} %copy-done.4, f32[128,1024]{1,0:T(8,128)S(1)} %copy-done.2), custom_call_target="tpu_custom_call" | custom-call | tf_op jit(solution)/shard_map/pallas_call | solution.py:394
  140.9 2.8 %collective-permute-done.9.opposite = f32[4,80,1024]{2,1,0:T(8,128)} collective-permute-done((f32[4,80,1024]{2,1,0:T(8,128)}, f32[4,80,1024]{2,1,0:T(8,128)}, u32[]{:S(2)}, u32[]{:S(2)}) %collective-permute-start.9) | collective-permute-done | bytes 1310752 | tf_op jit(solution)/shard_map/ppermute | solution.py:421
  143.7 4.0 %shard_map.87 = f32[4,128,1024]{2,1,0:T(8,128)} custom-call(f32[4,128,1024]{2,1,0:T(8,128)} %shard_map.85._, f32[4,128,1024]{2,1,0:T(8,128)S(1)} %copy-done, f32[4,80,1024]{2,1,0:T(8,128)} %collective-permute-done.9.opposite, f32[128,1024]{1,0:T(8,128)S(1)} %copy-done.2), custom_call_target="tpu_custom_call", output_to_operand_aliasing={{}: (0, {})} | custom-call | tf_op jit(solution)/shard_map/pallas_call | solution.py:394
  (52 shorter events, 12.2 us)
Async XLA Ops:
  2.7 21.9 %copy-start = (f32[4,128,1024]{2,1,0:T(8,128)S(1)}, f32[4,128,1024]{2,1,0:T(8,128)}, u32[]{:S(2)}) copy-start(f32[4,128,1024]{2,1,0:T(8,128)} %p.5) | copy-start | bytes 6291460
  2.7 21.9 %copy-start.1 = (s32[128,1024]{1,0:T(8,128)S(1)}, s32[128,1024]{1,0:T(8,128)}, u32[]{:S(2)}) copy-start(s32[128,1024]{1,0:T(8,128)} %ids.1) | copy-start | bytes 1572868
  2.7 21.9 %copy-start.15 = (s32[4]{0:T(128)S(1)}, s32[4]{0:T(128)}, u32[]{:S(2)}) copy-start(s32[4]{0:T(128)} %offs.1) | copy-start | bytes 52
  2.7 21.9 %copy-start.16 = (f32[8]{0:T(128)S(1)}, f32[8]{0:T(128)}, u32[]{:S(2)}) copy-start(f32[8]{0:T(128)} %nu_t.1) | copy-start | bytes 100
  2.7 21.9 %copy-start.17 = (f32[8]{0:T(128)S(1)}, f32[8]{0:T(128)}, u32[]{:S(2)}) copy-start(f32[8]{0:T(128)} %sg_t.1) | copy-start | bytes 100
  2.7 50.2 %collective-permute-start = (f32[4,48,1024]{2,1,0:T(8,128)}, f32[4,48,1024]{2,1,0:T(8,128)S(1)}, u32[]{:S(2)}, u32[]{:S(2)}) collective-permute-start(f32[4,48,1024]{2,1,0:T(8,128)} %slice.6), channel_id=1, source_target_pairs={{0,128},{8,136},{16,144},{24,152},{32,160},{40,168},{48,176},{56,1... | collective-permute-start | bytes 2359304 | tf_op jit(solution)/shard_map/ppermute | solution.py:412
  11.7 8.8 %collective-permute-start.1 = (f32[16,1024]{1,0:T(8,128)}, f32[16,1024]{1,0:T(8,128)S(1)}, u32[]{:S(2)}, u32[]{:S(2)}) collective-permute-start(f32[16,1024]{1,0:T(8,128)} %get-tuple-element.16), channel_id=1, source_target_pairs={{0,1},{1,2},{2,3},{3,4},{4,5},{5,6},{6,7},{8,9},{9,10},{10,11},{11... | collective-permute-start | bytes 196616 | tf_op jit(solution)/shard_map/ppermute | solution.py:414
  16.8 7.9 %collective-permute-start.2 = (f32[16,1024]{1,0:T(8,128)}, f32[16,1024]{1,0:T(8,128)S(1)}, u32[]{:S(2)}, u32[]{:S(2)}) collective-permute-start(f32[16,1024]{1,0:T(8,128)} %get-tuple-element.17), channel_id=1, source_target_pairs={{1,0},{2,1},{3,2},{4,3},{5,4},{6,5},{7,6},{9,8},{10,9},{11,10},{12... | collective-permute-start | bytes 196616 | tf_op jit(solution)/shard_map/ppermute | solution.py:415
  24.7 1.6 %copy-start.5 = (f32[4,128,1024]{2,1,0:T(8,128)S(1)}, f32[4,128,1024]{2,1,0:T(8,128)}, u32[]{:S(2)}) copy-start(f32[4,128,1024]{2,1,0:T(8,128)} %src.1) | copy-start | bytes 6291460
  40.0 0.9 copy-start.6
  40.8 0.8 copy-start.8
  41.7 0.9 copy-start.10
  42.5 0.7 copy-start.14
  43.2 1.5 %collective-permute-start.3 = (f32[64,1024]{1,0:T(8,128)S(1)}, f32[64,1024]{1,0:T(8,128)S(1)}, u32[]{:S(2)}, u32[]{:S(2)}) collective-permute-start(f32[64,1024]{1,0:T(8,128)S(1)} %get-tuple-element.19), channel_id=1, source_target_pairs={{0,8},{8,0},{16,24},{24,16},{32,40},{40,32},{48,56},{56,48},{64,72... | collective-permute-start | bytes 786440 | tf_op jit(solution)/shard_map/ppermute | solution.py:177
  44.8 0.7 copy-start.20
  47.2 5.7 %collective-permute-start.4 = (f32[32,1024]{1,0:T(8,128)}, f32[32,1024]{1,0:T(8,128)S(1)}, u32[]{:S(2)}, u32[]{:S(2)}) collective-permute-start(f32[32,1024]{1,0:T(8,128)} %get-tuple-element.21), channel_id=1, source_target_pairs={{0,16},{8,24},{16,0},{24,8},{32,48},{40,56},{48,32},{56,40},{64,80... | collective-permute-start | bytes 393224 | tf_op jit(solution)/shard_map/ppermute | solution.py:177
  53.0 0.7 copy-start.21
  53.0 0.9 copy-start.3
  70.1 12.4 %all-to-all-start.1 = ((f32[8,32,128]{2,1,0:T(8,128)}), f32[8,32,128]{2,1,0:T(8,128)S(1)}, u32[]{:S(2)}, u32[]{:S(2)}) async-start(f32[8,32,128]{2,1,0:T(8,128)} %shard_map.81), calls=%async_computation.1 | async-start | bytes 262144 | tf_op jit(solution)/shard_map/all_to_all | solution.py:230
  74.7 31.5 %copy-start.7 = (f32[160,1024]{1,0:T(8,128)S(1)}, f32[160,1024]{1,0:T(8,128)}, u32[]{:S(2)}) copy-start(f32[160,1024]{1,0:T(8,128)} %copy-done.6) | copy-start | bytes 1966084
  83.1 60.5 %collective-permute-start.9 = (f32[4,80,1024]{2,1,0:T(8,128)}, f32[4,80,1024]{2,1,0:T(8,128)}, u32[]{:S(2)}, u32[]{:S(2)}) collective-permute-start(f32[4,80,1024]{2,1,0:T(8,128)} %shard_map.86), channel_id=1, source_target_pairs={{0,128},{8,136},{16,144},{24,152},{32,160},{40,168},{48,176},{56,1... | collective-permute-start | bytes 3932168 | tf_op jit(solution)/shard_map/ppermute | solution.py:421
  83.7 5.2 %collective-permute-start.5 = (f32[8,32,128]{2,1,0:T(8,128)}, f32[8,32,128]{2,1,0:T(8,128)S(1)}, u32[]{:S(2)}, u32[]{:S(2)}) collective-permute-start(f32[8,32,128]{2,1,0:T(8,128)} %copy-done.18), channel_id=1, source_target_pairs={{0,16},{8,24},{16,0},{24,8},{32,48},{40,56},{48,32},{56,40},{64,80... | collective-permute-start | bytes 393224 | tf_op jit(solution)/shard_map/ppermute | solution.py:177
  88.9 0.7 copy-start.19
  90.5 47.8 %copy-start.4 = (f32[4,48,1024]{2,1,0:T(8,128)S(1)}, f32[4,48,1024]{2,1,0:T(8,128)}, u32[]{:S(2)}) copy-start(f32[4,48,1024]{2,1,0:T(8,128)} %copy-done.3) | copy-start | bytes 2359300
  90.5 1.8 %collective-permute-start.6 = (f32[16,32,128]{2,1,0:T(8,128)S(1)}, f32[16,32,128]{2,1,0:T(8,128)}, u32[]{:S(2)}, u32[]{:S(2)}) collective-permute-start(f32[16,32,128]{2,1,0:T(8,128)S(1)} %pad_maximum_fusion), channel_id=1, source_target_pairs={{0,8},{8,0},{16,24},{24,16},{32,40},{40,32},{48,56},{56,48},{64,72... | collective-permute-start | bytes 786440 | tf_op jit(solution)/shard_map/ppermute | solution.py:177
  94.2 8.4 %collective-permute-start.7 = (f32[8,1024]{1,0:T(8,128)}, f32[8,1024]{1,0:T(8,128)S(1)}, u32[]{:S(2)}, u32[]{:S(2)}) collective-permute-start(f32[8,1024]{1,0:T(8,128)} %get-tuple-element.23), channel_id=1, source_target_pairs={{0,1},{1,2},{2,3},{3,4},{4,5},{5,6},{6,7},{8,9},{9,10},{10,11},{11... | collective-permute-start | bytes 98312 | tf_op jit(solution)/shard_map/ppermute | solution.py:425
  98.7 7.5 %collective-permute-start.8 = (f32[8,1024]{1,0:T(8,128)}, f32[8,1024]{1,0:T(8,128)S(1)}, u32[]{:S(2)}, u32[]{:S(2)}) collective-permute-start(f32[8,1024]{1,0:T(8,128)} %get-tuple-element.24), channel_id=1, source_target_pairs={{1,0},{2,1},{3,2},{4,3},{5,4},{6,5},{7,6},{9,8},{10,9},{11,10},{12... | collective-permute-start | bytes 98312 | tf_op jit(solution)/shard_map/ppermute | solution.py:426
  106.3 1.1 copy-start.9
  107.3 1.1 copy-start.11
  108.4 1.0 copy-start.12
  122.2 0.8 copy-start.13
  138.3 1.0 copy-start.2
  (1 other events, 0.6 us)

commit v2 on v1

v2 whole, which is shorter than its diff:
```python
import functools

import jax
import jax.numpy as jnp
from jax import lax
from jax.experimental import pallas as pl
from jax.experimental.pallas import tpu as pltpu
from jax.sharding import PartitionSpec as P

SLOT_W = 8
REGIONS = 8
SWEEPS = 4
MINIMUM = 0.2
MAXIMUM = 2.0
ROWS = 128
COLS = 1024
STEPS = 4
EXTENDED = ROWS + 16
CHUNKS = (40, 16, 16, 40, 16)
TILE = 8

ANY = pl.BlockSpec(memory_space=pl.ANY)
VMEM = pl.BlockSpec(memory_space=pltpu.VMEM)
SMEM = pl.BlockSpec(memory_space=pltpu.SMEM)
LIMIT = pltpu.CompilerParams(vmem_limit_bytes=16 * 1024 * 1024)


def struct(*shape):
    return jax.ShapeDtypeStruct(shape, jnp.float32)


def block(i):
    return pl.ds(pl.multiple_of(i * 8, 8), 8)


def harmonic(left, right):
    return 2.0 * left * right / (left + right)


def above(cur, prev, first):
    return jnp.where(first, pltpu.roll(prev, 1, 0), pltpu.roll(cur, 1, 0))


def below(cur, after, last):
    return jnp.where(last, pltpu.roll(after, 7, 0), pltpu.roll(cur, 7, 0))


def row_masks():
    rows = lax.broadcasted_iota(jnp.int32, (8, COLS), 0)
    return rows == 0, rows == 7


def edges_kernel(first_p, last_p, first_ids, last_ids, down_ref, up_ref):
    for out, p, ids, row in ((down_ref, first_p, first_ids, 0), (up_ref, last_p, last_ids, 7)):
        for k in range(STEPS):
            out[k : k + 1, :] = p[k, row : row + 1, :]
            out[STEPS + k : STEPS + k + 1, :] = p[k, row : row + 1, :]
        out[8:16, :] = ids[...].astype(jnp.float32)


def edges(p, ids):
    tail = ROWS // 8 - 1
    return pl.pallas_call(
        edges_kernel,
        grid=(1,),
        in_specs=[
            pl.BlockSpec((STEPS, 8, COLS), lambda i: (0, 0, 0)),
            pl.BlockSpec((STEPS, 8, COLS), lambda i: (0, tail, 0)),
            pl.BlockSpec((8, COLS), lambda i: (0, 0)),
            pl.BlockSpec((8, COLS), lambda i: (tail, 0)),
        ],
        out_specs=[pl.BlockSpec((16, COLS), lambda i: (0, 0))] * 2,
        out_shape=[struct(16, COLS)] * 2,
        compiler_params=LIMIT,
    )(p, p, ids, ids)


def lookup(region, table):
    value = jnp.full(region.shape, table[0], jnp.float32)
    for r in range(1, REGIONS):
        value = jnp.where(region == r, table[r], value)
    return value


def stencil(load, count, fr, sg, fc, use):
    first, last = row_masks()
    cur = load(0)
    cur_up = pltpu.roll(cur, 7, 0)
    flow_before = jnp.zeros((8, COLS), jnp.float32)
    for b in range(count):
        if b + 1 < count:
            after = load(b + 1)
            after_up = pltpu.roll(after, 7, 0)
        else:
            after, after_up = cur, cur_up
        down = fr(b) * (cur - jnp.where(last, after_up, cur_up))
        down_rolled = pltpu.roll(down, 1, 0)
        side = fc(b) * (cur - pltpu.roll(cur, COLS - 1, 1))
        image = sg(b) * cur + (down - jnp.where(first, flow_before, down_rolled))
        image = image + (side - pltpu.roll(side, 1, 1))
        use(b, cur, image)
        cur, cur_up, flow_before = after, after_up, down_rolled


def rows8(b):
    return slice(8 * b, 8 * b + 8)


def residual_kernel(offs, nu_t, sg_t, p, src, ids, acc, nu, sg, fr, fc):
    first, last = row_masks()
    strip, tm = lax.axis_index("space"), lax.axis_index("tm")
    blocks = ROWS // 8
    for b in range(blocks):
        region = ids[rows8(b), :]
        nu[rows8(b), :] = lookup(region, nu_t)
        sg[rows8(b), :] = lookup(region, sg_t)
    for b in range(blocks):
        cur = nu[rows8(b), :]
        after = nu[rows8(min(b + 1, blocks - 1)), :]
        face = harmonic(cur, below(cur, after, last))
        if b == blocks - 1:
            face = jnp.where(last, 0.0, face)
        fr[rows8(b), :] = face
        fc[rows8(b), :] = harmonic(cur, pltpu.roll(cur, COLS - 1, 1))
    scale = signed() / (STEPS * lax.axis_size("tm"))
    acc[...] = jnp.zeros_like(acc)

    @pl.loop(0, STEPS)
    def _(k):
        own = jnp.where(strip < lax.axis_size("space") // 2, offs[k] * SLOT_W, 0)
        back = (-own) & (COLS - 1)

        def use(b, _, image):
            part = src[k, rows8(b), :] - pltpu.roll(image, own, 1)
            acc[rows8(b), :] += scale * part

        stencil(
            lambda b: pltpu.roll(p[k, rows8(b), :], back, 1),
            blocks,
            lambda b: fr[rows8(b), :],
            lambda b: sg[rows8(b), :],
            lambda b: fc[rows8(b), :],
            use,
        )


def residual(offs, nu_t, sg_t, p, src, ids):
    return pl.pallas_call(
        residual_kernel,
        in_specs=[SMEM] * 3 + [VMEM] * 3,
        out_specs=VMEM,
        out_shape=struct(ROWS, COLS),
        scratch_shapes=[pltpu.VMEM((ROWS, COLS), jnp.float32)] * 4,
        compiler_params=LIMIT,
        cost_estimate=pl.CostEstimate(flops=10_000_000, bytes_accessed=20_000_000, transcendentals=0),
    )(offs, nu_t, sg_t, p, src, ids)


def sides_kernel(offs, nu_t, acc, own_first, own_last, top, bot, mine, send):
    strip, tm = lax.axis_index("space"), lax.axis_index("tm")
    half_strips = lax.axis_size("space") // 2
    scale = signed() / (STEPS * lax.axis_size("tm"))
    core, y = tm & 1, (tm >> 1) & 1
    flip = core * 8 + y * 4
    rows = lax.broadcasted_iota(jnp.int32, (8, COLS), 0)
    parts = []
    for own, halo, kind, own_row, halo_row in (
        (own_first, top, strip - 1, 0, 7),
        (own_last, bot, strip + 1, 7, 0),
    ):
        inner = lookup(own[8:16, :], nu_t)[own_row : own_row + 1, :]
        outer = lookup(halo[8:16, :], nu_t)[halo_row : halo_row + 1, :]
        inner = jnp.broadcast_to(inner, (8, COLS))
        outer = jnp.broadcast_to(outer, (8, COLS))
        total = jnp.zeros((8, COLS), jnp.float32)
        for k in range(STEPS):
            turn = offs[k] * SLOT_W
            a = pltpu.roll(inner, jnp.where(strip < half_strips, turn, 0), 1)
            b = pltpu.roll(outer, jnp.where(kind < half_strips, turn, 0), 1)
            gap = own[k : k + 1, :] - halo[k : k + 1, :]
            total = total + harmonic(a, b) * jnp.broadcast_to(gap, (8, COLS))
        parts.append(jnp.where(rows == own_row, scale * total, 0.0))
    for out, shift in ((mine, 0), (send, 8)):
        for i in range(8):
            b = (i + shift) ^ flip
            edge = jnp.where(b == 0, 1.0, 0.0) * parts[0]
            edge = edge + jnp.where(b == ROWS // 8 - 1, 1.0, 0.0) * parts[1]
            out[rows8(i), :] = acc[block(b), :] - edge


def sides(offs, nu_t, acc, own_first, own_last, top, bot):
    return pl.pallas_call(
        sides_kernel,
        in_specs=[SMEM] * 2 + [VMEM] * 5,
        out_specs=[VMEM] * 2,
        out_shape=[struct(ROWS // 2, COLS)] * 2,
        compiler_params=LIMIT,
    )(offs, nu_t, acc, own_first, own_last, top, bot)


def operator_kernel(nu_t, sg_t, ids, top, bot, _, sg, fr, fc, dinv, nu):
    first, last = row_masks()
    strip = lax.axis_index("space")
    blocks = EXTENDED // 8
    for e in range(blocks):
        if e == 0:
            region = top[8:16, :].astype(jnp.int32)
        elif e == blocks - 1:
            region = bot[8:16, :].astype(jnp.int32)
        else:
            region = ids[rows8(e - 1), :]
        nu[rows8(e), :] = lookup(region, nu_t)
        sg[rows8(e), :] = lookup(region, sg_t)
    up = jnp.zeros((8, COLS), jnp.float32)
    for e in range(blocks):
        cur = nu[rows8(e), :]
        face = harmonic(cur, below(cur, nu[rows8(min(e + 1, blocks - 1)), :], last))
        fr[rows8(e), :] = face
        side = harmonic(cur, pltpu.roll(cur, COLS - 1, 1))
        fc[rows8(e), :] = side
        diagonal = sg[rows8(e), :] + above(face, up, first) + face + pltpu.roll(side, 1, 1) + side
        inverse = 1.0 / diagonal
        if e == 0:
            inverse = jnp.where(strip == 0, 0.0, inverse)
        if e == blocks - 1:
            inverse = jnp.where(strip == lax.axis_size("space") - 1, 0.0, inverse)
        dinv[rows8(e), :] = inverse
        up = face


def operator(nu_t, sg_t, ids, top, bot, after):
    return pl.pallas_call(
        operator_kernel,
        in_specs=[SMEM] * 2 + [VMEM] * 3 + [ANY],
        out_specs=[VMEM] * 4,
        out_shape=[struct(EXTENDED, COLS)] * 4,
        scratch_shapes=[pltpu.VMEM((EXTENDED, COLS), jnp.float32)],
        compiler_params=LIMIT,
    )(nu_t, sg_t, ids, top, bot, after)


def swap(x, bit):
    return lax.ppermute(x, "tm", [(i, i ^ bit) for i in range(lax.axis_size("tm"))])


def add_kernel(a, b, mine, send):
    n = mine.shape[0]
    mine[...] = a[:n, :] + b[:n, :]
    send[...] = a[n:, :] + b[n:, :]


def halves(a, b):
    n = a.shape[0] // 2
    return pl.pallas_call(
        add_kernel,
        in_specs=[VMEM] * 2,
        out_specs=[VMEM] * 2,
        out_shape=[struct(n, COLS)] * 2,
        compiler_params=LIMIT,
    )(a, b)


def merge_kernel(a, b, _, out):
    for z in range(out.shape[0]):
        piece = slice(z * 128, z * 128 + 128)
        out[z] = a[:, piece] + b[:, piece]


def merge(a, b, after, count):
    return pl.pallas_call(
        merge_kernel,
        in_specs=[VMEM, VMEM, ANY],
        out_specs=VMEM,
        out_shape=struct(count, a.shape[0], COLS // count),
        compiler_params=LIMIT,
    )(a, b, after)


def total_kernel(parts, out):
    total = parts[0]
    for i in range(1, parts.shape[0]):
        total = total + parts[i]
    for i in range(parts.shape[0]):
        out[i] = total


def total_for_all(parts):
    return pl.pallas_call(
        total_kernel,
        in_specs=[VMEM],
        out_specs=VMEM,
        out_shape=struct(*parts.shape),
        compiler_params=LIMIT,
    )(parts)


def among_z(blocks):
    groups = [[z * 4 + q for z in range(blocks.shape[0])] for q in range(4)]
    return lax.all_to_all(blocks, "tm", 0, 0, axis_index_groups=groups)


def gate_kernel(*_):
    pass


def gate(value, *after):
    return pl.pallas_call(
        gate_kernel,
        in_specs=[ANY] * (1 + len(after)),
        out_specs=ANY,
        out_shape=struct(*value.shape),
        input_output_aliases={0: 0},
        compiler_params=LIMIT,
    )(value, *after)


def edge_kernel(x, out):
    tm = lax.axis_index("tm")
    start = pl.multiple_of(jnp.where((tm & 3) == 0, 0, x.shape[1] - 8), 8)
    out[...] = x[:, pl.ds(start, 8), :]


def edge_rows(x):
    return pl.pallas_call(
        edge_kernel,
        in_specs=[VMEM],
        out_specs=VMEM,
        out_shape=struct(x.shape[0], 8, 128),
        compiler_params=LIMIT,
    )(x)


def for_core_kernel(x, other, edge_a, edge_b, out):
    quarter = x.shape[1]
    out[:, :quarter, :] = x[...]
    out[:, quarter : 2 * quarter, :] = other[...]
    out[:, 2 * quarter :, :] = edge_a[...] + edge_b[...]


def for_core(x, other, edge_a, edge_b):
    return pl.pallas_call(
        for_core_kernel,
        in_specs=[VMEM] * 4,
        out_specs=VMEM,
        out_shape=struct(x.shape[0], 2 * x.shape[1] + 8, 128),
        compiler_params=LIMIT,
    )(x, other, edge_a, edge_b)


def edge_routes(moments, strips):
    routes = []
    for flip in (0, 2):
        route = []
        for z in range(moments // 4):
            for s in range(strips):
                if s > 0:
                    route.append(((z * 4) * strips + s, (z * 4 + 1 + flip) * strips + s - 1))
                if s + 1 < strips:
                    route.append(((z * 4 + 3) * strips + s, (z * 4 + flip) * strips + s + 1))
        routes.append(route)
    return routes


def chebyshev_kernel(own, partner, sg, fr, fc, dinv, c_out, sums, target, res, s0, s1, c):
    tm = lax.axis_index("tm")
    core, y = tm & 1, (tm >> 1) & 1
    flip = core * 8 + y * 4
    blocks = EXTENDED // 8
    for ref, start in ((own, 0), (partner, 8)):
        for z in range(own.shape[0]):
            piece = slice(z * 128, z * 128 + 128)
            for i in range(8):
                target[block(((start + i) ^ flip) + 1), piece] = ref[z, rows8(i), :]
            halo = ref[z, 64:72, :]
            at = jnp.where(core == start // 8, 0, blocks - 1)
            target[block(at), piece] = halo

    center = (MAXIMUM + MINIMUM) / 2.0
    half_span = (MAXIMUM - MINIMUM) / 2.0
    ratio = center / half_span
    for e in range(blocks):
        step = target[rows8(e), :] * dinv[rows8(e), :] / center
        s0[rows8(e), :] = step
        c[rows8(e), :] = step

    def sweep(field, use):
        stencil(
            lambda e: field[rows8(e), :],
            blocks,
            lambda e: fr[rows8(e), :],
            lambda e: sg[rows8(e), :],
            lambda e: fc[rows8(e), :],
            use,
        )

    old = 1.0 / ratio
    now, then = s0, s1
    for number in range(SWEEPS - 1):
        new = 1.0 / (2.0 * ratio - old)

        def use(e, cur, image):
            left = (target if number == 0 else res)[rows8(e), :] - image
            res[rows8(e), :] = left
            step = new * old * cur + (2.0 * new / half_span) * (left * dinv[rows8(e), :])
            then[rows8(e), :] = step
            c[rows8(e), :] += step

        sweep(now, use)
        now, then = then, now
        old = new

    totals = [jnp.zeros((8, COLS), jnp.float32)] * 2

    def finish(e, cur, image):
        if 0 < e < blocks - 1:
            c_out[rows8(e - 1), :] = cur
            totals[0] = totals[0] + target[rows8(e), :] * cur
            totals[1] = totals[1] + cur * image

    sweep(c, finish)
    sums[...] = jnp.zeros_like(sums)
    for i in range(2):
        sums[:, i : i + 1, :] = jnp.full((sums.shape[0], 1, 128), jnp.sum(totals[i]), jnp.float32)


def chebyshev(own, partner, sg, fr, fc, dinv, strips):
    return pl.pallas_call(
        chebyshev_kernel,
        in_specs=[VMEM] * 6,
        out_specs=[VMEM] * 2,
        out_shape=[struct(ROWS, COLS), struct(strips, 8, 128)],
        scratch_shapes=[pltpu.VMEM((EXTENDED, COLS), jnp.float32)] * 5,
        compiler_params=LIMIT,
        cost_estimate=pl.CostEstimate(flops=10_000_000, bytes_accessed=10_000_000, transcendentals=0),
    )(own, partner, sg, fr, fc, dinv)


def step_length(sums):
    every = sums[0]
    for i in range(1, sums.shape[0]):
        every = every + sums[i]
    return jnp.sum(every[0:1, 0:1]) / jnp.sum(every[1:2, 0:1])


def signed():
    tm = lax.axis_index("tm")
    return jnp.where(tm < lax.axis_size("tm") // 2, 1.0, -1.0).astype(jnp.float32)


def correct_kernel(sums, c, out):
    out[...] = step_length(sums) * c[...]


def correct(sums, c):
    return pl.pallas_call(
        correct_kernel,
        in_specs=[VMEM] * 2,
        out_specs=VMEM,
        out_shape=struct(ROWS, COLS),
        compiler_params=LIMIT,
    )(sums, c)


def first_kernel(p, opposite, correction, out):
    out[...] = p[...] - 0.5 * (p[...] + opposite[...]) + signed() * correction[...][None]


def next_kernel(_, p, opposite, correction, out):
    first_kernel(p, opposite, correction, out)


def update(done, p, opposite, correction, start):
    tile = (STEPS, TILE, COLS)
    at = start // TILE
    specs = [
        pl.BlockSpec(tile, lambda i: (0, at + i, 0)),
        pl.BlockSpec(tile, lambda i: (0, i, 0)),
        pl.BlockSpec((TILE, COLS), lambda i: (at + i, 0)),
    ]
    operands = (p, opposite, correction)
    return pl.pallas_call(
        first_kernel if done is None else next_kernel,
        grid=(opposite.shape[1] // TILE,),
        in_specs=specs if done is None else [ANY] + specs,
        out_specs=pl.BlockSpec(tile, lambda i: (0, at + i, 0)),
        out_shape=struct(STEPS, ROWS, COLS),
        input_output_aliases={} if done is None else {0: 0},
        compiler_params=LIMIT,
    )(*(operands if done is None else (done,) + operands))


def per_device(p, source, offsets, ids, nu_t, sg_t):
    moments = lax.axis_size("tm")
    strips = lax.axis_size("space")
    across = [(i, (i + moments // 2) % moments) for i in range(moments)]
    to_next = [(i, i + 1) for i in range(strips - 1)]
    to_prev = [(j, i) for i, j in to_next]
    starts = [sum(CHUNKS[:i]) for i in range(len(CHUNKS))]

    def exchange(i, *after):
        rows = lax.slice_in_dim(p, starts[i], starts[i] + CHUNKS[i], axis=1)
        return lax.ppermute(gate(rows, *after) if after else rows, "tm", across)

    opposite = [exchange(0)]
    down, up = edges(p, ids)
    top = lax.ppermute(up, "space", to_next)
    bot = lax.ppermute(down, "space", to_prev)
    acc = residual(offsets, nu_t, sg_t, p, source, ids)
    mine, send = sides(offsets, nu_t, acc, down, up, top, bot)

    mine, send = halves(mine, swap(send, 1))
    pieces = merge(mine, swap(send, 2), opposite[0], moments // 4)
    opposite.append(exchange(1, pieces))
    total = total_for_all(among_z(pieces))
    opposite.append(exchange(2, total))
    x = among_z(total)
    for i in range(3, len(CHUNKS)):
        opposite.append(exchange(i, x, *opposite[1:3]))
    sg, fr, fc, dinv = operator(nu_t, sg_t, ids, top, bot, x)

    edge = edge_rows(x)
    edge_a, edge_b = (lax.ppermute(edge, ("tm", "space"), r) for r in edge_routes(moments, strips))
    own = for_core(x, swap(x, 2), edge_a, edge_b)
    c, sums = chebyshev(own, swap(own, 1), sg, fr, fc, dinv, strips)
    sums = lax.all_to_all(sums, "space", 0, 0)
    correction = correct(sums, c)
    updated = None
    for start, part in zip(starts, opposite):
        updated = update(updated, p, part, correction, start)
    return updated, correction


def solution(mesh):
    placed = (P("tm", "space", None), P("tm", "space", None), P("tm"), P("space", None), P(), P())
    return jax.shard_map(
        per_device,
        mesh=mesh,
        in_specs=placed,
        out_specs=(P("tm", "space", None), P("space", None)),
        check_vma=False,
    )
```

time: 149 us -> 126 us (0.85)
  starting transfers between devices: 29.1 us -> 52.7 us
  Pallas kernels: 42.6 us -> 25.7 us
  blocking collectives: 25.8 us -> 11.5 us
  local copies, waits for them, and re-layouts: 16.1 us -> 4.36 us
  waiting for transfers between devices: 31.9 us -> 29.8 us
  other arithmetic: 1.52 us -> 0 us
    all_to_all x1 -> x2, starting transfers between devices: 3.37 us -> 19.3 us  [among_z(): return lax.all_to_all(blocks, 'tm', 0, 0, axis_index_groups=groups)]
    all_to_all x2 -> x1, blocking collectives: 25.8 us -> 11.5 us  [per_device(): sums = lax.all_to_all(sums, 'space', 0, 0)]
    unnamed x44 -> x20, local copies, waits for them, and re-layouts: 12.8 us -> 1.92 us
    all_to_all x1 -> x2, waiting for transfers between devices: 7.76 us -> 15.6 us  [among_z(): return lax.all_to_all(blocks, 'tm', 0, 0, axis_index_groups=groups)]
    pallas_call x1, Pallas kernels: 12.8 us -> 5.04 us  [chebyshev(): pl.pallas_call(chebyshev_kernel, in_specs=[VMEM] * 6, out_specs=[VMEM] *...]
    ppermute x4, waiting for transfers between devices: 12.8 us -> 5.49 us  [swap(): lax.ppermute(x, 'tm', [(i, i ^ bit) for i in range(lax.axis_size('tm'))])]
    ppermute x4 -> x7, starting transfers between devices: 16.1 us -> 22.6 us  [the longest x5 19.4 us: exchange(): return lax.ppermute(gate(rows, *after) if after else rows, 'tm', across)]
    pallas_call x3 -> x9, Pallas kernels: 15.6 us -> 10.1 us  [the longest x1 7.48 us: residual(): pl.pallas_call(residual_kernel, in_specs=[SMEM] * 3 + [VMEM] * 3, out_spe...]
  transfers between devices with their start and end apart: 11 -> 15, of which waited for: 10 -> 6; matrix products, arithmetic and copies ran while one was open for 2% -> 1% of each run, Pallas kernels for 24% -> 19%
where the time goes in v2:
time: 126 us; the launch traced here: 125 us
  starting transfers between devices  52.7 us (42%)
  waiting for transfers between devices  29.8 us (24%)
  Pallas kernels  25.7 us (20%)
  blocking collectives  11.5 us (9%)
  local copies, waits for them, and re-layouts  4.36 us (3%)
    ppermute x5, starting transfers between devices, exchange(): return lax.ppermute(gate(rows, *after) if after else rows, 'tm', across)  19.4 us
    all_to_all x2, starting transfers between devices, among_z(): return lax.all_to_all(blocks, 'tm', 0, 0, axis_index_groups=groups)  19.3 us
    all_to_all x2, waiting for transfers between devices, among_z(): return lax.all_to_all(blocks, 'tm', 0, 0, axis_index_groups=groups)  15.6 us
    all_to_all x1, blocking collectives, per_device(): sums = lax.all_to_all(sums, 'space', 0, 0)  11.5 us
    pallas_call x5, Pallas kernels, update(): pl.pallas_call(first_kernel if done is None else next_kernel, grid=(oppos...  8.34 us
    pallas_call x1, Pallas kernels, residual(): pl.pallas_call(residual_kernel, in_specs=[SMEM] * 3 + [VMEM] * 3, out_spe...  7.48 us
    ppermute x4, waiting for transfers between devices, swap(): lax.ppermute(x, 'tm', [(i, i ^ bit) for i in range(lax.axis_size('tm'))])  5.49 us
    ppermute x2, waiting for transfers between devices, per_device(): lax.ppermute(edge, ('tm', 'space'), r)  5.41 us
  transfers between devices with their start and end apart: 15, of which 6 were waited for; matrix products, arithmetic and copies ran while one was open for 1% of the time, Pallas kernels for 19%

profile of v2, /device:TPU:2, one launch (start us, length us, event | category | flops | bytes accessed | tf_op | source)
XLA Modules:
  0.0 125.0 jit_solution(4156492693459248843)
XLA Ops:
  0.6 1.5 %fusion.1 = (f32[4,40,1024]{2,1,0:T(8,128)S(1)}, f32[4,40,1024]{2,1,0:T(8,128)S(1)}) fusion(f32[4,128,1024]{2,1,0:T(8,128)} %p.11), kind=kLoop, calls=%fused_computation.1 | loop fusion | bytes 2621440 | tf_op jit(solution)/shard_map/slice | solution.py:501
  2.2 7.3 %collective-permute-start = (f32[4,40,1024]{2,1,0:T(8,128)S(1)}, f32[4,40,1024]{2,1,0:T(8,128)S(1)}, u32[]{:S(2)}, u32[]{:S(2)}) collective-permute-start(f32[4,40,1024]{2,1,0:T(8,128)S(1)} %get-tuple-element.30), channel_id=1, source_target_pairs={{0,128},{8,136},{16,144},{24,152},{32,160},{40,168},{48,176},{56,1... | collective-permute-start | bytes 1966088 | tf_op jit(solution)/shard_map/ppermute | solution.py:502
  9.6 5.1 %collective-permute-start.2 = (f32[16,1024]{1,0:T(8,128)S(1)}, f32[16,1024]{1,0:T(8,128)S(1)}, u32[]{:S(2)}, u32[]{:S(2)}) collective-permute-start(f32[16,1024]{1,0:T(8,128)S(1)} %get-tuple-element.14.own_first), channel_id=1, source_target_pairs={{1,0},{2,1},{3,2},{4,3},{5,4},{6,5},{7,6},{9,8},{10,9},{11,10},{12... | collective-permute-start | bytes 196616 | tf_op jit(solution)/shard_map/ppermute | solution.py:507
  14.6 2.3 %collective-permute-start.1 = (f32[16,1024]{1,0:T(8,128)S(1)}, f32[16,1024]{1,0:T(8,128)S(1)}, u32[]{:S(2)}, u32[]{:S(2)}) collective-permute-start(f32[16,1024]{1,0:T(8,128)S(1)} %get-tuple-element.15.own_last), channel_id=1, source_target_pairs={{0,1},{1,2},{2,3},{3,4},{4,5},{5,6},{6,7},{8,9},{9,10},{10,11},{11... | collective-permute-start | bytes 196616 | tf_op jit(solution)/shard_map/ppermute | solution.py:506
  17.0 7.5 %shard_map.77.acc = f32[128,1024]{1,0:T(8,128)S(1)} custom-call(s32[4]{0:T(128)S(1)} %copy-done.8, f32[8]{0:T(128)S(1)} %copy-done.7, f32[8]{0:T(128)S(1)} %copy-done.9, f32[4,128,1024]{2,1,0:T(8,128)S(1)} %copy-done, f32[4,128,1024]{2,1,0:T(8,128)S(1)} %copy-done.5, s32[128,1024]{1,0:T(8,128)S(1)} %copy-done.2), custom_call_target="tpu_custom_call" | custom-call | flops 10000000 | bytes 20000000 | tf_op jit(solution)/shard_map/pallas_call | solution.py:148
  24.5 0.9 shard_map.79
  25.5 1.5 %collective-permute-done.3.b = f32[64,1024]{1,0:T(8,128)S(1)} collective-permute-done((f32[64,1024]{1,0:T(8,128)S(1)}, f32[64,1024]{1,0:T(8,128)S(1)}, u32[]{:S(2)}, u32[]{:S(2)}) %collective-permute-start.3) | collective-permute-done | bytes 262176 | tf_op jit(solution)/shard_map/ppermute | solution.py:243
  27.0 1.7 %collective-permute-start.4 = (f32[32,1024]{1,0:T(8,128)S(1)}, f32[32,1024]{1,0:T(8,128)S(1)}, u32[]{:S(2)}, u32[]{:S(2)}) collective-permute-start(f32[32,1024]{1,0:T(8,128)S(1)} %get-tuple-element.19), channel_id=1, source_target_pairs={{0,16},{8,24},{16,0},{24,8},{32,48},{40,56},{48,32},{56,40},{64,80... | collective-permute-start | bytes 393224 | tf_op jit(solution)/shard_map/ppermute | solution.py:243
  28.7 4.0 %collective-permute-done.4.b = f32[32,1024]{1,0:T(8,128)S(1)} collective-permute-done((f32[32,1024]{1,0:T(8,128)S(1)}, f32[32,1024]{1,0:T(8,128)S(1)}, u32[]{:S(2)}, u32[]{:S(2)}) %collective-permute-start.4) | collective-permute-done | bytes 131104 | tf_op jit(solution)/shard_map/ppermute | solution.py:243
  33.3 0.8 copy-done.3
  34.2 12.1 %all-to-all-start = ((f32[8,32,128]{2,1,0:T(8,128)}), f32[8,32,128]{2,1,0:T(8,128)S(1)}, u32[]{:S(2)}, u32[]{:S(2)}) async-start(f32[8,32,128]{2,1,0:T(8,128)} %shard_map.81.__1_), calls=%async_computation | async-start | bytes 262144 | tf_op jit(solution)/shard_map/all_to_all | solution.py:299
  46.3 0.9 fusion
  47.2 5.9 %collective-permute-start.9 = (f32[4,16,1024]{2,1,0:T(8,128)}, f32[4,16,1024]{2,1,0:T(8,128)}, u32[]{:S(2)}, u32[]{:S(2)}) collective-permute-start(f32[4,16,1024]{2,1,0:T(8,128)} %shard_map.89), channel_id=1, source_target_pairs={{0,128},{8,136},{16,144},{24,152},{32,160},{40,168},{48,176},{56,1... | collective-permute-start | bytes 786440 | tf_op jit(solution)/shard_map/ppermute | solution.py:502
  53.1 5.1 %all-to-all-done.parts = f32[8,32,128]{2,1,0:T(8,128)S(1)} async-done(((f32[8,32,128]{2,1,0:T(8,128)}), f32[8,32,128]{2,1,0:T(8,128)S(1)}, u32[]{:S(2)}, u32[]{:S(2)}) %all-to-all-start) | async-done | bytes 131104 | tf_op jit(solution)/shard_map/all_to_all | solution.py:299
  58.9 7.2 %all-to-all-start.1 = ((f32[8,32,128]{2,1,0:T(8,128)}), f32[8,32,128]{2,1,0:T(8,128)S(1)}, u32[]{:S(2)}, u32[]{:S(2)}) async-start(f32[8,32,128]{2,1,0:T(8,128)} %shard_map.82.__1_), calls=%async_computation.1 | async-start | bytes 262144 | tf_op jit(solution)/shard_map/all_to_all | solution.py:299
  66.1 3.3 %collective-permute-done.9.opposite.__2_ = f32[4,16,1024]{2,1,0:T(8,128)} collective-permute-done((f32[4,16,1024]{2,1,0:T(8,128)}, f32[4,16,1024]{2,1,0:T(8,128)}, u32[]{:S(2)}, u32[]{:S(2)}) %collective-permute-start.9) | collective-permute-done | bytes 262176 | tf_op jit(solution)/shard_map/ppermute | solution.py:502
  69.4 10.5 %all-to-all-done.1.x._.__1_ = f32[8,32,128]{2,1,0:T(8,128)S(1)} async-done(((f32[8,32,128]{2,1,0:T(8,128)}), f32[8,32,128]{2,1,0:T(8,128)S(1)}, u32[]{:S(2)}, u32[]{:S(2)}) %all-to-all-start.1) | async-done | bytes 131104 | tf_op jit(solution)/shard_map/all_to_all | solution.py:299
  79.9 3.7 %collective-permute-start.11 = (f32[4,40,1024]{2,1,0:T(8,128)S(1)}, f32[4,40,1024]{2,1,0:T(8,128)S(1)}, u32[]{:S(2)}, u32[]{:S(2)}) collective-permute-start(f32[4,40,1024]{2,1,0:T(8,128)S(1)} %shard_map.93), channel_id=1, source_target_pairs={{0,128},{8,136},{16,144},{24,152},{32,160},{40,168},{48,176},{56,1... | collective-permute-start | bytes 1966088 | tf_op jit(solution)/shard_map/ppermute | solution.py:502
  83.6 1.6 %collective-permute-start.5 = (f32[8,32,128]{2,1,0:T(8,128)S(1)}, f32[8,32,128]{2,1,0:T(8,128)S(1)}, u32[]{:S(2)}, u32[]{:S(2)}) collective-permute-start(f32[8,32,128]{2,1,0:T(8,128)S(1)} %all-to-all-done.1.x._.__1_), channel_id=1, source_target_pairs={{0,16},{8,24},{16,0},{24,8},{32,48},{40,56},{48,32},{56,40},{64,80... | collective-permute-start | bytes 393224 | tf_op jit(solution)/shard_map/ppermute | solution.py:243
  85.2 1.3 %collective-permute-start.7 = (f32[8,8,128]{2,1,0:T(8,128)S(1)}, f32[8,8,128]{2,1,0:T(8,128)S(1)}, u32[]{:S(2)}, u32[]{:S(2)}) collective-permute-start(f32[8,8,128]{2,1,0:T(8,128)S(1)} %shard_map.83), channel_id=1, source_target_pairs={{24,17},{1,24},{25,18},{2,25},{26,19},{3,26},{27,20},{4,27},{28,21... | collective-permute-start | bytes 98312 | tf_op jit(solution)/shard_map/ppermute | solution.py:522
  86.4 1.9 %collective-permute-start.6 = (f32[8,8,128]{2,1,0:T(8,128)S(1)}, f32[8,8,128]{2,1,0:T(8,128)S(1)}, u32[]{:S(2)}, u32[]{:S(2)}) collective-permute-start(f32[8,8,128]{2,1,0:T(8,128)S(1)} %shard_map.83), channel_id=1, source_target_pairs={{24,1},{1,8},{25,2},{2,9},{26,3},{3,10},{27,4},{4,11},{28,5},{5,12... | collective-permute-start | bytes 98312 | tf_op jit(solution)/shard_map/ppermute | solution.py:522
  88.4 5.4 %collective-permute-done.6.edge_a = f32[8,8,128]{2,1,0:T(8,128)S(1)} collective-permute-done((f32[8,8,128]{2,1,0:T(8,128)S(1)}, f32[8,8,128]{2,1,0:T(8,128)S(1)}, u32[]{:S(2)}, u32[]{:S(2)}) %collective-permute-start.6) | collective-permute-done | bytes 32800 | tf_op jit(solution)/shard_map/ppermute | solution.py:522
  93.9 2.5 %collective-permute-start.12 = (f32[4,16,1024]{2,1,0:T(8,128)S(1)}, f32[4,16,1024]{2,1,0:T(8,128)S(1)}, u32[]{:S(2)}, u32[]{:S(2)}) collective-permute-start(f32[4,16,1024]{2,1,0:T(8,128)S(1)} %shard_map.95), channel_id=1, source_target_pairs={{0,128},{8,136},{16,144},{24,152},{32,160},{40,168},{48,176},{56,1... | collective-permute-start | bytes 786440 | tf_op jit(solution)/shard_map/ppermute | solution.py:502
  96.4 1.7 %shard_map.85 = (f32[144,1024]{1,0:T(8,128)S(1)}, f32[144,1024]{1,0:T(8,128)S(1)}, f32[144,1024]{1,0:T(8,128)S(1)}, f32[144,1024]{1,0:T(8,128)S(1)}) custom-call(f32[8]{0:T(128)S(1)} %copy-done.7, f32[8]{0:T(128)S(1)} %copy-done.9, s32[128,1024]{1,0:T(8,128)S(1)} %copy-done.2, f32[16,1024]{1,0:T(8,128)S(1)} %collective-permute-done.1.top, ...), custom_call_target="tpu_custom_call" | custom-call | tf_op jit(solution)/shard_map/pallas_call | solution.py:232
  98.1 5.0 %shard_map.86 = (f32[128,1024]{1,0:T(8,128)S(1)}, f32[8,8,128]{2,1,0:T(8,128)S(1)}) custom-call(f32[8,72,128]{2,1,0:T(8,128)S(1)} %shard_map.84.own, f32[8,72,128]{2,1,0:T(8,128)S(1)} %collective-permute-done.8.partner, f32[144,1024]{1,0:T(8,128)S(1)} %get-tuple-element.20.sg, f32[144,1024]{1,0:T(8,128)S(1)} %get-tuple-element.21.fr, ...), custom_call_target="tpu_custom_call" | custom-call | flops 10000000 | bytes 10000000 | tf_op jit(solution)/shard_map/pallas_call | solution.py:427
  103.2 11.5 %all_to_all.15.sums = f32[8,8,128]{2,1,0:T(8,128)S(1)} all-to-all(f32[8,8,128]{2,1,0:T(8,128)S(1)} %get-tuple-element.24), channel_id=1, replica_groups=mesh['tm'=32,'space'=8] {'space'}, dimensions={0} | all-to-all | bytes 65536 | tf_op jit(solution)/shard_map/all_to_all | solution.py:525
  114.7 0.9 shard_map.87.correction
  115.6 1.0 copy-done.1
  116.6 2.1 %shard_map.88._ = f32[4,128,1024]{2,1,0:T(8,128)} custom-call(f32[4,128,1024]{2,1,0:T(8,128)S(1)} %copy-done, f32[4,40,1024]{2,1,0:T(8,128)S(1)} %copy-done.4, f32[128,1024]{1,0:T(8,128)S(1)} %copy-done.1), custom_call_target="tpu_custom_call" | custom-call | tf_op jit(solution)/shard_map/pallas_call | solution.py:481
  118.7 1.7 %shard_map.90._ = f32[4,128,1024]{2,1,0:T(8,128)} custom-call(f32[4,128,1024]{2,1,0:T(8,128)} %shard_map.88._, f32[4,128,1024]{2,1,0:T(8,128)S(1)} %copy-done, f32[4,16,1024]{2,1,0:T(8,128)} %collective-permute-done.9.opposite.__2_, f32[128,1024]{1,0:T(8,128)S(1)} %copy-done.1), custom_call_target="tpu_custom_call", output_to_operand_aliasing={{}: (0, {})} | custom-call | tf_op jit(solution)/shard_map/pallas_call | solution.py:481
  120.4 1.7 %shard_map.92._ = f32[4,128,1024]{2,1,0:T(8,128)} custom-call(f32[4,128,1024]{2,1,0:T(8,128)} %shard_map.90._, f32[4,128,1024]{2,1,0:T(8,128)S(1)} %copy-done, f32[4,16,1024]{2,1,0:T(8,128)} %collective-permute-done.10.opposite.__3_, f32[128,1024]{1,0:T(8,128)S(1)} %copy-done.1), custom_call_target="tpu_custom_call", output_to_operand_aliasing={{}: (0, {})} | custom-call | tf_op jit(solution)/shard_map/pallas_call | solution.py:481
  122.1 2.1 %shard_map.94._ = f32[4,128,1024]{2,1,0:T(8,128)} custom-call(f32[4,128,1024]{2,1,0:T(8,128)} %shard_map.92._, f32[4,128,1024]{2,1,0:T(8,128)S(1)} %copy-done, f32[4,40,1024]{2,1,0:T(8,128)S(1)} %collective-permute-done.11.opposite, f32[128,1024]{1,0:T(8,128)S(1)} %copy-done.1), custom_call_target="tpu_custom_call", output_to_operand_aliasing={{}: (0, {})} | custom-call | tf_op jit(solution)/shard_map/pallas_call | solution.py:481
  (41 shorter events, 2.5 us)
Async XLA Ops:
  0.6 8.9 %copy-start = (f32[4,128,1024]{2,1,0:T(8,128)S(1)}, f32[4,128,1024]{2,1,0:T(8,128)}, u32[]{:S(2)}) copy-start(f32[4,128,1024]{2,1,0:T(8,128)} %p.11) | copy-start | bytes 6291460
  0.6 8.9 %copy-start.2 = (s32[128,1024]{1,0:T(8,128)S(1)}, s32[128,1024]{1,0:T(8,128)}, u32[]{:S(2)}) copy-start(s32[128,1024]{1,0:T(8,128)} %ids.3) | copy-start | bytes 1572868
  2.2 14.7 %copy-start.5 = (f32[4,128,1024]{2,1,0:T(8,128)S(1)}, f32[4,128,1024]{2,1,0:T(8,128)}, u32[]{:S(2)}) copy-start(f32[4,128,1024]{2,1,0:T(8,128)} %src.1) | copy-start | bytes 6291460
  2.2 14.7 %copy-start.7 = (f32[8]{0:T(128)S(1)}, f32[8]{0:T(128)}, u32[]{:S(2)}) copy-start(f32[8]{0:T(128)} %nu_t.5) | copy-start | bytes 100
  2.2 14.7 %copy-start.8 = (s32[4]{0:T(128)S(1)}, s32[4]{0:T(128)}, u32[]{:S(2)}) copy-start(s32[4]{0:T(128)} %offs.3) | copy-start | bytes 52
  2.2 14.7 %copy-start.9 = (f32[8]{0:T(128)S(1)}, f32[8]{0:T(128)}, u32[]{:S(2)}) copy-start(f32[8]{0:T(128)} %sg_t.3) | copy-start | bytes 100
  2.2 30.4 %collective-permute-start = (f32[4,40,1024]{2,1,0:T(8,128)S(1)}, f32[4,40,1024]{2,1,0:T(8,128)S(1)}, u32[]{:S(2)}, u32[]{:S(2)}) collective-permute-start(f32[4,40,1024]{2,1,0:T(8,128)S(1)} %get-tuple-element.30), channel_id=1, source_target_pairs={{0,128},{8,136},{16,144},{24,152},{32,160},{40,168},{48,176},{56,1... | collective-permute-start | bytes 1966088 | tf_op jit(solution)/shard_map/ppermute | solution.py:502
  9.6 14.9 %collective-permute-start.2 = (f32[16,1024]{1,0:T(8,128)S(1)}, f32[16,1024]{1,0:T(8,128)S(1)}, u32[]{:S(2)}, u32[]{:S(2)}) collective-permute-start(f32[16,1024]{1,0:T(8,128)S(1)} %get-tuple-element.14.own_first), channel_id=1, source_target_pairs={{1,0},{2,1},{3,2},{4,3},{5,4},{6,5},{7,6},{9,8},{10,9},{11,10},{12... | collective-permute-start | bytes 196616 | tf_op jit(solution)/shard_map/ppermute | solution.py:507
  14.6 9.8 %collective-permute-start.1 = (f32[16,1024]{1,0:T(8,128)S(1)}, f32[16,1024]{1,0:T(8,128)S(1)}, u32[]{:S(2)}, u32[]{:S(2)}) collective-permute-start(f32[16,1024]{1,0:T(8,128)S(1)} %get-tuple-element.15.own_last), channel_id=1, source_target_pairs={{0,1},{1,2},{2,3},{3,4},{4,5},{5,6},{6,7},{8,9},{9,10},{10,11},{11... | collective-permute-start | bytes 196616 | tf_op jit(solution)/shard_map/ppermute | solution.py:506
  25.4 1.6 %collective-permute-start.3 = (f32[64,1024]{1,0:T(8,128)S(1)}, f32[64,1024]{1,0:T(8,128)S(1)}, u32[]{:S(2)}, u32[]{:S(2)}) collective-permute-start(f32[64,1024]{1,0:T(8,128)S(1)} %get-tuple-element.17), channel_id=1, source_target_pairs={{0,8},{8,0},{16,24},{24,16},{32,40},{40,32},{48,56},{56,48},{64,72... | collective-permute-start | bytes 786440 | tf_op jit(solution)/shard_map/ppermute | solution.py:243
  27.0 5.6 %collective-permute-start.4 = (f32[32,1024]{1,0:T(8,128)S(1)}, f32[32,1024]{1,0:T(8,128)S(1)}, u32[]{:S(2)}, u32[]{:S(2)}) collective-permute-start(f32[32,1024]{1,0:T(8,128)S(1)} %get-tuple-element.19), channel_id=1, source_target_pairs={{0,16},{8,24},{16,0},{24,8},{32,48},{40,56},{48,32},{56,40},{64,80... | collective-permute-start | bytes 393224 | tf_op jit(solution)/shard_map/ppermute | solution.py:243
  33.3 0.8 copy-start.3
  34.2 24.0 %all-to-all-start = ((f32[8,32,128]{2,1,0:T(8,128)}), f32[8,32,128]{2,1,0:T(8,128)S(1)}, u32[]{:S(2)}, u32[]{:S(2)}) async-start(f32[8,32,128]{2,1,0:T(8,128)} %shard_map.81.__1_), calls=%async_computation | async-start | bytes 262144 | tf_op jit(solution)/shard_map/all_to_all | solution.py:299
  47.2 22.2 %collective-permute-start.9 = (f32[4,16,1024]{2,1,0:T(8,128)}, f32[4,16,1024]{2,1,0:T(8,128)}, u32[]{:S(2)}, u32[]{:S(2)}) collective-permute-start(f32[4,16,1024]{2,1,0:T(8,128)} %shard_map.89), channel_id=1, source_target_pairs={{0,128},{8,136},{16,144},{24,152},{32,160},{40,168},{48,176},{56,1... | collective-permute-start | bytes 786440 | tf_op jit(solution)/shard_map/ppermute | solution.py:502
  58.9 21.0 %collective-permute-start.10 = (f32[4,16,1024]{2,1,0:T(8,128)}, f32[4,16,1024]{2,1,0:T(8,128)}, u32[]{:S(2)}, u32[]{:S(2)}) collective-permute-start(f32[4,16,1024]{2,1,0:T(8,128)} %shard_map.91), channel_id=1, source_target_pairs={{0,128},{8,136},{16,144},{24,152},{32,160},{40,168},{48,176},{56,1... | collective-permute-start | bytes 786440 | tf_op jit(solution)/shard_map/ppermute | solution.py:502
  58.9 21.0 %all-to-all-start.1 = ((f32[8,32,128]{2,1,0:T(8,128)}), f32[8,32,128]{2,1,0:T(8,128)S(1)}, u32[]{:S(2)}, u32[]{:S(2)}) async-start(f32[8,32,128]{2,1,0:T(8,128)} %shard_map.82.__1_), calls=%async_computation.1 | async-start | bytes 262144 | tf_op jit(solution)/shard_map/all_to_all | solution.py:299
  79.9 14.1 %copy-start.6 = (f32[4,16,1024]{2,1,0:T(8,128)S(1)}, f32[4,16,1024]{2,1,0:T(8,128)}, u32[]{:S(2)}) copy-start(f32[4,16,1024]{2,1,0:T(8,128)} %get-tuple-element.26.__0_) | copy-start | bytes 786436
  79.9 42.2 %collective-permute-start.11 = (f32[4,40,1024]{2,1,0:T(8,128)S(1)}, f32[4,40,1024]{2,1,0:T(8,128)S(1)}, u32[]{:S(2)}, u32[]{:S(2)}) collective-permute-start(f32[4,40,1024]{2,1,0:T(8,128)S(1)} %shard_map.93), channel_id=1, source_target_pairs={{0,128},{8,136},{16,144},{24,152},{32,160},{40,168},{48,176},{56,1... | collective-permute-start | bytes 1966088 | tf_op jit(solution)/shard_map/ppermute | solution.py:502
  83.6 10.2 %collective-permute-start.5 = (f32[8,32,128]{2,1,0:T(8,128)S(1)}, f32[8,32,128]{2,1,0:T(8,128)S(1)}, u32[]{:S(2)}, u32[]{:S(2)}) collective-permute-start(f32[8,32,128]{2,1,0:T(8,128)S(1)} %all-to-all-done.1.x._.__1_), channel_id=1, source_target_pairs={{0,16},{8,24},{16,0},{24,8},{32,48},{40,56},{48,32},{56,40},{64,80... | collective-permute-start | bytes 393224 | tf_op jit(solution)/shard_map/ppermute | solution.py:243
  85.2 3.2 %collective-permute-start.7 = (f32[8,8,128]{2,1,0:T(8,128)S(1)}, f32[8,8,128]{2,1,0:T(8,128)S(1)}, u32[]{:S(2)}, u32[]{:S(2)}) collective-permute-start(f32[8,8,128]{2,1,0:T(8,128)S(1)} %shard_map.83), channel_id=1, source_target_pairs={{24,17},{1,24},{25,18},{2,25},{26,19},{3,26},{27,20},{4,27},{28,21... | collective-permute-start | bytes 98312 | tf_op jit(solution)/shard_map/ppermute | solution.py:522
  86.4 7.3 %collective-permute-start.6 = (f32[8,8,128]{2,1,0:T(8,128)S(1)}, f32[8,8,128]{2,1,0:T(8,128)S(1)}, u32[]{:S(2)}, u32[]{:S(2)}) collective-permute-start(f32[8,8,128]{2,1,0:T(8,128)S(1)} %shard_map.83), channel_id=1, source_target_pairs={{24,1},{1,8},{25,2},{2,9},{26,3},{3,10},{27,4},{4,11},{28,5},{5,12... | collective-permute-start | bytes 98312 | tf_op jit(solution)/shard_map/ppermute | solution.py:522
  93.8 4.3 %collective-permute-start.8 = (f32[8,72,128]{2,1,0:T(8,128)S(1)}, f32[8,72,128]{2,1,0:T(8,128)S(1)}, u32[]{:S(2)}, u32[]{:S(2)}) collective-permute-start(f32[8,72,128]{2,1,0:T(8,128)S(1)} %shard_map.84.own), channel_id=1, source_target_pairs={{0,8},{8,0},{16,24},{24,16},{32,40},{40,32},{48,56},{56,48},{64,72... | collective-permute-start | bytes 884744 | tf_op jit(solution)/shard_map/ppermute | solution.py:243
  93.9 30.2 %collective-permute-start.12 = (f32[4,16,1024]{2,1,0:T(8,128)S(1)}, f32[4,16,1024]{2,1,0:T(8,128)S(1)}, u32[]{:S(2)}, u32[]{:S(2)}) collective-permute-start(f32[4,16,1024]{2,1,0:T(8,128)S(1)} %shard_map.95), channel_id=1, source_target_pairs={{0,128},{8,136},{16,144},{24,152},{32,160},{40,168},{48,176},{56,1... | collective-permute-start | bytes 786440 | tf_op jit(solution)/shard_map/ppermute | solution.py:502
  98.1 17.5 %copy-start.4 = (f32[4,40,1024]{2,1,0:T(8,128)S(1)}, f32[4,40,1024]{2,1,0:T(8,128)}, u32[]{:S(2)}) copy-start(f32[4,40,1024]{2,1,0:T(8,128)} %copy-done.3) | copy-start | bytes 1966084
  115.6 1.0 copy-start.1

commit v3 on v2

--- a/solution.py
+++ b/solution.py
@@ -16,8 +16,7 @@
 COLS = 1024
 STEPS = 4
 EXTENDED = ROWS + 16
-CHUNKS = (40, 16, 16, 40, 16)
-TILE = 8
+CHUNKS = (40, 16, 56, 16)
 
 ANY = pl.BlockSpec(memory_space=pl.ANY)
 VMEM = pl.BlockSpec(memory_space=pltpu.VMEM)
@@ -299,6 +298,21 @@
     return lax.all_to_all(blocks, "tm", 0, 0, axis_index_groups=groups)
 
 
+def fetch_kernel(start, p, *refs):
+    out = refs[-1]
+    out[...] = p[:, start : start + out.shape[1], :]
+
+
+def fetch(p, start, rows, *after):
+    return pl.pallas_call(
+        functools.partial(fetch_kernel, start),
+        in_specs=[VMEM] + [ANY] * len(after),
+        out_specs=VMEM,
+        out_shape=struct(STEPS, rows, COLS),
+        compiler_params=LIMIT,
+    )(p, *after)
+
+
 def gate_kernel(*_):
     pass
 
@@ -447,46 +461,54 @@
     return jnp.where(tm < lax.axis_size("tm") // 2, 1.0, -1.0).astype(jnp.float32)
 
 
-def correct_kernel(sums, c, out):
-    out[...] = step_length(sums) * c[...]
-
-
-def correct(sums, c):
-    return pl.pallas_call(
-        correct_kernel,
-        in_specs=[VMEM] * 2,
-        out_specs=VMEM,
-        out_shape=struct(ROWS, COLS),
-        compiler_params=LIMIT,
-    )(sums, c)
-
-
-def first_kernel(p, opposite, correction, out):
-    out[...] = p[...] - 0.5 * (p[...] + opposite[...]) + signed() * correction[...][None]
-
-
-def next_kernel(_, p, opposite, correction, out):
-    first_kernel(p, opposite, correction, out)
-
-
-def update(done, p, opposite, correction, start):
-    tile = (STEPS, TILE, COLS)
-    at = start // TILE
-    specs = [
-        pl.BlockSpec(tile, lambda i: (0, at + i, 0)),
-        pl.BlockSpec(tile, lambda i: (0, i, 0)),
-        pl.BlockSpec((TILE, COLS), lambda i: (at + i, 0)),
-    ]
-    operands = (p, opposite, correction)
-    return pl.pallas_call(
-        first_kernel if done is None else next_kernel,
-        grid=(opposite.shape[1] // TILE,),
-        in_specs=specs if done is None else [ANY] + specs,
-        out_specs=pl.BlockSpec(tile, lambda i: (0, at + i, 0)),
-        out_shape=struct(STEPS, ROWS, COLS),
-        input_output_aliases={} if done is None else {0: 0},
-        compiler_params=LIMIT,
-    )(*(operands if done is None else (done,) + operands))
+def update_kernel(starts, fresh, *refs):
+    refs = refs if fresh else refs[1:]
+    sums, c, p = refs[:3]
+    opposite, refs = refs[3 : 3 + len(starts)], refs[3 + len(starts) :]
+    if fresh:
+        out, correction, buffer, kept, out_sem, kept_sem = refs
+    else:
+        out, buffer, out_sem = refs
+    omega, sign = step_length(sums), signed()
+    copies = []
+    for i, (start, part) in enumerate(zip(starts, opposite)):
+        for r in range(0, part.shape[1], 8):
+            here = slice(start + r, start + r + 8)
+            corrected = omega * c[here, :]
+            for k in range(STEPS):
+                field = p[k, here, :]
+                moved = field - 0.5 * (field + part[k, r : r + 8, :])
+                buffer[k, here, :] = moved + sign * corrected
+        rows = pl.ds(start, part.shape[1])
+        copies.append(pltpu.make_async_copy(buffer.at[:, rows], out.at[:, rows], out_sem.at[i]))
+        copies[-1].start()
+    if fresh:
+        kept[...] = omega * c[...]
+        copies.append(pltpu.make_async_copy(kept, correction, kept_sem))
+        copies[-1].start()
+    for copy in copies:
+        copy.wait()
+
+
+def update(done, sums, c, p, opposite, starts):
+    fresh = done is None
+    shape, strip = (STEPS, ROWS, COLS), (ROWS, COLS)
+    sems = pltpu.SemaphoreType.DMA((len(starts),))
+    buffer = pltpu.VMEM(shape, jnp.float32)
+    operands = (sums, c, p, *opposite)
+    return pl.pallas_call(
+        functools.partial(update_kernel, starts, fresh),
+        in_specs=([] if fresh else [ANY]) + [VMEM] * len(operands),
+        out_specs=[ANY] * 2 if fresh else ANY,
+        out_shape=[struct(*shape), struct(*strip)] if fresh else struct(*shape),
+        scratch_shapes=(
+            [buffer, pltpu.VMEM(strip, jnp.float32), sems, pltpu.SemaphoreType.DMA]
+            if fresh
+            else [buffer, sems]
+        ),
+        input_output_aliases={} if fresh else {0: 0},
+        compiler_params=LIMIT,
+    )(*(operands if fresh else (done,) + operands))
 
 
 def per_device(p, source, offsets, ids, nu_t, sg_t):
@@ -498,10 +520,13 @@
     starts = [sum(CHUNKS[:i]) for i in range(len(CHUNKS))]
 
     def exchange(i, *after):
+        return lax.ppermute(fetch(p, starts[i], CHUNKS[i], *after), "tm", across)
+
+    def ready(i, *after):
         rows = lax.slice_in_dim(p, starts[i], starts[i] + CHUNKS[i], axis=1)
-        return lax.ppermute(gate(rows, *after) if after else rows, "tm", across)
-
-    opposite = [exchange(0)]
+        return lax.ppermute(gate(rows, *after), "tm", across)
+
+    opposite = [lax.ppermute(p[:, : CHUNKS[0]], "tm", across)]
     down, up = edges(p, ids)
     top = lax.ppermute(up, "space", to_next)
     bot = lax.ppermute(down, "space", to_prev)
@@ -510,12 +535,11 @@
 
     mine, send = halves(mine, swap(send, 1))
     pieces = merge(mine, swap(send, 2), opposite[0], moments // 4)
-    opposite.append(exchange(1, pieces))
+    opposite.append(ready(1, pieces))
     total = total_for_all(among_z(pieces))
-    opposite.append(exchange(2, total))
     x = among_z(total)
-    for i in range(3, len(CHUNKS)):
-        opposite.append(exchange(i, x, *opposite[1:3]))
+    for i in range(2, len(CHUNKS)):
+        opposite.append(ready(i, x, opposite[1]))
     sg, fr, fc, dinv = operator(nu_t, sg_t, ids, top, bot, x)
 
     edge = edge_rows(x)
@@ -523,11 +547,8 @@
     own = for_core(x, swap(x, 2), edge_a, edge_b)
     c, sums = chebyshev(own, swap(own, 1), sg, fr, fc, dinv, strips)
     sums = lax.all_to_all(sums, "space", 0, 0)
-    correction = correct(sums, c)
-    updated = None
-    for start, part in zip(starts, opposite):
-        updated = update(updated, p, part, correction, start)
-    return updated, correction
+    updated, correction = update(None, sums, c, p, opposite[:-1], starts[:-1])
+    return update(updated, sums, c, p, opposite[-1:], starts[-1:]), correction
 
 
 def solution(mesh):

time: 126 us -> 123 us (0.976)
  Pallas kernels: 25.7 us -> 19.8 us
  waiting for transfers between devices: 29.8 us -> 34.4 us
  starting transfers between devices: 52.7 us -> 50.5 us
  local copies, waits for them, and re-layouts: 4.36 us -> 5.63 us
    ppermute x5 -> x4, waiting for transfers between devices: 3.32 us -> 18.4 us  [the longest x3 18.4 us: ready(): return lax.ppermute(gate(rows, *after), 'tm', across)]
    all_to_all x2, starting transfers between devices: 19.3 us -> 11.6 us  [among_z(): return lax.all_to_all(blocks, 'tm', 0, 0, axis_index_groups=groups)]
    all_to_all x2, waiting for transfers between devices: 15.6 us -> 8.91 us  [among_z(): return lax.all_to_all(blocks, 'tm', 0, 0, axis_index_groups=groups)]
    pallas_call x6 -> x2, Pallas kernels: 9.25 us -> 3.33 us  [update(): pl.pallas_call(functools.partial(update_kernel, starts, fresh), in_specs=...]
    ppermute x2, starting transfers between devices: 3.2 us -> 7.65 us  [per_device(): lax.ppermute(edge, ('tm', 'space'), r)]
    ppermute x2, waiting for transfers between devices: 5.41 us -> 1.57 us  [per_device(): lax.ppermute(edge, ('tm', 'space'), r)]
    ppermute x1, starting transfers between devices: 2.27 us -> 5.37 us  [per_device(): top = lax.ppermute(up, 'space', to_next)]
    ppermute x1, starting transfers between devices: 5.07 us -> 3.14 us  [per_device(): bot = lax.ppermute(down, 'space', to_prev)]
  transfers between devices with their start and end apart: 15 -> 14, of which waited for: 6 -> 8; matrix products, arithmetic and copies ran while one was open for 1% -> 1% of each run, Pallas kernels for 19% -> 15%
where the time goes in v3:
time: 123 us; the launch traced here: 122 us
  starting transfers between devices  50.5 us (41%)
  waiting for transfers between devices  34.4 us (28%)
  Pallas kernels  19.8 us (16%)
  blocking collectives  11.2 us (9%)
  local copies, waits for them, and re-layouts  5.63 us (5%)
    ppermute x3, waiting for transfers between devices, ready(): return lax.ppermute(gate(rows, *after), 'tm', across)  18.4 us
    ppermute x3, starting transfers between devices, ready(): return lax.ppermute(gate(rows, *after), 'tm', across)  12 us
    all_to_all x2, starting transfers between devices, among_z(): return lax.all_to_all(blocks, 'tm', 0, 0, axis_index_groups=groups)  11.6 us
    all_to_all x1, blocking collectives, per_device(): sums = lax.all_to_all(sums, 'space', 0, 0)  11.2 us
    all_to_all x2, waiting for transfers between devices, among_z(): return lax.all_to_all(blocks, 'tm', 0, 0, axis_index_groups=groups)  8.91 us
    ppermute x2, starting transfers between devices, per_device(): lax.ppermute(edge, ('tm', 'space'), r)  7.65 us
    pallas_call x1, Pallas kernels, residual(): pl.pallas_call(residual_kernel, in_specs=[SMEM] * 3 + [VMEM] * 3, out_spe...  7.48 us
    ppermute x1, starting transfers between devices, per_device(): opposite = [lax.ppermute(p[:, :CHUNKS[0]], 'tm', across)]  7.28 us
  transfers between devices with their start and end apart: 14, of which 8 were waited for; matrix products, arithmetic and copies ran while one was open for 1% of the time, Pallas kernels for 15%

profile of v3, /device:TPU:2, one launch (start us, length us, event | category | flops | bytes accessed | tf_op | source)
XLA Modules:
  0.0 122.4 jit_solution(4343650110724281120)
XLA Ops:
  0.6 1.1 slice.12
  1.8 7.3 %collective-permute-start.4 = (f32[4,40,1024]{2,1,0:T(8,128)S(1)}, f32[4,40,1024]{2,1,0:T(8,128)S(1)}, u32[]{:S(2)}, u32[]{:S(2)}) collective-permute-start(f32[4,40,1024]{2,1,0:T(8,128)S(1)} %slice.12), channel_id=1, source_target_pairs={{0,128},{8,136},{16,144},{24,152},{32,160},{40,168},{48,176},{56,1... | collective-permute-start | bytes 1966088 | tf_op jit(solution)/shard_map/ppermute | solution.py:529
  9.1 1.6 %copy-done = f32[4,128,1024]{2,1,0:T(8,128)S(1)} copy-done((f32[4,128,1024]{2,1,0:T(8,128)S(1)}, f32[4,128,1024]{2,1,0:T(8,128)}, u32[]{:S(2)}) %copy-start) | copy-done | bytes 2097176
  10.7 1.0 copy-done.2
  11.8 5.4 %collective-permute-start = (f32[16,1024]{1,0:T(8,128)S(1)}, f32[16,1024]{1,0:T(8,128)S(1)}, u32[]{:S(2)}, u32[]{:S(2)}) collective-permute-start(f32[16,1024]{1,0:T(8,128)S(1)} %get-tuple-element.17.own_last), channel_id=1, source_target_pairs={{0,1},{1,2},{2,3},{3,4},{4,5},{5,6},{6,7},{8,9},{9,10},{10,11},{11... | collective-permute-start | bytes 196616 | tf_op jit(solution)/shard_map/ppermute | solution.py:531
  17.1 3.1 %collective-permute-start.1 = (f32[16,1024]{1,0:T(8,128)S(1)}, f32[16,1024]{1,0:T(8,128)S(1)}, u32[]{:S(2)}, u32[]{:S(2)}) collective-permute-start(f32[16,1024]{1,0:T(8,128)S(1)} %get-tuple-element.16.own_first), channel_id=1, source_target_pairs={{1,0},{2,1},{3,2},{4,3},{5,4},{6,5},{7,6},{9,8},{10,9},{11,10},{12... | collective-permute-start | bytes 196616 | tf_op jit(solution)/shard_map/ppermute | solution.py:532
  20.4 7.5 %shard_map.77.acc = f32[128,1024]{1,0:T(8,128)S(1)} custom-call(s32[4]{0:T(128)S(1)} %copy-done.7, f32[8]{0:T(128)S(1)} %copy-done.6, f32[8]{0:T(128)S(1)} %copy-done.8, f32[4,128,1024]{2,1,0:T(8,128)S(1)} %copy-done.1, f32[4,128,1024]{2,1,0:T(8,128)S(1)} %copy-done.4, s32[128,1024]{1,0:T(8,128)S(1)} %copy-done.3), custom_call_target="tpu_custom_call" | custom-call | flops 10000000 | bytes 20000000 | tf_op jit(solution)/shard_map/pallas_call | solution.py:147
  27.9 0.9 shard_map.79
  28.9 1.5 %collective-permute-done.2.b = f32[64,1024]{1,0:T(8,128)S(1)} collective-permute-done((f32[64,1024]{1,0:T(8,128)S(1)}, f32[64,1024]{1,0:T(8,128)S(1)}, u32[]{:S(2)}, u32[]{:S(2)}) %collective-permute-start.2) | collective-permute-done | bytes 262176 | tf_op jit(solution)/shard_map/ppermute | solution.py:242
  30.4 1.7 %collective-permute-start.3 = (f32[32,1024]{1,0:T(8,128)S(1)}, f32[32,1024]{1,0:T(8,128)S(1)}, u32[]{:S(2)}, u32[]{:S(2)}) collective-permute-start(f32[32,1024]{1,0:T(8,128)S(1)} %get-tuple-element.21), channel_id=1, source_target_pairs={{0,16},{8,24},{16,0},{24,8},{32,48},{40,56},{48,32},{56,40},{64,80... | collective-permute-start | bytes 393224 | tf_op jit(solution)/shard_map/ppermute | solution.py:242
  32.1 4.0 %collective-permute-done.3.b = f32[32,1024]{1,0:T(8,128)S(1)} collective-permute-done((f32[32,1024]{1,0:T(8,128)S(1)}, f32[32,1024]{1,0:T(8,128)S(1)}, u32[]{:S(2)}, u32[]{:S(2)}) %collective-permute-start.3) | collective-permute-done | bytes 131104 | tf_op jit(solution)/shard_map/ppermute | solution.py:242
  36.7 8.3 %all-to-all-start = ((f32[8,32,128]{2,1,0:T(8,128)}), f32[8,32,128]{2,1,0:T(8,128)S(1)}, u32[]{:S(2)}, u32[]{:S(2)}) async-start(f32[8,32,128]{2,1,0:T(8,128)} %shard_map.81.__1_), calls=%async_computation | async-start | bytes 262144 | tf_op jit(solution)/shard_map/all_to_all | solution.py:298
  45.0 0.8 fusion
  45.8 5.9 %collective-permute-start.9 = (f32[4,16,1024]{2,1,0:T(8,128)}, f32[4,16,1024]{2,1,0:T(8,128)}, u32[]{:S(2)}, u32[]{:S(2)}) collective-permute-start(f32[4,16,1024]{2,1,0:T(8,128)} %shard_map.87), channel_id=1, source_target_pairs={{0,128},{8,136},{16,144},{24,152},{32,160},{40,168},{48,176},{56,1... | collective-permute-start | bytes 786440 | tf_op jit(solution)/shard_map/ppermute | solution.py:527
  51.8 5.2 %all-to-all-done.parts = f32[8,32,128]{2,1,0:T(8,128)S(1)} async-done(((f32[8,32,128]{2,1,0:T(8,128)}), f32[8,32,128]{2,1,0:T(8,128)S(1)}, u32[]{:S(2)}, u32[]{:S(2)}) %all-to-all-start) | async-done | bytes 131104 | tf_op jit(solution)/shard_map/all_to_all | solution.py:298
  57.6 3.4 %all-to-all-start.1 = ((f32[8,32,128]{2,1,0:T(8,128)}), f32[8,32,128]{2,1,0:T(8,128)S(1)}, u32[]{:S(2)}, u32[]{:S(2)}) async-start(f32[8,32,128]{2,1,0:T(8,128)} %shard_map.82), calls=%async_computation.1 | async-start | bytes 262144 | tf_op jit(solution)/shard_map/all_to_all | solution.py:298
  61.0 1.0 slice.14.__0_
  62.0 4.0 %collective-permute-done.9.__2_.refs_4_ = f32[4,16,1024]{2,1,0:T(8,128)} collective-permute-done((f32[4,16,1024]{2,1,0:T(8,128)}, f32[4,16,1024]{2,1,0:T(8,128)}, u32[]{:S(2)}, u32[]{:S(2)}) %collective-permute-start.9) | collective-permute-done | bytes 262176 | tf_op jit(solution)/shard_map/ppermute | solution.py:527
  66.0 3.7 %all-to-all-done.1.x._.__1_ = f32[8,32,128]{2,1,0:T(8,128)S(1)} async-done(((f32[8,32,128]{2,1,0:T(8,128)}), f32[8,32,128]{2,1,0:T(8,128)S(1)}, u32[]{:S(2)}, u32[]{:S(2)}) %all-to-all-start.1) | async-done | bytes 131104 | tf_op jit(solution)/shard_map/all_to_all | solution.py:298
  69.7 1.4 %collective-permute-start.10 = (f32[4,56,1024]{2,1,0:T(8,128)}, f32[4,56,1024]{2,1,0:T(8,128)S(1)}, u32[]{:S(2)}, u32[]{:S(2)}) collective-permute-start(f32[4,56,1024]{2,1,0:T(8,128)} %shard_map.88), channel_id=1, source_target_pairs={{0,128},{8,136},{16,144},{24,152},{32,160},{40,168},{48,176},{56,1... | collective-permute-start | bytes 2752520 | tf_op jit(solution)/shard_map/ppermute | solution.py:527
  71.1 1.6 %collective-permute-start.5 = (f32[8,32,128]{2,1,0:T(8,128)S(1)}, f32[8,32,128]{2,1,0:T(8,128)S(1)}, u32[]{:S(2)}, u32[]{:S(2)}) collective-permute-start(f32[8,32,128]{2,1,0:T(8,128)S(1)} %all-to-all-done.1.x._.__1_), channel_id=1, source_target_pairs={{0,16},{8,24},{16,0},{24,8},{32,48},{40,56},{48,32},{56,40},{64,80... | collective-permute-start | bytes 393224 | tf_op jit(solution)/shard_map/ppermute | solution.py:242
  72.7 1.9 %collective-permute-start.6 = (f32[8,8,128]{2,1,0:T(8,128)S(1)}, f32[8,8,128]{2,1,0:T(8,128)S(1)}, u32[]{:S(2)}, u32[]{:S(2)}) collective-permute-start(f32[8,8,128]{2,1,0:T(8,128)S(1)} %shard_map.83), channel_id=1, source_target_pairs={{24,1},{1,8},{25,2},{2,9},{26,3},{3,10},{27,4},{4,11},{28,5},{5,12... | collective-permute-start | bytes 98312 | tf_op jit(solution)/shard_map/ppermute | solution.py:546
  74.6 5.7 %collective-permute-start.7 = (f32[8,8,128]{2,1,0:T(8,128)S(1)}, f32[8,8,128]{2,1,0:T(8,128)S(1)}, u32[]{:S(2)}, u32[]{:S(2)}) collective-permute-start(f32[8,8,128]{2,1,0:T(8,128)S(1)} %shard_map.83), channel_id=1, source_target_pairs={{24,17},{1,24},{25,18},{2,25},{26,19},{3,26},{27,20},{4,27},{28,21... | collective-permute-start | bytes 98312 | tf_op jit(solution)/shard_map/ppermute | solution.py:546
  80.4 1.6 %collective-permute-done.7.edge_b = f32[8,8,128]{2,1,0:T(8,128)S(1)} collective-permute-done((f32[8,8,128]{2,1,0:T(8,128)S(1)}, f32[8,8,128]{2,1,0:T(8,128)S(1)}, u32[]{:S(2)}, u32[]{:S(2)}) %collective-permute-start.7) | collective-permute-done | bytes 32800 | tf_op jit(solution)/shard_map/ppermute | solution.py:546
  82.1 4.6 %collective-permute-start.11 = (f32[4,16,1024]{2,1,0:T(8,128)S(1)}, f32[4,16,1024]{2,1,0:T(8,128)S(1)}, u32[]{:S(2)}, u32[]{:S(2)}) collective-permute-start(f32[4,16,1024]{2,1,0:T(8,128)S(1)} %shard_map.90), channel_id=1, source_target_pairs={{0,128},{8,136},{16,144},{24,152},{32,160},{40,168},{48,176},{56,1... | collective-permute-start | bytes 786440 | tf_op jit(solution)/shard_map/ppermute | solution.py:527
  86.8 1.7 %shard_map.85 = (f32[144,1024]{1,0:T(8,128)S(1)}, f32[144,1024]{1,0:T(8,128)S(1)}, f32[144,1024]{1,0:T(8,128)S(1)}, f32[144,1024]{1,0:T(8,128)S(1)}) custom-call(f32[8]{0:T(128)S(1)} %copy-done.6, f32[8]{0:T(128)S(1)} %copy-done.8, s32[128,1024]{1,0:T(8,128)S(1)} %copy-done.3, f32[16,1024]{1,0:T(8,128)S(1)} %collective-permute-done.top, ...), custom_call_target="tpu_custom_call" | custom-call | tf_op jit(solution)/shard_map/pallas_call | solution.py:231
  88.4 5.0 %shard_map.86 = (f32[128,1024]{1,0:T(8,128)S(1)}, f32[8,8,128]{2,1,0:T(8,128)S(1)}) custom-call(f32[8,72,128]{2,1,0:T(8,128)S(1)} %shard_map.84.own, f32[8,72,128]{2,1,0:T(8,128)S(1)} %collective-permute-done.8.partner, f32[144,1024]{1,0:T(8,128)S(1)} %get-tuple-element.22.sg, f32[144,1024]{1,0:T(8,128)S(1)} %get-tuple-element.23.fr, ...), custom_call_target="tpu_custom_call" | custom-call | flops 10000000 | bytes 10000000 | tf_op jit(solution)/shard_map/pallas_call | solution.py:441
  93.5 11.2 %all_to_all.15.refs_0_.refs_1_ = f32[8,8,128]{2,1,0:T(8,128)S(1)} all-to-all(f32[8,8,128]{2,1,0:T(8,128)S(1)} %get-tuple-element.26), channel_id=1, replica_groups=mesh['tm'=32,'space'=8] {'space'}, dimensions={0} | all-to-all | bytes 65536 | tf_op jit(solution)/shard_map/all_to_all | solution.py:549
  104.6 11.1 %collective-permute-done.10.refs_5_ = f32[4,56,1024]{2,1,0:T(8,128)S(1)} collective-permute-done((f32[4,56,1024]{2,1,0:T(8,128)}, f32[4,56,1024]{2,1,0:T(8,128)S(1)}, u32[]{:S(2)}, u32[]{:S(2)}) %collective-permute-start.10) | collective-permute-done | bytes 917536 | tf_op jit(solution)/shard_map/ppermute | solution.py:527
  115.7 2.5 %shard_map.89 = (f32[4,128,1024]{2,1,0:T(8,128)}, f32[128,1024]{1,0:T(8,128)}) custom-call(f32[8,8,128]{2,1,0:T(8,128)S(1)} %all_to_all.15.refs_0_.refs_1_, f32[128,1024]{1,0:T(8,128)S(1)} %get-tuple-element.27.refs_1_.refs_2_, f32[4,128,1024]{2,1,0:T(8,128)S(1)} %copy-done.1, f32[4,40,1024]{2,1,0:T(8,128)S(1)} %collective-permute-done.4._.refs_3_, ...), custom_call_target="tpu_custom_call" | custom-call | tf_op jit(solution)/shard_map/pallas_call | solution.py:499
  118.3 3.3 %collective-permute-done.11.refs_4_ = f32[4,16,1024]{2,1,0:T(8,128)S(1)} collective-permute-done((f32[4,16,1024]{2,1,0:T(8,128)S(1)}, f32[4,16,1024]{2,1,0:T(8,128)S(1)}, u32[]{:S(2)}, u32[]{:S(2)}) %collective-permute-start.11) | collective-permute-done | bytes 262176 | tf_op jit(solution)/shard_map/ppermute | solution.py:527
  121.5 0.8 shard_map.91
  (33 shorter events, 1.7 us)
Async XLA Ops:
  1.8 34.3 %collective-permute-start.4 = (f32[4,40,1024]{2,1,0:T(8,128)S(1)}, f32[4,40,1024]{2,1,0:T(8,128)S(1)}, u32[]{:S(2)}, u32[]{:S(2)}) collective-permute-start(f32[4,40,1024]{2,1,0:T(8,128)S(1)} %slice.12), channel_id=1, source_target_pairs={{0,128},{8,136},{16,144},{24,152},{32,160},{40,168},{48,176},{56,1... | collective-permute-start | bytes 1966088 | tf_op jit(solution)/shard_map/ppermute | solution.py:529
  9.1 1.6 %copy-start = (f32[4,128,1024]{2,1,0:T(8,128)S(1)}, f32[4,128,1024]{2,1,0:T(8,128)}, u32[]{:S(2)}) copy-start(f32[4,128,1024]{2,1,0:T(8,128)} %refs_3_.1) | copy-start | bytes 6291460
  10.6 1.0 copy-start.2
  11.7 8.6 %copy-start.1 = (f32[4,128,1024]{2,1,0:T(8,128)S(1)}, f32[4,128,1024]{2,1,0:T(8,128)}, u32[]{:S(2)}) copy-start(f32[4,128,1024]{2,1,0:T(8,128)} %refs_3_.1) | copy-start | bytes 6291460
  11.7 8.6 %copy-start.3 = (s32[128,1024]{1,0:T(8,128)S(1)}, s32[128,1024]{1,0:T(8,128)}, u32[]{:S(2)}) copy-start(s32[128,1024]{1,0:T(8,128)} %ids.3) | copy-start | bytes 1572868
  11.7 8.6 %copy-start.4 = (f32[4,128,1024]{2,1,0:T(8,128)S(1)}, f32[4,128,1024]{2,1,0:T(8,128)}, u32[]{:S(2)}) copy-start(f32[4,128,1024]{2,1,0:T(8,128)} %src.1) | copy-start | bytes 6291460
  11.7 8.6 %copy-start.6 = (f32[8]{0:T(128)S(1)}, f32[8]{0:T(128)}, u32[]{:S(2)}) copy-start(f32[8]{0:T(128)} %nu_t.5) | copy-start | bytes 100
  11.7 8.6 %copy-start.7 = (s32[4]{0:T(128)S(1)}, s32[4]{0:T(128)}, u32[]{:S(2)}) copy-start(s32[4]{0:T(128)} %offs.3) | copy-start | bytes 52
  11.7 8.6 %copy-start.8 = (f32[8]{0:T(128)S(1)}, f32[8]{0:T(128)}, u32[]{:S(2)}) copy-start(f32[8]{0:T(128)} %sg_t.3) | copy-start | bytes 100
  11.8 16.1 %collective-permute-start = (f32[16,1024]{1,0:T(8,128)S(1)}, f32[16,1024]{1,0:T(8,128)S(1)}, u32[]{:S(2)}, u32[]{:S(2)}) collective-permute-start(f32[16,1024]{1,0:T(8,128)S(1)} %get-tuple-element.17.own_last), channel_id=1, source_target_pairs={{0,1},{1,2},{2,3},{3,4},{4,5},{5,6},{6,7},{8,9},{9,10},{10,11},{11... | collective-permute-start | bytes 196616 | tf_op jit(solution)/shard_map/ppermute | solution.py:531
  17.1 10.7 %collective-permute-start.1 = (f32[16,1024]{1,0:T(8,128)S(1)}, f32[16,1024]{1,0:T(8,128)S(1)}, u32[]{:S(2)}, u32[]{:S(2)}) collective-permute-start(f32[16,1024]{1,0:T(8,128)S(1)} %get-tuple-element.16.own_first), channel_id=1, source_target_pairs={{1,0},{2,1},{3,2},{4,3},{5,4},{6,5},{7,6},{9,8},{10,9},{11,10},{12... | collective-permute-start | bytes 196616 | tf_op jit(solution)/shard_map/ppermute | solution.py:532
  28.8 1.6 %collective-permute-start.2 = (f32[64,1024]{1,0:T(8,128)S(1)}, f32[64,1024]{1,0:T(8,128)S(1)}, u32[]{:S(2)}, u32[]{:S(2)}) collective-permute-start(f32[64,1024]{1,0:T(8,128)S(1)} %get-tuple-element.19), channel_id=1, source_target_pairs={{0,8},{8,0},{16,24},{24,16},{32,40},{40,32},{48,56},{56,48},{64,72... | collective-permute-start | bytes 786440 | tf_op jit(solution)/shard_map/ppermute | solution.py:242
  30.4 5.6 %collective-permute-start.3 = (f32[32,1024]{1,0:T(8,128)S(1)}, f32[32,1024]{1,0:T(8,128)S(1)}, u32[]{:S(2)}, u32[]{:S(2)}) collective-permute-start(f32[32,1024]{1,0:T(8,128)S(1)} %get-tuple-element.21), channel_id=1, source_target_pairs={{0,16},{8,24},{16,0},{24,8},{32,48},{40,56},{48,32},{56,40},{64,80... | collective-permute-start | bytes 393224 | tf_op jit(solution)/shard_map/ppermute | solution.py:242
  36.7 20.3 %all-to-all-start = ((f32[8,32,128]{2,1,0:T(8,128)}), f32[8,32,128]{2,1,0:T(8,128)S(1)}, u32[]{:S(2)}, u32[]{:S(2)}) async-start(f32[8,32,128]{2,1,0:T(8,128)} %shard_map.81.__1_), calls=%async_computation | async-start | bytes 262144 | tf_op jit(solution)/shard_map/all_to_all | solution.py:298
  45.8 20.2 %collective-permute-start.9 = (f32[4,16,1024]{2,1,0:T(8,128)}, f32[4,16,1024]{2,1,0:T(8,128)}, u32[]{:S(2)}, u32[]{:S(2)}) collective-permute-start(f32[4,16,1024]{2,1,0:T(8,128)} %shard_map.87), channel_id=1, source_target_pairs={{0,128},{8,136},{16,144},{24,152},{32,160},{40,168},{48,176},{56,1... | collective-permute-start | bytes 786440 | tf_op jit(solution)/shard_map/ppermute | solution.py:527
  57.6 12.1 %all-to-all-start.1 = ((f32[8,32,128]{2,1,0:T(8,128)}), f32[8,32,128]{2,1,0:T(8,128)S(1)}, u32[]{:S(2)}, u32[]{:S(2)}) async-start(f32[8,32,128]{2,1,0:T(8,128)} %shard_map.82), calls=%async_computation.1 | async-start | bytes 262144 | tf_op jit(solution)/shard_map/all_to_all | solution.py:298
  69.7 12.4 %copy-start.5 = (f32[4,16,1024]{2,1,0:T(8,128)S(1)}, f32[4,16,1024]{2,1,0:T(8,128)}, u32[]{:S(2)}) copy-start(f32[4,16,1024]{2,1,0:T(8,128)} %get-tuple-element.30.__0_) | copy-start | bytes 786436
  69.7 46.0 %collective-permute-start.10 = (f32[4,56,1024]{2,1,0:T(8,128)}, f32[4,56,1024]{2,1,0:T(8,128)S(1)}, u32[]{:S(2)}, u32[]{:S(2)}) collective-permute-start(f32[4,56,1024]{2,1,0:T(8,128)} %shard_map.88), channel_id=1, source_target_pairs={{0,128},{8,136},{16,144},{24,152},{32,160},{40,168},{48,176},{56,1... | collective-permute-start | bytes 2752520 | tf_op jit(solution)/shard_map/ppermute | solution.py:527
  71.1 10.8 %collective-permute-start.5 = (f32[8,32,128]{2,1,0:T(8,128)S(1)}, f32[8,32,128]{2,1,0:T(8,128)S(1)}, u32[]{:S(2)}, u32[]{:S(2)}) collective-permute-start(f32[8,32,128]{2,1,0:T(8,128)S(1)} %all-to-all-done.1.x._.__1_), channel_id=1, source_target_pairs={{0,16},{8,24},{16,0},{24,8},{32,48},{40,56},{48,32},{56,40},{64,80... | collective-permute-start | bytes 393224 | tf_op jit(solution)/shard_map/ppermute | solution.py:242
  72.7 7.7 %collective-permute-start.6 = (f32[8,8,128]{2,1,0:T(8,128)S(1)}, f32[8,8,128]{2,1,0:T(8,128)S(1)}, u32[]{:S(2)}, u32[]{:S(2)}) collective-permute-start(f32[8,8,128]{2,1,0:T(8,128)S(1)} %shard_map.83), channel_id=1, source_target_pairs={{24,1},{1,8},{25,2},{2,9},{26,3},{3,10},{27,4},{4,11},{28,5},{5,12... | collective-permute-start | bytes 98312 | tf_op jit(solution)/shard_map/ppermute | solution.py:546
  74.6 7.3 %collective-permute-start.7 = (f32[8,8,128]{2,1,0:T(8,128)S(1)}, f32[8,8,128]{2,1,0:T(8,128)S(1)}, u32[]{:S(2)}, u32[]{:S(2)}) collective-permute-start(f32[8,8,128]{2,1,0:T(8,128)S(1)} %shard_map.83), channel_id=1, source_target_pairs={{24,17},{1,24},{25,18},{2,25},{26,19},{3,26},{27,20},{4,27},{28,21... | collective-permute-start | bytes 98312 | tf_op jit(solution)/shard_map/ppermute | solution.py:546
  82.0 6.4 %collective-permute-start.8 = (f32[8,72,128]{2,1,0:T(8,128)S(1)}, f32[8,72,128]{2,1,0:T(8,128)S(1)}, u32[]{:S(2)}, u32[]{:S(2)}) collective-permute-start(f32[8,72,128]{2,1,0:T(8,128)S(1)} %shard_map.84.own), channel_id=1, source_target_pairs={{0,8},{8,0},{16,24},{24,16},{32,40},{40,32},{48,56},{56,48},{64,72... | collective-permute-start | bytes 884744 | tf_op jit(solution)/shard_map/ppermute | solution.py:242
  82.1 39.4 %collective-permute-start.11 = (f32[4,16,1024]{2,1,0:T(8,128)S(1)}, f32[4,16,1024]{2,1,0:T(8,128)S(1)}, u32[]{:S(2)}, u32[]{:S(2)}) collective-permute-start(f32[4,16,1024]{2,1,0:T(8,128)S(1)} %shard_map.90), channel_id=1, source_target_pairs={{0,128},{8,136},{16,144},{24,152},{32,160},{40,168},{48,176},{56,1... | collective-permute-start | bytes 786440 | tf_op jit(solution)/shard_map/ppermute | solution.py:527

commit v4 on v3

--- a/solution.py
+++ b/solution.py
@@ -16,7 +16,7 @@
 COLS = 1024
 STEPS = 4
 EXTENDED = ROWS + 16
-CHUNKS = (40, 16, 56, 16)
+CHUNKS = (40, 16, 16, 32, 24)
 
 ANY = pl.BlockSpec(memory_space=pl.ANY)
 VMEM = pl.BlockSpec(memory_space=pltpu.VMEM)
@@ -298,21 +298,6 @@
     return lax.all_to_all(blocks, "tm", 0, 0, axis_index_groups=groups)
 
 
-def fetch_kernel(start, p, *refs):
-    out = refs[-1]
-    out[...] = p[:, start : start + out.shape[1], :]
-
-
-def fetch(p, start, rows, *after):
-    return pl.pallas_call(
-        functools.partial(fetch_kernel, start),
-        in_specs=[VMEM] + [ANY] * len(after),
-        out_specs=VMEM,
-        out_shape=struct(STEPS, rows, COLS),
-        compiler_params=LIMIT,
-    )(p, *after)
-
-
 def gate_kernel(*_):
     pass
 
@@ -519,9 +504,6 @@
     to_prev = [(j, i) for i, j in to_next]
     starts = [sum(CHUNKS[:i]) for i in range(len(CHUNKS))]
 
-    def exchange(i, *after):
-        return lax.ppermute(fetch(p, starts[i], CHUNKS[i], *after), "tm", across)
-
     def ready(i, *after):
         rows = lax.slice_in_dim(p, starts[i], starts[i] + CHUNKS[i], axis=1)
         return lax.ppermute(gate(rows, *after), "tm", across)
@@ -537,9 +519,10 @@
     pieces = merge(mine, swap(send, 2), opposite[0], moments // 4)
     opposite.append(ready(1, pieces))
     total = total_for_all(among_z(pieces))
+    opposite.append(ready(2, opposite[1]))
     x = among_z(total)
-    for i in range(2, len(CHUNKS)):
-        opposite.append(ready(i, x, opposite[1]))
+    for i in range(3, len(CHUNKS)):
+        opposite.append(ready(i, x, opposite[2]))
     sg, fr, fc, dinv = operator(nu_t, sg_t, ids, top, bot, x)
 
     edge = edge_rows(x)

time: 123 us -> 121 us (0.984)
  waiting for transfers between devices: 34.4 us -> 32.9 us
  starting transfers between devices: 50.5 us -> 49.2 us
    ppermute x3 -> x4, starting transfers between devices: 12 us -> 20.4 us  [ready(): return lax.ppermute(gate(rows, *after), 'tm', across)]
    all_to_all x2, starting transfers between devices: 11.6 us -> 6.74 us  [among_z(): return lax.all_to_all(blocks, 'tm', 0, 0, axis_index_groups=groups)]
    ppermute x2, starting transfers between devices: 7.65 us -> 3.74 us  [per_device(): lax.ppermute(edge, ('tm', 'space'), r)]
    ppermute x2, waiting for transfers between devices: 1.57 us -> 5.41 us  [per_device(): lax.ppermute(edge, ('tm', 'space'), r)]
    ppermute x3 -> x4, waiting for transfers between devices: 18.4 us -> 15.2 us  [ready(): return lax.ppermute(gate(rows, *after), 'tm', across)]
    ppermute x1, starting transfers between devices: 5.37 us -> 2.27 us  [per_device(): top = lax.ppermute(up, 'space', to_next)]
    ppermute x1, starting transfers between devices: 3.14 us -> 5.34 us  [per_device(): bot = lax.ppermute(down, 'space', to_prev)]
    all_to_all x2, waiting for transfers between devices: 8.91 us -> 7.63 us  [among_z(): return lax.all_to_all(blocks, 'tm', 0, 0, axis_index_groups=groups)]
  transfers between devices with their start and end apart: 14 -> 15, of which waited for: 8 -> 7; matrix products, arithmetic and copies ran while one was open for 1% -> 1% of each run, Pallas kernels for 15% -> 15%
where the time goes in v4:
time: 121 us; the launch traced here: 120 us
  starting transfers between devices  49.2 us (41%)
  waiting for transfers between devices  32.9 us (27%)
  Pallas kernels  19.9 us (16%)
  blocking collectives  11.5 us (10%)
  local copies, waits for them, and re-layouts  5.48 us (5%)
    ppermute x4, starting transfers between devices, ready(): return lax.ppermute(gate(rows, *after), 'tm', across)  20.4 us
    ppermute x4, waiting for transfers between devices, ready(): return lax.ppermute(gate(rows, *after), 'tm', across)  15.2 us
    all_to_all x1, blocking collectives, per_device(): sums = lax.all_to_all(sums, 'space', 0, 0)  11.5 us
    all_to_all x2, waiting for transfers between devices, among_z(): return lax.all_to_all(blocks, 'tm', 0, 0, axis_index_groups=groups)  7.63 us
    pallas_call x1, Pallas kernels, residual(): pl.pallas_call(residual_kernel, in_specs=[SMEM] * 3 + [VMEM] * 3, out_spe...  7.48 us
    ppermute x1, starting transfers between devices, per_device(): opposite = [lax.ppermute(p[:, :CHUNKS[0]], 'tm', across)]  7.28 us
    all_to_all x2, starting transfers between devices, among_z(): return lax.all_to_all(blocks, 'tm', 0, 0, axis_index_groups=groups)  6.74 us
    ppermute x2, waiting for transfers between devices, per_device(): lax.ppermute(edge, ('tm', 'space'), r)  5.41 us
  transfers between devices with their start and end apart: 15, of which 7 were waited for; matrix products, arithmetic and copies ran while one was open for 1% of the time, Pallas kernels for 15%

profile of v4, /device:TPU:2, one launch (start us, length us, event | category | flops | bytes accessed | tf_op | source)
XLA Modules:
  0.0 119.9 jit_solution(7425295867734571991)
XLA Ops:
  0.6 1.1 slice.15
  1.8 7.3 %collective-permute-start.4 = (f32[4,40,1024]{2,1,0:T(8,128)S(1)}, f32[4,40,1024]{2,1,0:T(8,128)S(1)}, u32[]{:S(2)}, u32[]{:S(2)}) collective-permute-start(f32[4,40,1024]{2,1,0:T(8,128)S(1)} %slice.15), channel_id=1, source_target_pairs={{0,128},{8,136},{16,144},{24,152},{32,160},{40,168},{48,176},{56,1... | collective-permute-start | bytes 1966088 | tf_op jit(solution)/shard_map/ppermute | solution.py:511
  9.1 1.6 %copy-done = f32[4,128,1024]{2,1,0:T(8,128)S(1)} copy-done((f32[4,128,1024]{2,1,0:T(8,128)S(1)}, f32[4,128,1024]{2,1,0:T(8,128)}, u32[]{:S(2)}) %copy-start) | copy-done | bytes 2097176
  10.7 1.0 copy-done.2
  11.8 5.3 %collective-permute-start.1 = (f32[16,1024]{1,0:T(8,128)S(1)}, f32[16,1024]{1,0:T(8,128)S(1)}, u32[]{:S(2)}, u32[]{:S(2)}) collective-permute-start(f32[16,1024]{1,0:T(8,128)S(1)} %get-tuple-element.16.own_first), channel_id=1, source_target_pairs={{1,0},{2,1},{3,2},{4,3},{5,4},{6,5},{7,6},{9,8},{10,9},{11,10},{12... | collective-permute-start | bytes 196616 | tf_op jit(solution)/shard_map/ppermute | solution.py:514
  17.1 2.3 %collective-permute-start = (f32[16,1024]{1,0:T(8,128)S(1)}, f32[16,1024]{1,0:T(8,128)S(1)}, u32[]{:S(2)}, u32[]{:S(2)}) collective-permute-start(f32[16,1024]{1,0:T(8,128)S(1)} %get-tuple-element.17.own_last), channel_id=1, source_target_pairs={{0,1},{1,2},{2,3},{3,4},{4,5},{5,6},{6,7},{8,9},{9,10},{10,11},{11... | collective-permute-start | bytes 196616 | tf_op jit(solution)/shard_map/ppermute | solution.py:513
  19.5 7.5 %shard_map.77.acc = f32[128,1024]{1,0:T(8,128)S(1)} custom-call(s32[4]{0:T(128)S(1)} %copy-done.6, f32[8]{0:T(128)S(1)} %copy-done.5, f32[8]{0:T(128)S(1)} %copy-done.7, f32[4,128,1024]{2,1,0:T(8,128)S(1)} %copy-done.1, f32[4,128,1024]{2,1,0:T(8,128)S(1)} %copy-done.4, s32[128,1024]{1,0:T(8,128)S(1)} %copy-done.3), custom_call_target="tpu_custom_call" | custom-call | flops 10000000 | bytes 20000000 | tf_op jit(solution)/shard_map/pallas_call | solution.py:147
  27.0 0.9 shard_map.79
  28.0 1.5 %collective-permute-done.2.b = f32[64,1024]{1,0:T(8,128)S(1)} collective-permute-done((f32[64,1024]{1,0:T(8,128)S(1)}, f32[64,1024]{1,0:T(8,128)S(1)}, u32[]{:S(2)}, u32[]{:S(2)}) %collective-permute-start.2) | collective-permute-done | bytes 262176 | tf_op jit(solution)/shard_map/ppermute | solution.py:242
  29.5 1.7 %collective-permute-start.3 = (f32[32,1024]{1,0:T(8,128)S(1)}, f32[32,1024]{1,0:T(8,128)S(1)}, u32[]{:S(2)}, u32[]{:S(2)}) collective-permute-start(f32[32,1024]{1,0:T(8,128)S(1)} %get-tuple-element.21), channel_id=1, source_target_pairs={{0,16},{8,24},{16,0},{24,8},{32,48},{40,56},{48,32},{56,40},{64,80... | collective-permute-start | bytes 393224 | tf_op jit(solution)/shard_map/ppermute | solution.py:242
  31.2 0.8 fusion
  32.0 3.1 %collective-permute-done.3.b = f32[32,1024]{1,0:T(8,128)S(1)} collective-permute-done((f32[32,1024]{1,0:T(8,128)S(1)}, f32[32,1024]{1,0:T(8,128)S(1)}, u32[]{:S(2)}, u32[]{:S(2)}) %collective-permute-start.3) | collective-permute-done | bytes 131104 | tf_op jit(solution)/shard_map/ppermute | solution.py:242
  35.8 7.8 %collective-permute-start.9 = (f32[4,16,1024]{2,1,0:T(8,128)}, f32[4,16,1024]{2,1,0:T(8,128)}, u32[]{:S(2)}, u32[]{:S(2)}) collective-permute-start(f32[4,16,1024]{2,1,0:T(8,128)} %shard_map.87), channel_id=1, source_target_pairs={{0,128},{8,136},{16,144},{24,152},{32,160},{40,168},{48,176},{56,1... | collective-permute-start | bytes 786440 | tf_op jit(solution)/shard_map/ppermute | solution.py:509
  43.7 3.4 %all-to-all-start = ((f32[8,32,128]{2,1,0:T(8,128)}), f32[8,32,128]{2,1,0:T(8,128)S(1)}, u32[]{:S(2)}, u32[]{:S(2)}) async-start(f32[8,32,128]{2,1,0:T(8,128)} %shard_map.81.__1_), calls=%async_computation | async-start | bytes 262144 | tf_op jit(solution)/shard_map/all_to_all | solution.py:298
  47.0 8.5 %collective-permute-done.9.__1_.refs_4_ = f32[4,16,1024]{2,1,0:T(8,128)} collective-permute-done((f32[4,16,1024]{2,1,0:T(8,128)}, f32[4,16,1024]{2,1,0:T(8,128)}, u32[]{:S(2)}, u32[]{:S(2)}) %collective-permute-start.9) | collective-permute-done | bytes 262176 | tf_op jit(solution)/shard_map/ppermute | solution.py:509
  55.5 6.6 %collective-permute-start.10 = (f32[4,16,1024]{2,1,0:T(8,128)}, f32[4,16,1024]{2,1,0:T(8,128)}, u32[]{:S(2)}, u32[]{:S(2)}) collective-permute-start(f32[4,16,1024]{2,1,0:T(8,128)} %shard_map.88), channel_id=1, source_target_pairs={{0,128},{8,136},{16,144},{24,152},{32,160},{40,168},{48,176},{56,1... | collective-permute-start | bytes 786440 | tf_op jit(solution)/shard_map/ppermute | solution.py:509
  62.7 3.4 %all-to-all-start.1 = ((f32[8,32,128]{2,1,0:T(8,128)}), f32[8,32,128]{2,1,0:T(8,128)S(1)}, u32[]{:S(2)}, u32[]{:S(2)}) async-start(f32[8,32,128]{2,1,0:T(8,128)} %shard_map.82), calls=%async_computation.1 | async-start | bytes 262144 | tf_op jit(solution)/shard_map/all_to_all | solution.py:298
  66.1 0.8 slice.18.__0_
  67.0 7.6 %all-to-all-done.1.x._.__1_ = f32[8,32,128]{2,1,0:T(8,128)S(1)} async-done(((f32[8,32,128]{2,1,0:T(8,128)}), f32[8,32,128]{2,1,0:T(8,128)S(1)}, u32[]{:S(2)}, u32[]{:S(2)}) %all-to-all-start.1) | async-done | bytes 131104 | tf_op jit(solution)/shard_map/all_to_all | solution.py:298
  74.6 2.6 %collective-permute-start.11 = (f32[4,32,1024]{2,1,0:T(8,128)}, f32[4,32,1024]{2,1,0:T(8,128)S(1)}, u32[]{:S(2)}, u32[]{:S(2)}) collective-permute-start(f32[4,32,1024]{2,1,0:T(8,128)} %shard_map.89), channel_id=1, source_target_pairs={{0,128},{8,136},{16,144},{24,152},{32,160},{40,168},{48,176},{56,1... | collective-permute-start | bytes 1572872 | tf_op jit(solution)/shard_map/ppermute | solution.py:509
  77.2 1.6 %collective-permute-start.5 = (f32[8,32,128]{2,1,0:T(8,128)S(1)}, f32[8,32,128]{2,1,0:T(8,128)S(1)}, u32[]{:S(2)}, u32[]{:S(2)}) collective-permute-start(f32[8,32,128]{2,1,0:T(8,128)S(1)} %all-to-all-done.1.x._.__1_), channel_id=1, source_target_pairs={{0,16},{8,24},{16,0},{24,8},{32,48},{40,56},{48,32},{56,40},{64,80... | collective-permute-start | bytes 393224 | tf_op jit(solution)/shard_map/ppermute | solution.py:242
  78.8 3.4 %collective-permute-start.12 = (f32[4,24,1024]{2,1,0:T(8,128)S(1)}, f32[4,24,1024]{2,1,0:T(8,128)S(1)}, u32[]{:S(2)}, u32[]{:S(2)}) collective-permute-start(f32[4,24,1024]{2,1,0:T(8,128)S(1)} %shard_map.91), channel_id=1, source_target_pairs={{0,128},{8,136},{16,144},{24,152},{32,160},{40,168},{48,176},{56,1... | collective-permute-start | bytes 1179656 | tf_op jit(solution)/shard_map/ppermute | solution.py:509
  82.2 1.8 %collective-permute-start.7 = (f32[8,8,128]{2,1,0:T(8,128)S(1)}, f32[8,8,128]{2,1,0:T(8,128)S(1)}, u32[]{:S(2)}, u32[]{:S(2)}) collective-permute-start(f32[8,8,128]{2,1,0:T(8,128)S(1)} %shard_map.83), channel_id=1, source_target_pairs={{24,17},{1,24},{25,18},{2,25},{26,19},{3,26},{27,20},{4,27},{28,21... | collective-permute-start | bytes 98312 | tf_op jit(solution)/shard_map/ppermute | solution.py:529
  84.1 1.9 %collective-permute-start.6 = (f32[8,8,128]{2,1,0:T(8,128)S(1)}, f32[8,8,128]{2,1,0:T(8,128)S(1)}, u32[]{:S(2)}, u32[]{:S(2)}) collective-permute-start(f32[8,8,128]{2,1,0:T(8,128)S(1)} %shard_map.83), channel_id=1, source_target_pairs={{24,1},{1,8},{25,2},{2,9},{26,3},{3,10},{27,4},{4,11},{28,5},{5,12... | collective-permute-start | bytes 98312 | tf_op jit(solution)/shard_map/ppermute | solution.py:529
  86.0 5.4 %collective-permute-done.6.edge_a = f32[8,8,128]{2,1,0:T(8,128)S(1)} collective-permute-done((f32[8,8,128]{2,1,0:T(8,128)S(1)}, f32[8,8,128]{2,1,0:T(8,128)S(1)}, u32[]{:S(2)}, u32[]{:S(2)}) %collective-permute-start.6) | collective-permute-done | bytes 32800 | tf_op jit(solution)/shard_map/ppermute | solution.py:529
  91.5 1.7 %shard_map.85 = (f32[144,1024]{1,0:T(8,128)S(1)}, f32[144,1024]{1,0:T(8,128)S(1)}, f32[144,1024]{1,0:T(8,128)S(1)}, f32[144,1024]{1,0:T(8,128)S(1)}) custom-call(f32[8]{0:T(128)S(1)} %copy-done.5, f32[8]{0:T(128)S(1)} %copy-done.7, s32[128,1024]{1,0:T(8,128)S(1)} %copy-done.3, f32[16,1024]{1,0:T(8,128)S(1)} %collective-permute-done.top, ...), custom_call_target="tpu_custom_call" | custom-call | tf_op jit(solution)/shard_map/pallas_call | solution.py:231
  93.2 5.0 %shard_map.86 = (f32[128,1024]{1,0:T(8,128)S(1)}, f32[8,8,128]{2,1,0:T(8,128)S(1)}) custom-call(f32[8,72,128]{2,1,0:T(8,128)S(1)} %shard_map.84.own, f32[8,72,128]{2,1,0:T(8,128)S(1)} %collective-permute-done.8.partner, f32[144,1024]{1,0:T(8,128)S(1)} %get-tuple-element.22.sg, f32[144,1024]{1,0:T(8,128)S(1)} %get-tuple-element.23.fr, ...), custom_call_target="tpu_custom_call" | custom-call | flops 10000000 | bytes 10000000 | tf_op jit(solution)/shard_map/pallas_call | solution.py:426
  98.3 11.5 %all_to_all.15.refs_0_.refs_1_ = f32[8,8,128]{2,1,0:T(8,128)S(1)} all-to-all(f32[8,8,128]{2,1,0:T(8,128)S(1)} %get-tuple-element.26), channel_id=1, replica_groups=mesh['tm'=32,'space'=8] {'space'}, dimensions={0} | all-to-all | bytes 65536 | tf_op jit(solution)/shard_map/all_to_all | solution.py:532
  109.8 1.3 %collective-permute-done.11.refs_6_ = f32[4,32,1024]{2,1,0:T(8,128)S(1)} collective-permute-done((f32[4,32,1024]{2,1,0:T(8,128)}, f32[4,32,1024]{2,1,0:T(8,128)S(1)}, u32[]{:S(2)}, u32[]{:S(2)}) %collective-permute-start.11) | collective-permute-done | bytes 524320 | tf_op jit(solution)/shard_map/ppermute | solution.py:509
  111.1 2.6 %shard_map.90 = (f32[4,128,1024]{2,1,0:T(8,128)}, f32[128,1024]{1,0:T(8,128)}) custom-call(f32[8,8,128]{2,1,0:T(8,128)S(1)} %all_to_all.15.refs_0_.refs_1_, f32[128,1024]{1,0:T(8,128)S(1)} %get-tuple-element.27.refs_1_.refs_2_, f32[4,128,1024]{2,1,0:T(8,128)S(1)} %copy-done.1, f32[4,40,1024]{2,1,0:T(8,128)S(1)} %collective-permute-done.4._.refs_3_, ...), custom_call_target="tpu_custom_call" | custom-call | tf_op jit(solution)/shard_map/pallas_call | solution.py:484
  113.6 5.4 %collective-permute-done.12.refs_4_ = f32[4,24,1024]{2,1,0:T(8,128)S(1)} collective-permute-done((f32[4,24,1024]{2,1,0:T(8,128)S(1)}, f32[4,24,1024]{2,1,0:T(8,128)S(1)}, u32[]{:S(2)}, u32[]{:S(2)}) %collective-permute-start.12) | collective-permute-done | bytes 393248 | tf_op jit(solution)/shard_map/ppermute | solution.py:509
  119.0 0.9 shard_map.92
  (35 shorter events, 1.7 us)
Async XLA Ops:
  1.8 33.4 %collective-permute-start.4 = (f32[4,40,1024]{2,1,0:T(8,128)S(1)}, f32[4,40,1024]{2,1,0:T(8,128)S(1)}, u32[]{:S(2)}, u32[]{:S(2)}) collective-permute-start(f32[4,40,1024]{2,1,0:T(8,128)S(1)} %slice.15), channel_id=1, source_target_pairs={{0,128},{8,136},{16,144},{24,152},{32,160},{40,168},{48,176},{56,1... | collective-permute-start | bytes 1966088 | tf_op jit(solution)/shard_map/ppermute | solution.py:511
  9.1 1.6 %copy-start = (f32[4,128,1024]{2,1,0:T(8,128)S(1)}, f32[4,128,1024]{2,1,0:T(8,128)}, u32[]{:S(2)}) copy-start(f32[4,128,1024]{2,1,0:T(8,128)} %refs_3_.1) | copy-start | bytes 6291460
  10.6 1.0 copy-start.2
  11.7 7.7 %copy-start.1 = (f32[4,128,1024]{2,1,0:T(8,128)S(1)}, f32[4,128,1024]{2,1,0:T(8,128)}, u32[]{:S(2)}) copy-start(f32[4,128,1024]{2,1,0:T(8,128)} %refs_3_.1) | copy-start | bytes 6291460
  11.7 7.7 %copy-start.3 = (s32[128,1024]{1,0:T(8,128)S(1)}, s32[128,1024]{1,0:T(8,128)}, u32[]{:S(2)}) copy-start(s32[128,1024]{1,0:T(8,128)} %ids.3) | copy-start | bytes 1572868
  11.7 7.7 %copy-start.4 = (f32[4,128,1024]{2,1,0:T(8,128)S(1)}, f32[4,128,1024]{2,1,0:T(8,128)}, u32[]{:S(2)}) copy-start(f32[4,128,1024]{2,1,0:T(8,128)} %src.1) | copy-start | bytes 6291460
  11.7 7.7 %copy-start.5 = (f32[8]{0:T(128)S(1)}, f32[8]{0:T(128)}, u32[]{:S(2)}) copy-start(f32[8]{0:T(128)} %nu_t.5) | copy-start | bytes 100
  11.7 7.7 %copy-start.6 = (s32[4]{0:T(128)S(1)}, s32[4]{0:T(128)}, u32[]{:S(2)}) copy-start(s32[4]{0:T(128)} %offs.3) | copy-start | bytes 52
  11.7 7.7 %copy-start.7 = (f32[8]{0:T(128)S(1)}, f32[8]{0:T(128)}, u32[]{:S(2)}) copy-start(f32[8]{0:T(128)} %sg_t.3) | copy-start | bytes 100
  11.8 15.2 %collective-permute-start.1 = (f32[16,1024]{1,0:T(8,128)S(1)}, f32[16,1024]{1,0:T(8,128)S(1)}, u32[]{:S(2)}, u32[]{:S(2)}) collective-permute-start(f32[16,1024]{1,0:T(8,128)S(1)} %get-tuple-element.16.own_first), channel_id=1, source_target_pairs={{1,0},{2,1},{3,2},{4,3},{5,4},{6,5},{7,6},{9,8},{10,9},{11,10},{12... | collective-permute-start | bytes 196616 | tf_op jit(solution)/shard_map/ppermute | solution.py:514
  17.1 9.8 %collective-permute-start = (f32[16,1024]{1,0:T(8,128)S(1)}, f32[16,1024]{1,0:T(8,128)S(1)}, u32[]{:S(2)}, u32[]{:S(2)}) collective-permute-start(f32[16,1024]{1,0:T(8,128)S(1)} %get-tuple-element.17.own_last), channel_id=1, source_target_pairs={{0,1},{1,2},{2,3},{3,4},{4,5},{5,6},{6,7},{8,9},{9,10},{10,11},{11... | collective-permute-start | bytes 196616 | tf_op jit(solution)/shard_map/ppermute | solution.py:513
  27.9 1.6 %collective-permute-start.2 = (f32[64,1024]{1,0:T(8,128)S(1)}, f32[64,1024]{1,0:T(8,128)S(1)}, u32[]{:S(2)}, u32[]{:S(2)}) collective-permute-start(f32[64,1024]{1,0:T(8,128)S(1)} %get-tuple-element.19), channel_id=1, source_target_pairs={{0,8},{8,0},{16,24},{24,16},{32,40},{40,32},{48,56},{56,48},{64,72... | collective-permute-start | bytes 786440 | tf_op jit(solution)/shard_map/ppermute | solution.py:242
  29.5 5.6 %collective-permute-start.3 = (f32[32,1024]{1,0:T(8,128)S(1)}, f32[32,1024]{1,0:T(8,128)S(1)}, u32[]{:S(2)}, u32[]{:S(2)}) collective-permute-start(f32[32,1024]{1,0:T(8,128)S(1)} %get-tuple-element.21), channel_id=1, source_target_pairs={{0,16},{8,24},{16,0},{24,8},{32,48},{40,56},{48,32},{56,40},{64,80... | collective-permute-start | bytes 393224 | tf_op jit(solution)/shard_map/ppermute | solution.py:242
  35.8 19.7 %collective-permute-start.9 = (f32[4,16,1024]{2,1,0:T(8,128)}, f32[4,16,1024]{2,1,0:T(8,128)}, u32[]{:S(2)}, u32[]{:S(2)}) collective-permute-start(f32[4,16,1024]{2,1,0:T(8,128)} %shard_map.87), channel_id=1, source_target_pairs={{0,128},{8,136},{16,144},{24,152},{32,160},{40,168},{48,176},{56,1... | collective-permute-start | bytes 786440 | tf_op jit(solution)/shard_map/ppermute | solution.py:509
  43.7 18.4 %all-to-all-start = ((f32[8,32,128]{2,1,0:T(8,128)}), f32[8,32,128]{2,1,0:T(8,128)S(1)}, u32[]{:S(2)}, u32[]{:S(2)}) async-start(f32[8,32,128]{2,1,0:T(8,128)} %shard_map.81.__1_), calls=%async_computation | async-start | bytes 262144 | tf_op jit(solution)/shard_map/all_to_all | solution.py:298
  55.5 19.1 %collective-permute-start.10 = (f32[4,16,1024]{2,1,0:T(8,128)}, f32[4,16,1024]{2,1,0:T(8,128)}, u32[]{:S(2)}, u32[]{:S(2)}) collective-permute-start(f32[4,16,1024]{2,1,0:T(8,128)} %shard_map.88), channel_id=1, source_target_pairs={{0,128},{8,136},{16,144},{24,152},{32,160},{40,168},{48,176},{56,1... | collective-permute-start | bytes 786440 | tf_op jit(solution)/shard_map/ppermute | solution.py:509
  62.7 11.8 %all-to-all-start.1 = ((f32[8,32,128]{2,1,0:T(8,128)}), f32[8,32,128]{2,1,0:T(8,128)S(1)}, u32[]{:S(2)}, u32[]{:S(2)}) async-start(f32[8,32,128]{2,1,0:T(8,128)} %shard_map.82), calls=%async_computation.1 | async-start | bytes 262144 | tf_op jit(solution)/shard_map/all_to_all | solution.py:298
  74.6 36.5 %collective-permute-start.11 = (f32[4,32,1024]{2,1,0:T(8,128)}, f32[4,32,1024]{2,1,0:T(8,128)S(1)}, u32[]{:S(2)}, u32[]{:S(2)}) collective-permute-start(f32[4,32,1024]{2,1,0:T(8,128)} %shard_map.89), channel_id=1, source_target_pairs={{0,128},{8,136},{16,144},{24,152},{32,160},{40,168},{48,176},{56,1... | collective-permute-start | bytes 1572872 | tf_op jit(solution)/shard_map/ppermute | solution.py:509
  77.2 14.2 %collective-permute-start.5 = (f32[8,32,128]{2,1,0:T(8,128)S(1)}, f32[8,32,128]{2,1,0:T(8,128)S(1)}, u32[]{:S(2)}, u32[]{:S(2)}) collective-permute-start(f32[8,32,128]{2,1,0:T(8,128)S(1)} %all-to-all-done.1.x._.__1_), channel_id=1, source_target_pairs={{0,16},{8,24},{16,0},{24,8},{32,48},{40,56},{48,32},{56,40},{64,80... | collective-permute-start | bytes 393224 | tf_op jit(solution)/shard_map/ppermute | solution.py:242
  78.8 40.2 %collective-permute-start.12 = (f32[4,24,1024]{2,1,0:T(8,128)S(1)}, f32[4,24,1024]{2,1,0:T(8,128)S(1)}, u32[]{:S(2)}, u32[]{:S(2)}) collective-permute-start(f32[4,24,1024]{2,1,0:T(8,128)S(1)} %shard_map.91), channel_id=1, source_target_pairs={{0,128},{8,136},{16,144},{24,152},{32,160},{40,168},{48,176},{56,1... | collective-permute-start | bytes 1179656 | tf_op jit(solution)/shard_map/ppermute | solution.py:509
  82.2 3.8 %collective-permute-start.7 = (f32[8,8,128]{2,1,0:T(8,128)S(1)}, f32[8,8,128]{2,1,0:T(8,128)S(1)}, u32[]{:S(2)}, u32[]{:S(2)}) collective-permute-start(f32[8,8,128]{2,1,0:T(8,128)S(1)} %shard_map.83), channel_id=1, source_target_pairs={{24,17},{1,24},{25,18},{2,25},{26,19},{3,26},{27,20},{4,27},{28,21... | collective-permute-start | bytes 98312 | tf_op jit(solution)/shard_map/ppermute | solution.py:529
  84.1 7.3 %collective-permute-start.6 = (f32[8,8,128]{2,1,0:T(8,128)S(1)}, f32[8,8,128]{2,1,0:T(8,128)S(1)}, u32[]{:S(2)}, u32[]{:S(2)}) collective-permute-start(f32[8,8,128]{2,1,0:T(8,128)S(1)} %shard_map.83), channel_id=1, source_target_pairs={{24,1},{1,8},{25,2},{2,9},{26,3},{3,10},{27,4},{4,11},{28,5},{5,12... | collective-permute-start | bytes 98312 | tf_op jit(solution)/shard_map/ppermute | solution.py:529
  91.4 1.8 %collective-permute-start.8 = (f32[8,72,128]{2,1,0:T(8,128)S(1)}, f32[8,72,128]{2,1,0:T(8,128)S(1)}, u32[]{:S(2)}, u32[]{:S(2)}) collective-permute-start(f32[8,72,128]{2,1,0:T(8,128)S(1)} %shard_map.84.own), channel_id=1, source_target_pairs={{0,8},{8,0},{16,24},{24,16},{32,40},{40,32},{48,56},{56,48},{64,72... | collective-permute-start | bytes 884744 | tf_op jit(solution)/shard_map/ppermute | solution.py:242

commit v5 on v4

--- a/solution.py
+++ b/solution.py
@@ -521,9 +521,9 @@
     total = total_for_all(among_z(pieces))
     opposite.append(ready(2, opposite[1]))
     x = among_z(total)
-    for i in range(3, len(CHUNKS)):
-        opposite.append(ready(i, x, opposite[2]))
+    opposite.append(ready(3, x, opposite[2]))
     sg, fr, fc, dinv = operator(nu_t, sg_t, ids, top, bot, x)
+    opposite.append(ready(4, sg))
 
     edge = edge_rows(x)
     edge_a, edge_b = (lax.ppermute(edge, ("tm", "space"), r) for r in edge_routes(moments, strips))

time: 121 us -> 121 us (level)
    ppermute x4, waiting for transfers between devices: 4.66 us -> 6.23 us  [swap(): lax.ppermute(x, 'tm', [(i, i ^ bit) for i in range(lax.axis_size('tm'))])]
    ppermute x4, waiting for transfers between devices: 15.2 us -> 13.8 us  [ready(): return lax.ppermute(gate(rows, *after), 'tm', across)]
where the time goes in v5:
time: 121 us; the launch traced here: 120 us
  starting transfers between devices  49.2 us (41%)
  waiting for transfers between devices  33.1 us (27%)
  Pallas kernels  19.7 us (16%)
  blocking collectives  11.5 us (10%)
  local copies, waits for them, and re-layouts  5.48 us (5%)
    ppermute x4, starting transfers between devices, ready(): return lax.ppermute(gate(rows, *after), 'tm', across)  20.4 us
    ppermute x4, waiting for transfers between devices, ready(): return lax.ppermute(gate(rows, *after), 'tm', across)  13.8 us
    all_to_all x1, blocking collectives, per_device(): sums = lax.all_to_all(sums, 'space', 0, 0)  11.5 us
    all_to_all x2, waiting for transfers between devices, among_z(): return lax.all_to_all(blocks, 'tm', 0, 0, axis_index_groups=groups)  7.63 us
    pallas_call x1, Pallas kernels, residual(): pl.pallas_call(residual_kernel, in_specs=[SMEM] * 3 + [VMEM] * 3, out_spe...  7.48 us
    ppermute x1, starting transfers between devices, per_device(): opposite = [lax.ppermute(p[:, :CHUNKS[0]], 'tm', across)]  7.28 us
    all_to_all x2, starting transfers between devices, among_z(): return lax.all_to_all(blocks, 'tm', 0, 0, axis_index_groups=groups)  6.74 us
    ppermute x4, waiting for transfers between devices, swap(): lax.ppermute(x, 'tm', [(i, i ^ bit) for i in range(lax.axis_size('tm'))])  6.23 us
  transfers between devices with their start and end apart: 15, of which 7 were waited for; matrix products, arithmetic and copies ran while one was open for 1% of the time, Pallas kernels for 15%

profile of v5, /device:TPU:2, one launch (start us, length us, event | category | flops | bytes accessed | tf_op | source)
XLA Modules:
  0.0 119.9 jit_solution(12117378487729815803)
XLA Ops:
  0.6 1.1 slice.15
  1.8 7.3 %collective-permute-start.4 = (f32[4,40,1024]{2,1,0:T(8,128)S(1)}, f32[4,40,1024]{2,1,0:T(8,128)S(1)}, u32[]{:S(2)}, u32[]{:S(2)}) collective-permute-start(f32[4,40,1024]{2,1,0:T(8,128)S(1)} %slice.15), channel_id=1, source_target_pairs={{0,128},{8,136},{16,144},{24,152},{32,160},{40,168},{48,176},{56,1... | collective-permute-start | bytes 1966088 | tf_op jit(solution)/shard_map/ppermute | solution.py:511
  9.1 1.6 %copy-done = f32[4,128,1024]{2,1,0:T(8,128)S(1)} copy-done((f32[4,128,1024]{2,1,0:T(8,128)S(1)}, f32[4,128,1024]{2,1,0:T(8,128)}, u32[]{:S(2)}) %copy-start) | copy-done | bytes 2097176
  10.7 1.0 copy-done.2
  11.8 5.3 %collective-permute-start.1 = (f32[16,1024]{1,0:T(8,128)S(1)}, f32[16,1024]{1,0:T(8,128)S(1)}, u32[]{:S(2)}, u32[]{:S(2)}) collective-permute-start(f32[16,1024]{1,0:T(8,128)S(1)} %get-tuple-element.16.own_first), channel_id=1, source_target_pairs={{1,0},{2,1},{3,2},{4,3},{5,4},{6,5},{7,6},{9,8},{10,9},{11,10},{12... | collective-permute-start | bytes 196616 | tf_op jit(solution)/shard_map/ppermute | solution.py:514
  17.1 2.3 %collective-permute-start = (f32[16,1024]{1,0:T(8,128)S(1)}, f32[16,1024]{1,0:T(8,128)S(1)}, u32[]{:S(2)}, u32[]{:S(2)}) collective-permute-start(f32[16,1024]{1,0:T(8,128)S(1)} %get-tuple-element.17.own_last), channel_id=1, source_target_pairs={{0,1},{1,2},{2,3},{3,4},{4,5},{5,6},{6,7},{8,9},{9,10},{10,11},{11... | collective-permute-start | bytes 196616 | tf_op jit(solution)/shard_map/ppermute | solution.py:513
  19.5 7.5 %shard_map.77.acc = f32[128,1024]{1,0:T(8,128)S(1)} custom-call(s32[4]{0:T(128)S(1)} %copy-done.6, f32[8]{0:T(128)S(1)} %copy-done.5, f32[8]{0:T(128)S(1)} %copy-done.7, f32[4,128,1024]{2,1,0:T(8,128)S(1)} %copy-done.1, f32[4,128,1024]{2,1,0:T(8,128)S(1)} %copy-done.4, s32[128,1024]{1,0:T(8,128)S(1)} %copy-done.3), custom_call_target="tpu_custom_call" | custom-call | flops 10000000 | bytes 20000000 | tf_op jit(solution)/shard_map/pallas_call | solution.py:147
  27.0 0.9 shard_map.79
  28.0 1.5 %collective-permute-done.2.b = f32[64,1024]{1,0:T(8,128)S(1)} collective-permute-done((f32[64,1024]{1,0:T(8,128)S(1)}, f32[64,1024]{1,0:T(8,128)S(1)}, u32[]{:S(2)}, u32[]{:S(2)}) %collective-permute-start.2) | collective-permute-done | bytes 262176 | tf_op jit(solution)/shard_map/ppermute | solution.py:242
  29.5 1.7 %collective-permute-start.3 = (f32[32,1024]{1,0:T(8,128)S(1)}, f32[32,1024]{1,0:T(8,128)S(1)}, u32[]{:S(2)}, u32[]{:S(2)}) collective-permute-start(f32[32,1024]{1,0:T(8,128)S(1)} %get-tuple-element.21), channel_id=1, source_target_pairs={{0,16},{8,24},{16,0},{24,8},{32,48},{40,56},{48,32},{56,40},{64,80... | collective-permute-start | bytes 393224 | tf_op jit(solution)/shard_map/ppermute | solution.py:242
  31.2 0.8 fusion
  32.0 3.1 %collective-permute-done.3.b = f32[32,1024]{1,0:T(8,128)S(1)} collective-permute-done((f32[32,1024]{1,0:T(8,128)S(1)}, f32[32,1024]{1,0:T(8,128)S(1)}, u32[]{:S(2)}, u32[]{:S(2)}) %collective-permute-start.3) | collective-permute-done | bytes 131104 | tf_op jit(solution)/shard_map/ppermute | solution.py:242
  35.8 7.8 %collective-permute-start.9 = (f32[4,16,1024]{2,1,0:T(8,128)}, f32[4,16,1024]{2,1,0:T(8,128)}, u32[]{:S(2)}, u32[]{:S(2)}) collective-permute-start(f32[4,16,1024]{2,1,0:T(8,128)} %shard_map.87), channel_id=1, source_target_pairs={{0,128},{8,136},{16,144},{24,152},{32,160},{40,168},{48,176},{56,1... | collective-permute-start | bytes 786440 | tf_op jit(solution)/shard_map/ppermute | solution.py:509
  43.7 3.4 %all-to-all-start = ((f32[8,32,128]{2,1,0:T(8,128)}), f32[8,32,128]{2,1,0:T(8,128)S(1)}, u32[]{:S(2)}, u32[]{:S(2)}) async-start(f32[8,32,128]{2,1,0:T(8,128)} %shard_map.81.__1_), calls=%async_computation | async-start | bytes 262144 | tf_op jit(solution)/shard_map/all_to_all | solution.py:298
  47.0 8.5 %collective-permute-done.9.__1_.refs_4_ = f32[4,16,1024]{2,1,0:T(8,128)} collective-permute-done((f32[4,16,1024]{2,1,0:T(8,128)}, f32[4,16,1024]{2,1,0:T(8,128)}, u32[]{:S(2)}, u32[]{:S(2)}) %collective-permute-start.9) | collective-permute-done | bytes 262176 | tf_op jit(solution)/shard_map/ppermute | solution.py:509
  55.5 6.6 %collective-permute-start.10 = (f32[4,16,1024]{2,1,0:T(8,128)}, f32[4,16,1024]{2,1,0:T(8,128)}, u32[]{:S(2)}, u32[]{:S(2)}) collective-permute-start(f32[4,16,1024]{2,1,0:T(8,128)} %shard_map.88), channel_id=1, source_target_pairs={{0,128},{8,136},{16,144},{24,152},{32,160},{40,168},{48,176},{56,1... | collective-permute-start | bytes 786440 | tf_op jit(solution)/shard_map/ppermute | solution.py:509
  62.7 3.4 %all-to-all-start.1 = ((f32[8,32,128]{2,1,0:T(8,128)}), f32[8,32,128]{2,1,0:T(8,128)S(1)}, u32[]{:S(2)}, u32[]{:S(2)}) async-start(f32[8,32,128]{2,1,0:T(8,128)} %shard_map.82), calls=%async_computation.1 | async-start | bytes 262144 | tf_op jit(solution)/shard_map/all_to_all | solution.py:298
  66.1 0.8 slice.18.__0_
  67.0 7.6 %all-to-all-done.1.x._.__1_ = f32[8,32,128]{2,1,0:T(8,128)S(1)} async-done(((f32[8,32,128]{2,1,0:T(8,128)}), f32[8,32,128]{2,1,0:T(8,128)S(1)}, u32[]{:S(2)}, u32[]{:S(2)}) %all-to-all-start.1) | async-done | bytes 131104 | tf_op jit(solution)/shard_map/all_to_all | solution.py:298
  74.6 2.6 %collective-permute-start.11 = (f32[4,32,1024]{2,1,0:T(8,128)}, f32[4,32,1024]{2,1,0:T(8,128)S(1)}, u32[]{:S(2)}, u32[]{:S(2)}) collective-permute-start(f32[4,32,1024]{2,1,0:T(8,128)} %shard_map.89), channel_id=1, source_target_pairs={{0,128},{8,136},{16,144},{24,152},{32,160},{40,168},{48,176},{56,1... | collective-permute-start | bytes 1572872 | tf_op jit(solution)/shard_map/ppermute | solution.py:509
  77.2 1.6 %collective-permute-start.5 = (f32[8,32,128]{2,1,0:T(8,128)S(1)}, f32[8,32,128]{2,1,0:T(8,128)S(1)}, u32[]{:S(2)}, u32[]{:S(2)}) collective-permute-start(f32[8,32,128]{2,1,0:T(8,128)S(1)} %all-to-all-done.1.x._.__1_), channel_id=1, source_target_pairs={{0,16},{8,24},{16,0},{24,8},{32,48},{40,56},{48,32},{56,40},{64,80... | collective-permute-start | bytes 393224 | tf_op jit(solution)/shard_map/ppermute | solution.py:242
  78.8 1.7 %shard_map.85 = (f32[144,1024]{1,0:T(8,128)S(1)}, f32[144,1024]{1,0:T(8,128)S(1)}, f32[144,1024]{1,0:T(8,128)S(1)}, f32[144,1024]{1,0:T(8,128)S(1)}) custom-call(f32[8]{0:T(128)S(1)} %copy-done.5, f32[8]{0:T(128)S(1)} %copy-done.7, s32[128,1024]{1,0:T(8,128)S(1)} %copy-done.3, f32[16,1024]{1,0:T(8,128)S(1)} %collective-permute-done.top, ...), custom_call_target="tpu_custom_call" | custom-call | tf_op jit(solution)/shard_map/pallas_call | solution.py:231
  80.5 3.4 %collective-permute-start.12 = (f32[4,24,1024]{2,1,0:T(8,128)S(1)}, f32[4,24,1024]{2,1,0:T(8,128)S(1)}, u32[]{:S(2)}, u32[]{:S(2)}) collective-permute-start(f32[4,24,1024]{2,1,0:T(8,128)S(1)} %shard_map.91), channel_id=1, source_target_pairs={{0,128},{8,136},{16,144},{24,152},{32,160},{40,168},{48,176},{56,1... | collective-permute-start | bytes 1179656 | tf_op jit(solution)/shard_map/ppermute | solution.py:509
  83.9 1.8 %collective-permute-start.7 = (f32[8,8,128]{2,1,0:T(8,128)S(1)}, f32[8,8,128]{2,1,0:T(8,128)S(1)}, u32[]{:S(2)}, u32[]{:S(2)}) collective-permute-start(f32[8,8,128]{2,1,0:T(8,128)S(1)} %shard_map.83), channel_id=1, source_target_pairs={{24,17},{1,24},{25,18},{2,25},{26,19},{3,26},{27,20},{4,27},{28,21... | collective-permute-start | bytes 98312 | tf_op jit(solution)/shard_map/ppermute | solution.py:529
  85.7 1.9 %collective-permute-start.6 = (f32[8,8,128]{2,1,0:T(8,128)S(1)}, f32[8,8,128]{2,1,0:T(8,128)S(1)}, u32[]{:S(2)}, u32[]{:S(2)}) collective-permute-start(f32[8,8,128]{2,1,0:T(8,128)S(1)} %shard_map.83), channel_id=1, source_target_pairs={{24,1},{1,8},{25,2},{2,9},{26,3},{3,10},{27,4},{4,11},{28,5},{5,12... | collective-permute-start | bytes 98312 | tf_op jit(solution)/shard_map/ppermute | solution.py:529
  87.7 5.4 %collective-permute-done.6.edge_a = f32[8,8,128]{2,1,0:T(8,128)S(1)} collective-permute-done((f32[8,8,128]{2,1,0:T(8,128)S(1)}, f32[8,8,128]{2,1,0:T(8,128)S(1)}, u32[]{:S(2)}, u32[]{:S(2)}) %collective-permute-start.6) | collective-permute-done | bytes 32800 | tf_op jit(solution)/shard_map/ppermute | solution.py:529
  93.2 1.6 %collective-permute-done.8.partner = f32[8,72,128]{2,1,0:T(8,128)S(1)} collective-permute-done((f32[8,72,128]{2,1,0:T(8,128)S(1)}, f32[8,72,128]{2,1,0:T(8,128)S(1)}, u32[]{:S(2)}, u32[]{:S(2)}) %collective-permute-start.8) | collective-permute-done | bytes 294944 | tf_op jit(solution)/shard_map/ppermute | solution.py:242
  94.8 4.9 %shard_map.86 = (f32[128,1024]{1,0:T(8,128)S(1)}, f32[8,8,128]{2,1,0:T(8,128)S(1)}) custom-call(f32[8,72,128]{2,1,0:T(8,128)S(1)} %shard_map.84.own, f32[8,72,128]{2,1,0:T(8,128)S(1)} %collective-permute-done.8.partner, f32[144,1024]{1,0:T(8,128)S(1)} %get-tuple-element.22.sg.__1_, f32[144,1024]{1,0:T(8,128)S(1)} %get-tuple-element.23.fr, ...), custom_call_target="tpu_custom_call" | custom-call | flops 10000000 | bytes 10000000 | tf_op jit(solution)/shard_map/pallas_call | solution.py:426
  99.6 11.5 %all_to_all.15.refs_0_.refs_1_ = f32[8,8,128]{2,1,0:T(8,128)S(1)} all-to-all(f32[8,8,128]{2,1,0:T(8,128)S(1)} %get-tuple-element.26), channel_id=1, replica_groups=mesh['tm'=32,'space'=8] {'space'}, dimensions={0} | all-to-all | bytes 65536 | tf_op jit(solution)/shard_map/all_to_all | solution.py:532
  111.1 2.6 %shard_map.90 = (f32[4,128,1024]{2,1,0:T(8,128)}, f32[128,1024]{1,0:T(8,128)}) custom-call(f32[8,8,128]{2,1,0:T(8,128)S(1)} %all_to_all.15.refs_0_.refs_1_, f32[128,1024]{1,0:T(8,128)S(1)} %get-tuple-element.27.refs_1_.refs_2_, f32[4,128,1024]{2,1,0:T(8,128)S(1)} %copy-done.1, f32[4,40,1024]{2,1,0:T(8,128)S(1)} %collective-permute-done.4._.refs_3_, ...), custom_call_target="tpu_custom_call" | custom-call | tf_op jit(solution)/shard_map/pallas_call | solution.py:484
  113.7 5.3 %collective-permute-done.12.refs_4_ = f32[4,24,1024]{2,1,0:T(8,128)S(1)} collective-permute-done((f32[4,24,1024]{2,1,0:T(8,128)S(1)}, f32[4,24,1024]{2,1,0:T(8,128)S(1)}, u32[]{:S(2)}, u32[]{:S(2)}) %collective-permute-start.12) | collective-permute-done | bytes 393248 | tf_op jit(solution)/shard_map/ppermute | solution.py:509
  119.0 0.9 shard_map.92
  (35 shorter events, 1.7 us)
Async XLA Ops:
  1.8 33.4 %collective-permute-start.4 = (f32[4,40,1024]{2,1,0:T(8,128)S(1)}, f32[4,40,1024]{2,1,0:T(8,128)S(1)}, u32[]{:S(2)}, u32[]{:S(2)}) collective-permute-start(f32[4,40,1024]{2,1,0:T(8,128)S(1)} %slice.15), channel_id=1, source_target_pairs={{0,128},{8,136},{16,144},{24,152},{32,160},{40,168},{48,176},{56,1... | collective-permute-start | bytes 1966088 | tf_op jit(solution)/shard_map/ppermute | solution.py:511
  9.1 1.6 %copy-start = (f32[4,128,1024]{2,1,0:T(8,128)S(1)}, f32[4,128,1024]{2,1,0:T(8,128)}, u32[]{:S(2)}) copy-start(f32[4,128,1024]{2,1,0:T(8,128)} %refs_3_.1) | copy-start | bytes 6291460
  10.6 1.0 copy-start.2
  11.7 7.7 %copy-start.1 = (f32[4,128,1024]{2,1,0:T(8,128)S(1)}, f32[4,128,1024]{2,1,0:T(8,128)}, u32[]{:S(2)}) copy-start(f32[4,128,1024]{2,1,0:T(8,128)} %refs_3_.1) | copy-start | bytes 6291460
  11.7 7.7 %copy-start.3 = (s32[128,1024]{1,0:T(8,128)S(1)}, s32[128,1024]{1,0:T(8,128)}, u32[]{:S(2)}) copy-start(s32[128,1024]{1,0:T(8,128)} %ids.3) | copy-start | bytes 1572868
  11.7 7.7 %copy-start.4 = (f32[4,128,1024]{2,1,0:T(8,128)S(1)}, f32[4,128,1024]{2,1,0:T(8,128)}, u32[]{:S(2)}) copy-start(f32[4,128,1024]{2,1,0:T(8,128)} %src.1) | copy-start | bytes 6291460
  11.7 7.7 %copy-start.5 = (f32[8]{0:T(128)S(1)}, f32[8]{0:T(128)}, u32[]{:S(2)}) copy-start(f32[8]{0:T(128)} %nu_t.5) | copy-start | bytes 100
  11.7 7.7 %copy-start.6 = (s32[4]{0:T(128)S(1)}, s32[4]{0:T(128)}, u32[]{:S(2)}) copy-start(s32[4]{0:T(128)} %offs.3) | copy-start | bytes 52
  11.7 7.7 %copy-start.7 = (f32[8]{0:T(128)S(1)}, f32[8]{0:T(128)}, u32[]{:S(2)}) copy-start(f32[8]{0:T(128)} %sg_t.3) | copy-start | bytes 100
  11.8 15.2 %collective-permute-start.1 = (f32[16,1024]{1,0:T(8,128)S(1)}, f32[16,1024]{1,0:T(8,128)S(1)}, u32[]{:S(2)}, u32[]{:S(2)}) collective-permute-start(f32[16,1024]{1,0:T(8,128)S(1)} %get-tuple-element.16.own_first), channel_id=1, source_target_pairs={{1,0},{2,1},{3,2},{4,3},{5,4},{6,5},{7,6},{9,8},{10,9},{11,10},{12... | collective-permute-start | bytes 196616 | tf_op jit(solution)/shard_map/ppermute | solution.py:514
  17.1 9.8 %collective-permute-start = (f32[16,1024]{1,0:T(8,128)S(1)}, f32[16,1024]{1,0:T(8,128)S(1)}, u32[]{:S(2)}, u32[]{:S(2)}) collective-permute-start(f32[16,1024]{1,0:T(8,128)S(1)} %get-tuple-element.17.own_last), channel_id=1, source_target_pairs={{0,1},{1,2},{2,3},{3,4},{4,5},{5,6},{6,7},{8,9},{9,10},{10,11},{11... | collective-permute-start | bytes 196616 | tf_op jit(solution)/shard_map/ppermute | solution.py:513
  27.9 1.6 %collective-permute-start.2 = (f32[64,1024]{1,0:T(8,128)S(1)}, f32[64,1024]{1,0:T(8,128)S(1)}, u32[]{:S(2)}, u32[]{:S(2)}) collective-permute-start(f32[64,1024]{1,0:T(8,128)S(1)} %get-tuple-element.19), channel_id=1, source_target_pairs={{0,8},{8,0},{16,24},{24,16},{32,40},{40,32},{48,56},{56,48},{64,72... | collective-permute-start | bytes 786440 | tf_op jit(solution)/shard_map/ppermute | solution.py:242
  29.5 5.6 %collective-permute-start.3 = (f32[32,1024]{1,0:T(8,128)S(1)}, f32[32,1024]{1,0:T(8,128)S(1)}, u32[]{:S(2)}, u32[]{:S(2)}) collective-permute-start(f32[32,1024]{1,0:T(8,128)S(1)} %get-tuple-element.21), channel_id=1, source_target_pairs={{0,16},{8,24},{16,0},{24,8},{32,48},{40,56},{48,32},{56,40},{64,80... | collective-permute-start | bytes 393224 | tf_op jit(solution)/shard_map/ppermute | solution.py:242
  35.8 19.7 %collective-permute-start.9 = (f32[4,16,1024]{2,1,0:T(8,128)}, f32[4,16,1024]{2,1,0:T(8,128)}, u32[]{:S(2)}, u32[]{:S(2)}) collective-permute-start(f32[4,16,1024]{2,1,0:T(8,128)} %shard_map.87), channel_id=1, source_target_pairs={{0,128},{8,136},{16,144},{24,152},{32,160},{40,168},{48,176},{56,1... | collective-permute-start | bytes 786440 | tf_op jit(solution)/shard_map/ppermute | solution.py:509
  43.7 18.4 %all-to-all-start = ((f32[8,32,128]{2,1,0:T(8,128)}), f32[8,32,128]{2,1,0:T(8,128)S(1)}, u32[]{:S(2)}, u32[]{:S(2)}) async-start(f32[8,32,128]{2,1,0:T(8,128)} %shard_map.81.__1_), calls=%async_computation | async-start | bytes 262144 | tf_op jit(solution)/shard_map/all_to_all | solution.py:298
  55.5 19.1 %collective-permute-start.10 = (f32[4,16,1024]{2,1,0:T(8,128)}, f32[4,16,1024]{2,1,0:T(8,128)}, u32[]{:S(2)}, u32[]{:S(2)}) collective-permute-start(f32[4,16,1024]{2,1,0:T(8,128)} %shard_map.88), channel_id=1, source_target_pairs={{0,128},{8,136},{16,144},{24,152},{32,160},{40,168},{48,176},{56,1... | collective-permute-start | bytes 786440 | tf_op jit(solution)/shard_map/ppermute | solution.py:509
  62.7 11.8 %all-to-all-start.1 = ((f32[8,32,128]{2,1,0:T(8,128)}), f32[8,32,128]{2,1,0:T(8,128)S(1)}, u32[]{:S(2)}, u32[]{:S(2)}) async-start(f32[8,32,128]{2,1,0:T(8,128)} %shard_map.82), calls=%async_computation.1 | async-start | bytes 262144 | tf_op jit(solution)/shard_map/all_to_all | solution.py:298
  74.6 36.6 %collective-permute-start.11 = (f32[4,32,1024]{2,1,0:T(8,128)}, f32[4,32,1024]{2,1,0:T(8,128)S(1)}, u32[]{:S(2)}, u32[]{:S(2)}) collective-permute-start(f32[4,32,1024]{2,1,0:T(8,128)} %shard_map.89), channel_id=1, source_target_pairs={{0,128},{8,136},{16,144},{24,152},{32,160},{40,168},{48,176},{56,1... | collective-permute-start | bytes 1572872 | tf_op jit(solution)/shard_map/ppermute | solution.py:509
  77.2 15.9 %collective-permute-start.5 = (f32[8,32,128]{2,1,0:T(8,128)S(1)}, f32[8,32,128]{2,1,0:T(8,128)S(1)}, u32[]{:S(2)}, u32[]{:S(2)}) collective-permute-start(f32[8,32,128]{2,1,0:T(8,128)S(1)} %all-to-all-done.1.x._.__1_), channel_id=1, source_target_pairs={{0,16},{8,24},{16,0},{24,8},{32,48},{40,56},{48,32},{56,40},{64,80... | collective-permute-start | bytes 393224 | tf_op jit(solution)/shard_map/ppermute | solution.py:242
  80.5 38.6 %collective-permute-start.12 = (f32[4,24,1024]{2,1,0:T(8,128)S(1)}, f32[4,24,1024]{2,1,0:T(8,128)S(1)}, u32[]{:S(2)}, u32[]{:S(2)}) collective-permute-start(f32[4,24,1024]{2,1,0:T(8,128)S(1)} %shard_map.91), channel_id=1, source_target_pairs={{0,128},{8,136},{16,144},{24,152},{32,160},{40,168},{48,176},{56,1... | collective-permute-start | bytes 1179656 | tf_op jit(solution)/shard_map/ppermute | solution.py:509
  83.9 3.8 %collective-permute-start.7 = (f32[8,8,128]{2,1,0:T(8,128)S(1)}, f32[8,8,128]{2,1,0:T(8,128)S(1)}, u32[]{:S(2)}, u32[]{:S(2)}) collective-permute-start(f32[8,8,128]{2,1,0:T(8,128)S(1)} %shard_map.83), channel_id=1, source_target_pairs={{24,17},{1,24},{25,18},{2,25},{26,19},{3,26},{27,20},{4,27},{28,21... | collective-permute-start | bytes 98312 | tf_op jit(solution)/shard_map/ppermute | solution.py:529
  85.7 7.3 %collective-permute-start.6 = (f32[8,8,128]{2,1,0:T(8,128)S(1)}, f32[8,8,128]{2,1,0:T(8,128)S(1)}, u32[]{:S(2)}, u32[]{:S(2)}) collective-permute-start(f32[8,8,128]{2,1,0:T(8,128)S(1)} %shard_map.83), channel_id=1, source_target_pairs={{24,1},{1,8},{25,2},{2,9},{26,3},{3,10},{27,4},{4,11},{28,5},{5,12... | collective-permute-start | bytes 98312 | tf_op jit(solution)/shard_map/ppermute | solution.py:529
  93.1 1.7 %collective-permute-start.8 = (f32[8,72,128]{2,1,0:T(8,128)S(1)}, f32[8,72,128]{2,1,0:T(8,128)S(1)}, u32[]{:S(2)}, u32[]{:S(2)}) collective-permute-start(f32[8,72,128]{2,1,0:T(8,128)S(1)} %shard_map.84.own), channel_id=1, source_target_pairs={{0,8},{8,0},{16,24},{24,16},{32,40},{40,32},{48,56},{56,48},{64,72... | collective-permute-start | bytes 884744 | tf_op jit(solution)/shard_map/ppermute | solution.py:242
